TPU v7x, 256 devices: a whole 4x4x8 slice. The times are simulated.
256 devices in a mesh: shard: 32 (over y, z), worker: 8 (over x, core).
Axes of the slice: x: 4, y: 4, z: 8, core: 2. Of those that a mesh axis runs over, the one named last changes fastest.
Arguments:
- grads: bfloat16 [32, 1024, 1024], P(None, 'shard'), may hold values from -0.29882812 to 0.29882812
- owners: int32 [32, 1], replicated, may hold values from 0 to 7; in each aligned block of 32 rows (0 to 31, 32 to 63, ...) at most 6 rows name the same one
- left: float32 [8, 6, 1024, 1024], P('worker', None, 'shard'), as said below
- right: float32 [8, 6, 1024, 1024], P('worker', None, 'shard'), as said below
- left_root: float32 [8, 6, 1024, 1024], P('worker', None, 'shard'), as said below
- right_root: float32 [8, 6, 1024, 1024], P('worker', None, 'shard'), as said below
Outputs:
- new_left: float32 [8, 6, 1024, 1024], P('worker', None, 'shard')
- new_right: float32 [8, 6, 1024, 1024], P('worker', None, 'shard')
- precond: bfloat16 [32, 1024, 1024], P(None, 'shard')
Inputs may be any that keep to these rules, and one draw needn't show every extreme that they name: `owners`: no worker owns more than 6 blocks, and some worker owns exactly 6. `left`: each matrix is symmetric with a positive diagonal. `right`: each matrix is symmetric with a positive diagonal. `left_root`: each matrix is symmetric with a positive diagonal. `right_root`: each matrix is symmetric with a positive diagonal.
All inputs are finite; a program needn't handle non-finite values.
Results may differ from a plain program's by a relative error of at most 0.0049.
Values may be sent and summed in bfloat16 or wider, within the bound.
No kernel may reach another device: no remote copies, remote signals or barrier semaphores. Data moves between devices by JAX's collectives and lax.ppermute only.
A program may use at most 128 MiB of HBM per device.

v0:
```python
import jax
import jax.numpy as jnp
from jax import lax
from jax.sharding import PartitionSpec as P

decay_rate = 0.9
highest = lax.Precision.HIGHEST


def slot_table(owner):
    count = owner.shape[0]
    earlier = lax.broadcasted_iota(jnp.int32, (count, count), 1) < lax.broadcasted_iota(
        jnp.int32, (count, count), 0
    )
    same = owner[:, None] == owner[None, :]
    return jnp.sum((same & earlier).astype(jnp.int32), axis=1)


def body(grads, owners, left, right, left_root, right_root):
    capacity = left.shape[1]
    rows = left.shape[2]
    count = owners.shape[0]
    owner = owners[:, 0]
    slot = slot_table(owner)
    worker_id = lax.axis_index("worker")
    first_col = lax.axis_index("shard") * rows
    slot_ids = lax.broadcasted_iota(jnp.int32, (capacity, count), 0)
    mine = (owner[None, :] == worker_id) & (slot[None, :] == slot_ids)
    picker = mine.astype(jnp.bfloat16)
    filled = jnp.any(mine, axis=1)[:, None, None]
    local_g = jnp.einsum("cb,brk->crk", picker, grads, preferred_element_type=jnp.float32).astype(
        jnp.bfloat16
    )
    root_right = right_root[0]
    root_left = left_root[0]
    piece = lax.all_gather(local_g, "shard", axis=1, tiled=True)
    left_part = jnp.einsum("crk,cnk->crn", local_g, piece, preferred_element_type=jnp.float32)
    gram_left = left_part
    columns = lax.dynamic_slice_in_dim(piece, first_col, rows, 2)
    gram_right = jnp.einsum("cnr,cnk->crk", columns, piece, preferred_element_type=jnp.float32)
    image_part = jnp.einsum(
        "crk,cnk->crn", root_right, piece.astype(jnp.float32), precision=highest
    )
    image_t = image_part
    gram_left, gram_right, image_t = (gram_left, gram_right, image_t)
    upd_left = jnp.where(filled, decay_rate * left[0] + (1.0 - decay_rate) * gram_left, left[0])
    upd_right = jnp.where(filled, decay_rate * right[0] + (1.0 - decay_rate) * gram_right, right[0])
    image_b = image_t.astype(jnp.bfloat16)
    result = jnp.einsum(
        "cri,cji->crj",
        root_left,
        lax.all_gather(image_b, "shard", axis=1, tiled=True).astype(jnp.float32),
        precision=highest,
    ).astype(jnp.bfloat16)
    every_slot = lax.all_gather(result, "worker", axis=0, tiled=True)
    flat = owner * capacity + slot
    precond = jnp.take(every_slot, flat, axis=0)
    return (upd_left[None], upd_right[None], precond)


def solution(mesh):
    return jax.shard_map(
        body,
        mesh=mesh,
        in_specs=(
            P(None, "shard", None),
            P(),
            P("worker", None, "shard", None),
            P("worker", None, "shard", None),
            P("worker", None, "shard", None),
            P("worker", None, "shard", None),
        ),
        out_specs=(
            P("worker", None, "shard", None),
            P("worker", None, "shard", None),
            P(None, "shard", None),
        ),
        check_vma=False,
    )
```

profile of v0, /device:TPU:1, one launch (start us, length us, event | category | flops | bytes accessed | tf_op | source)
XLA Modules:
  0.0 323.5 jit_solution(13688285086961528662)
XLA Ops:
  7.2 0.0 copy-start
  7.2 0.0 copy-start.2
  7.2 0.0 all-gather.4.cloned.1.call-start
  7.2 1.0 convert_reduce_fusion
  8.2 0.7 broadcast_compare_fusion
  8.9 0.0 copy-done
  8.9 2.3 fusion
  11.2 1.0 copy.29
  12.2 0.0 all-gather.4.cloned.1.call-update
  12.2 0.0 all-gather.6.cloned.1.call-start
  12.3 123.2 %all-gather.4.cloned.1.call-done = bf16[6,1024,1024]{2,1,0:T(8,128)(2,1)} async-done(((bf16[6,32,1024]{2,1,0:T(8,128)(2,1)}), bf16[6,1024,1024]{2,1,0:T(8,128)(2,1)}) %all-gather.4.cloned.1.call-update) | async-done | bytes 12582928 | tf_op jit(solution)/shard_map/all_gather | solution.py:36
  135.5 0.0 copy-done.2
  135.5 14.5 %fusion.19 = bf16[6,32,1024]{2,1,0:T(8,128)(2,1)} fusion(bf16[6,1024,1024]{2,1,0:T(8,128)(2,1)} %all-gather.4.cloned.1.call-done, f32[1,6,32,1024]{3,2,1,0:T(8,128)S(1)} %copy-done.2), kind=kOutput, calls=%fused_computation.16 | convolution fusion | flops 2416115712 | bytes 13762560 | tf_op jit(solution)/shard_map/crk,cnk->crn/dot_general | solution.py:41
  150.0 0.0 all-gather.6.cloned.1.call-update
  150.0 0.0 copy-start.5
  150.0 0.0 copy-start.3
  150.0 0.2 all-gather.8.cloned.1.call-start
  150.3 116.7 %all-gather.6.cloned.1.call-done = bf16[6,1024,1024]{2,1,0:T(8,128)(2,1)} async-done(((bf16[6,32,1024]{2,1,0:T(8,128)(2,1)}), bf16[6,1024,1024]{2,1,0:T(8,128)(2,1)}) %all-gather.6.cloned.1.call-update) | async-done | bytes 12582928 | tf_op jit(solution)/shard_map/all_gather | solution.py:52
  266.9 14.6 %fusion.20 = bf16[6,32,1024]{2,1,0:T(8,128)(2,1)} fusion(bf16[6,1024,1024]{2,1,0:T(8,128)(2,1)} %all-gather.6.cloned.1.call-done, f32[1,6,32,1024]{3,2,1,0:T(8,128)} %param.10), kind=kOutput, calls=%fused_computation.17 | convolution fusion | flops 2416115712 | bytes 13762560 | tf_op jit(solution)/shard_map/cri,cji->crj/dot_general | solution.py:49
  281.6 0.0 all-gather.8.cloned.1.call-update
  281.6 0.0 copy-done.5
  281.6 0.1 fusion.26
  281.8 0.0 copy-done.3
  281.8 0.0 copy-start.1
  281.8 0.0 copy-start.4
  281.8 8.6 %fusion.16 = f32[1,6,32,1024]{3,2,1,0:T(8,128)} fusion(bf16[6,1024,1024]{2,1,0:T(8,128)(2,1)} %all-gather.4.cloned.1.call-done, s32[]{:T(128)S(6)} %select_n.22, f32[1,6,32,1024]{3,2,1,0:T(8,128)S(1)} %copy-done.3, pred[6]{0:T(512)(128)(4,1)S(1)} %fusion.26), kind=kOutput, calls=%fused_computation.13 | convolution fusion | flops 403439616 | bytes 15728650 | tf_op jit(solution)/shard_map/cnr,cnk->crk/dot_general | solution.py:40
  290.4 0.0 copy-done.1
  290.4 0.0 copy-done.4
  290.4 9.7 %fusion.6 = f32[1,6,32,1024]{3,2,1,0:T(8,128)} fusion(bf16[6,32,1024]{2,1,0:T(8,128)(2,1)S(1)} %copy-done.1, bf16[6,1024,1024]{2,1,0:T(8,128)(2,1)} %all-gather.4.cloned.1.call-done, f32[1,6,32,1024]{3,2,1,0:T(8,128)S(1)} %copy-done.4, pred[6]{0:T(512)(128)(4,1)S(1)} %fusion.26), kind=kOutput, calls=%fused_computation.9 | convolution fusion | flops 403439616 | bytes 14548998 | tf_op jit(solution)/shard_map/crk,cnk->crn/dot_general | solution.py:37
  300.2 9.7 %all-gather.8.cloned.1.call-done = bf16[48,32,1024]{2,1,0:T(8,128)(2,1)} async-done(((bf16[6,32,1024]{2,1,0:T(8,128)(2,1)}), bf16[48,32,1024]{2,1,0:T(8,128)(2,1)}) %all-gather.8.cloned.1.call-update) | async-done | bytes 3145744 | tf_op jit(solution)/shard_map/all_gather | solution.py:55
  309.9 3.9 %gather_fusion = bf16[32,32,1024]{2,1,0:T(8,128)(2,1)} fusion(bf16[48,32,1024]{2,1,0:T(8,128)(2,1)} %all-gather.8.cloned.1.call-done, s32[1024]{0:T(1024)S(1)} %pad_clamp_fusion), kind=kCustom, calls=%fused_computation | custom fusion | bytes 4194432 | tf_op jit(solution)/shard_map/jit(_take)/gather | solution.py:57
  313.8 3.2 broadcast_select_fusion
  (2 shorter events, 0.0 us)
Async XLA Ops:
  7.2 1.7 copy-start
  7.2 128.3 %copy-start.2 = (f32[1,6,32,1024]{3,2,1,0:T(8,128)S(1)}, f32[1,6,32,1024]{3,2,1,0:T(8,128)}, u32[]{:S(2)}) copy-start(f32[1,6,32,1024]{3,2,1,0:T(8,128)} %param.11) | copy-start | bytes 2359300
  7.2 128.3 %all-gather.4.cloned.1.call-start = ((), (), s32[]{:S(2)}) async-start(), calls=%async_computation | async-start | bytes 12976128 | tf_op jit(solution)/shard_map/all_gather | solution.py:36
  12.2 254.7 %all-gather.6.cloned.1.call-start = ((), (), s32[]{:S(2)}) async-start(), calls=%async_computation.1 | async-start | bytes 12976128 | tf_op jit(solution)/shard_map/all_gather | solution.py:52
  150.0 131.6 %copy-start.5 = (s32[32,1]{0,1:T(1,128)S(1)}, s32[32,1]{0,1:T(1,128)}, u32[]{:S(2)}) copy-start(s32[32,1]{0,1:T(1,128)} %param.7) | copy-start | bytes 388
  150.0 131.7 %copy-start.3 = (f32[1,6,32,1024]{3,2,1,0:T(8,128)S(1)}, f32[1,6,32,1024]{3,2,1,0:T(8,128)}, u32[]{:S(2)}) copy-start(f32[1,6,32,1024]{3,2,1,0:T(8,128)} %param.9) | copy-start | bytes 2359300
  150.0 159.9 %all-gather.8.cloned.1.call-start = ((), (), s32[]{:S(2)}) async-start(), calls=%async_computation.2 | async-start | bytes 3538944 | tf_op jit(solution)/shard_map/all_gather | solution.py:55
  281.8 8.7 %copy-start.1 = (bf16[6,32,1024]{2,1,0:T(8,128)(2,1)S(1)}, bf16[6,32,1024]{2,1,0:T(8,128)(2,1)}, u32[]{:S(2)}) copy-start(bf16[6,32,1024]{2,1,0:T(8,128)(2,1)} %copy.29) | copy-start | bytes 1179652
  281.8 8.7 %copy-start.4 = (f32[1,6,32,1024]{3,2,1,0:T(8,128)S(1)}, f32[1,6,32,1024]{3,2,1,0:T(8,128)}, u32[]{:S(2)}) copy-start(f32[1,6,32,1024]{3,2,1,0:T(8,128)} %param.8) | copy-start | bytes 2359300
Sparse Core Ops, SparseCore 0:
  12.3 123.1 all-gather.3
  150.1 116.7 all-gather.5
  281.7 28.1 all-gather.7
where the time goes:
time: 324 us; the launch traced here: 323 us
  waiting for transfers between devices  250 us (77%)
  matrix products  49.8 us (15%)
  between operations  13.8 us (4%)
  other arithmetic  4.96 us (2%)
  local copies, waits for them, and re-layouts  4.89 us (2%)
    all_gather x1, waiting for transfers between devices, body(): piece = lax.all_gather(local_g, 'shard', axis=1, tiled=True)  123 us
    all_gather x1, waiting for transfers between devices, body(): lax.all_gather(image_b, 'shard', axis=1, tiled=True).astype(jnp.float32)  117 us
    dot_general x1, matrix products, body(): jnp.einsum('cri,cji->crj', root_left, lax.all_gather(image_b, 'shard', ax...  14.6 us
    dot_general x1, matrix products, body(): jnp.einsum('crk,cnk->crn', root_right, piece.astype(jnp.float32), precisi...  14.5 us
    dot_general x1, matrix products, body(): jnp.einsum('crk,cnk->crn', local_g, piece, preferred_element_type=jnp.flo...  9.74 us
    all_gather x1, waiting for transfers between devices, body(): every_slot = lax.all_gather(result, 'worker', axis=0, tiled=True)  9.71 us
    dot_general x1, matrix products, body(): jnp.einsum('cnr,cnk->crk', columns, piece, preferred_element_type=jnp.flo...  8.64 us
  transfers between devices with their start and end apart: 3, of which 3 were waited for; matrix products, arithmetic and copies ran while one was open for 6% of the time, Pallas kernels for 0%

commit v1 on v0

v1 whole, which is shorter than its diff:
```python
import jax
import jax.numpy as jnp
from jax import lax
from jax.sharding import PartitionSpec as P

decay_rate = 0.9
bf16 = jnp.bfloat16
f32 = jnp.float32


def slot_table(owner):
    count = owner.shape[0]
    earlier = lax.broadcasted_iota(jnp.int32, (count, count), 1) < lax.broadcasted_iota(
        jnp.int32, (count, count), 0
    )
    same = owner[:, None] == owner[None, :]
    return jnp.sum((same & earlier).astype(jnp.int32), axis=1)


def body(grads, owners, left, right, left_root, right_root):
    count, rows, order = grads.shape
    capacity = left.shape[1]
    workers = lax.axis_size("worker")
    shards = lax.axis_size("shard")
    part = order // workers
    w = lax.axis_index("worker")
    s = lax.axis_index("shard")
    owner = owners[:, 0]
    slot = slot_table(owner)
    flat = owner * capacity + slot
    spots = lax.broadcasted_iota(jnp.int32, (workers * capacity, count), 0)
    named = flat[None, :] == spots
    holder = jnp.argmax(named, axis=1).astype(jnp.int32)
    filled = lax.dynamic_slice_in_dim(jnp.any(named, axis=1), w * capacity, capacity)[
        :, None, None
    ]

    roots = jnp.concatenate([left_root, right_root], axis=0)
    row_ids = lax.broadcasted_iota(jnp.int32, roots.shape, 2) + s * rows
    on_diag = lax.broadcasted_iota(jnp.int32, roots.shape, 3) == row_ids
    diag = jnp.sum(jnp.where(on_diag, roots, 0.0), axis=3)
    diags = lax.all_gather(diag, ("shard", "worker"), axis=0, tiled=False)
    diags = diags.reshape(shards, workers, 2, capacity, rows)

    g_part = lax.dynamic_slice_in_dim(grads, w * part, part, 2)
    g_cols = lax.all_to_all(g_part, "shard", 0, 0, tiled=True).reshape(order, part)
    g_full = lax.all_gather(g_cols, "worker", axis=0, tiled=False)

    off = jnp.where(on_diag, 0.0, roots).astype(bf16)
    off = off.reshape(2, capacity, rows, workers, part).transpose(3, 1, 0, 2, 4)
    off = lax.all_to_all(off, "worker", 0, 0, tiled=True)
    off = off.reshape(workers * capacity, 2, rows, part)
    off = jnp.take(off, flat, axis=0)
    off = lax.all_to_all(off, "shard", 0, 0, tiled=True)
    l_cols = off[:, 0].reshape(order, part)
    r_cols = off[:, 1].reshape(order, part)
    l_full = lax.all_gather(l_cols, "worker", axis=0, tiled=False)

    my_flat = flat[s]
    my_diag = lax.dynamic_slice(
        diags,
        (0, my_flat // capacity, 0, my_flat % capacity, 0),
        (shards, 1, 2, 1, rows),
    ).reshape(shards, 2, rows)
    l_diag = my_diag[:, 0].reshape(order)
    r_diag = lax.dynamic_slice_in_dim(my_diag[:, 1].reshape(order), w * part, part)

    g_rows = lax.dynamic_slice_in_dim(g_full, w * part, part, 1)
    gram_left = jnp.einsum("vnk,vmk->nm", g_full, g_rows, preferred_element_type=f32)
    gram_right = jnp.einsum("vnk,nm->vkm", g_full, g_cols, preferred_element_type=f32)
    image = jnp.einsum(
        "vnk,vkm->nm", g_full, r_cols.reshape(workers, part, part), preferred_element_type=f32
    )
    image = (image + g_cols.astype(f32) * r_diag[None, :]).astype(bf16)
    result = jnp.einsum(
        "vnk,vkm->nm", l_full, image.reshape(workers, part, part), preferred_element_type=f32
    )
    result = (result + image.astype(f32) * l_diag[:, None]).astype(bf16)

    result = lax.all_to_all(result.reshape(shards, rows, part), "shard", 0, 0, tiled=True)
    precond = lax.all_gather(result, "worker", axis=2, tiled=True)

    grams = jnp.stack(
        [
            gram_left.astype(bf16).reshape(shards, rows, part),
            gram_right.astype(bf16).reshape(shards, rows, part),
        ],
        axis=1,
    )
    grams = lax.all_to_all(grams, "shard", 0, 0, tiled=True)
    grams = jnp.take(grams, holder, axis=0).reshape(workers, capacity, 2, rows, part)
    grams = lax.all_to_all(grams, "worker", 0, 0, tiled=True)
    grams = grams.transpose(2, 1, 3, 0, 4).reshape(2, capacity, rows, order).astype(f32)
    upd_left = jnp.where(filled, decay_rate * left[0] + (1.0 - decay_rate) * grams[0], left[0])
    upd_right = jnp.where(filled, decay_rate * right[0] + (1.0 - decay_rate) * grams[1], right[0])
    return (upd_left[None], upd_right[None], precond)


def solution(mesh):
    factor = P("worker", None, "shard", None)
    return jax.shard_map(
        body,
        mesh=mesh,
        in_specs=(P(None, "shard", None), P(), factor, factor, factor, factor),
        out_specs=(factor, factor, P(None, "shard", None)),
        check_vma=False,
    )
```

time: 324 us -> 245 us (0.76)
  waiting for transfers between devices: 250 us -> 44.4 us
  blocking collectives: 0 us -> 128 us
  matrix products: 49.8 us -> 7.81 us
  starting transfers between devices: 0.3 us -> 22.1 us
  local copies, waits for them, and re-layouts: 4.89 us -> 17.3 us
  other arithmetic: 4.96 us -> 8.98 us
    all_gather x3, waiting for transfers between devices: 250 us -> 0.02 us  [the longest x1 0.02 us: body(): l_full = lax.all_gather(l_cols, 'worker', axis=0, tiled=False)]
    all_gather x0 -> x1, blocking collectives: none -> 70.9 us  [body(): diags = lax.all_gather(diag, ('shard', 'worker'), axis=0, tiled=False)]
    all_to_all x0 -> x3, blocking collectives: none -> 56.8 us  [the longest x1 21.6 us: body(): lax.all_to_all(g_part, 'shard', 0, 0, tiled=True).reshape(order, part)]
    all_to_all x0 -> x3, waiting for transfers between devices: none -> 44.4 us  [the longest x1 18.9 us: body(): off = lax.all_to_all(off, 'worker', 0, 0, tiled=True)]
    dot_general x5 -> x4, matrix products: 49.8 us -> 7.81 us  [the longest x1 2.45 us: body(): jnp.einsum('vnk,vmk->nm', g_full, g_rows, preferred_element_type=f32)]
    all_to_all x0 -> x3, starting transfers between devices: none -> 22 us  [the longest x1 8.02 us: body(): off = lax.all_to_all(off, 'worker', 0, 0, tiled=True)]
    unnamed x12 -> x17, local copies, waits for them, and re-layouts: 0.04 us -> 8.14 us
  transfers between devices with their start and end apart: 3 -> 6, of which waited for: 3 -> 3; matrix products, arithmetic and copies ran while one was open for 6% -> 11% of each run, Pallas kernels for 0% -> 0%
where the time goes in v1:
time: 245 us; the launch traced here: 244 us
  blocking collectives  128 us (52%)
  waiting for transfers between devices  44.4 us (18%)
  starting transfers between devices  22.1 us (9%)
  local copies, waits for them, and re-layouts  17.3 us (7%)
  between operations  15.9 us (6%)
  other arithmetic  8.98 us (4%)
  matrix products  7.81 us (3%)
    all_gather x1, blocking collectives, body(): diags = lax.all_gather(diag, ('shard', 'worker'), axis=0, tiled=False)  70.9 us
    all_to_all x1, blocking collectives, body(): lax.all_to_all(g_part, 'shard', 0, 0, tiled=True).reshape(order, part)  21.6 us
    all_to_all x1, blocking collectives, body(): off = lax.all_to_all(off, 'shard', 0, 0, tiled=True)  19 us
    all_to_all x1, waiting for transfers between devices, body(): off = lax.all_to_all(off, 'worker', 0, 0, tiled=True)  18.9 us
    all_to_all x1, blocking collectives, body(): lax.all_to_all(result.reshape(shards, rows, part), 'shard', 0, 0, tiled=T...  16.1 us
    all_to_all x1, waiting for transfers between devices, body(): grams = lax.all_to_all(grams, 'shard', 0, 0, tiled=True)  13.3 us
    all_to_all x1, waiting for transfers between devices, body(): grams = lax.all_to_all(grams, 'worker', 0, 0, tiled=True)  12.1 us
    unnamed x17, local copies, waits for them, and re-layouts  8.14 us
  transfers between devices with their start and end apart: 6, of which 3 were waited for; matrix products, arithmetic and copies ran while one was open for 11% of the time, Pallas kernels for 0%

profile of v1, /device:TPU:1, one launch (start us, length us, event | category | flops | bytes accessed | tf_op | source)
XLA Modules:
  0.0 244.2 jit_solution(1484385310314361195)
XLA Ops:
  7.2 0.0 all-gather.5.cloned.1.call-start
  7.2 1.5 copy-done
  8.8 0.1 constant_dynamic-slice_fusion.1
  8.8 21.6 %all_to_all.30 = bf16[32,32,128]{2,1,0:T(8,128)(2,1)} all-to-all(bf16[32,32,128]{2,1,0:T(8,128)(2,1)S(1)} %constant_dynamic-slice_fusion.1), channel_id=1, replica_groups=mesh['shard'=32,'worker'=8] {'shard'}, dimensions={0} | all-to-all | bytes 524288 | tf_op jit(solution)/shard_map/all_to_all | solution.py:46
  30.5 0.0 all-gather.5.cloned.1.call-update
  30.5 1.3 copy.65
  31.8 0.9 copy.66
  32.7 1.2 fusion.7
  34.0 1.7 copy.62
  35.7 8.0 %all-to-all-start.3 = ((bf16[8,6,2,32,128]{4,2,3,1,0:T(2,128)(2,1)}), bf16[8,6,2,32,128]{4,2,3,1,0:T(2,128)(2,1)}, u32[]{:S(2)}, u32[]{:S(2)}) async-start(bf16[8,6,2,32,128]{4,2,3,1,0:T(2,128)(2,1)} %copy.62), calls=%async_computation.3 | async-start | bytes 1572864 | tf_op jit(solution)/shard_map/all_to_all | solution.py:51
  43.7 0.2 convert_reduce_fusion
  43.9 18.9 %all-to-all-done.3 = bf16[8,6,2,32,128]{4,2,3,1,0:T(2,128)(2,1)} async-done(((bf16[8,6,2,32,128]{4,2,3,1,0:T(2,128)(2,1)}), bf16[8,6,2,32,128]{4,2,3,1,0:T(2,128)(2,1)}, u32[]{:S(2)}, u32[]{:S(2)}) %all-to-all-start.3) | async-done | bytes 786464 | tf_op jit(solution)/shard_map/all_to_all | solution.py:51
  62.8 2.2 copy.63
  65.0 1.8 gather_fusion.1
  66.8 0.1 broadcast_select_fusion
  66.9 19.0 %all_to_all.31 = bf16[32,2,32,128]{3,2,1,0:T(8,128)(2,1)S(1)} all-to-all(bf16[32,2,32,128]{3,2,1,0:T(8,128)(2,1)S(1)} %broadcast_select_fusion), channel_id=1, replica_groups=mesh['shard'=32,'worker'=8] {'shard'}, dimensions={0} | all-to-all | bytes 1048576 | tf_op jit(solution)/shard_map/all_to_all | solution.py:54
  86.0 0.7 fusion.14
  86.7 0.0 all-gather.9.cloned.1.call-start
  86.8 0.6 dynamic_slice.21
  89.4 1.4 fusion.1
  90.8 70.9 %all-gather = f32[512,6,32]{2,1,0:T(8,128)S(1)} all-gather(f32[2,6,32]{2,1,0:T(8,128)S(1)} %fusion.1), channel_id=2, replica_groups=mesh['shard'=32,'worker'=8] {'shard','worker'}, dimensions={0}, use_global_device_ids=true | all-gather | bytes 394752 | tf_op jit(solution)/shard_map/all_gather | solution.py:42
  161.7 0.1 slice_reduce_fusion
  161.8 0.1 reshape_squeeze.3
  161.9 0.1 dynamic_slice.23
  162.0 0.1 mul.82
  162.0 2.3 fusion.6
  164.4 0.0 all-gather.7.cloned.1.call-done
  164.4 2.3 fusion.5
  166.7 16.1 %all_to_all.32 = bf16[32,32,128]{2,1,0:T(8,128)(2,1)} all-to-all(bf16[32,32,128]{2,1,0:T(8,128)(2,1)S(1)} %bitcast.86), channel_id=1, replica_groups=mesh['shard'=32,'worker'=8] {'shard'}, dimensions={0} | all-to-all | bytes 524288 | tf_op jit(solution)/shard_map/all_to_all | solution.py:80
  182.8 2.5 %fusion.4 = bf16[1024,128]{1,0:T(8,128)(2,1)S(1)} fusion(bf16[8,1024,128]{2,1,0:T(8,128)(2,1)} %all-gather.5.cloned.1.call-done, s32[]{:T(128)S(6)} %select_n.73), kind=kOutput, calls=%fused_computation.13 | convolution fusion | flops 268566528 | bytes 2621444 | tf_op jit(solution)/shard_map/vnk,vmk->nm/dot_general | solution.py:69
  185.3 0.8 convolution_convert_fusion
  186.1 0.8 pad_maximum_fusion
  186.9 6.5 %all-to-all-start.1 = ((bf16[32,2,32,128]{3,2,1,0:T(8,128)(2,1)}), bf16[32,2,32,128]{3,2,1,0:T(8,128)(2,1)S(1)}, u32[]{:S(2)}, u32[]{:S(2)}) async-start(bf16[32,2,32,128]{3,2,1,0:T(8,128)(2,1)} %pad_maximum_fusion), calls=%async_computation.1 | async-start | bytes 1048576 | tf_op jit(solution)/shard_map/all_to_all | solution.py:90
  193.5 0.6 iota_reduce_fusion
  194.1 0.1 broadcast_in_dim.49
  194.2 13.3 %all-to-all-done.1 = bf16[32,2,32,128]{3,2,1,0:T(8,128)(2,1)S(1)} async-done(((bf16[32,2,32,128]{3,2,1,0:T(8,128)(2,1)}), bf16[32,2,32,128]{3,2,1,0:T(8,128)(2,1)S(1)}, u32[]{:S(2)}, u32[]{:S(2)}) %all-to-all-start.1) | async-done | bytes 524320 | tf_op jit(solution)/shard_map/all_to_all | solution.py:90
  207.5 1.6 gather_fusion
  209.0 2.2 copy_select_fusion
  211.2 7.4 %all-to-all-start.2 = ((bf16[8,6,2,32,128]{4,3,1,2,0:T(8,128)(2,1)}), bf16[8,6,2,32,128]{4,3,1,2,0:T(8,128)(2,1)S(1)}, u32[]{:S(2)}, u32[]{:S(2)}) async-start(bf16[8,6,2,32,128]{4,3,1,2,0:T(8,128)(2,1)} %copy_select_fusion), calls=%async_computation.2 | async-start | bytes 1572864 | tf_op jit(solution)/shard_map/all_to_all | solution.py:92
  218.6 0.1 fusion.11
  218.7 0.1 dynamic_slice.18
  218.8 12.1 %all-to-all-done.2 = bf16[8,6,2,32,128]{4,3,1,2,0:T(8,128)(2,1)S(1)} async-done(((bf16[8,6,2,32,128]{4,3,1,2,0:T(8,128)(2,1)}), bf16[8,6,2,32,128]{4,3,1,2,0:T(8,128)(2,1)S(1)}, u32[]{:S(2)}, u32[]{:S(2)}) %all-to-all-start.2) | async-done | bytes 786464 | tf_op jit(solution)/shard_map/all_to_all | solution.py:92
  230.9 0.5 convert_bitcast_fusion
  231.4 0.1 slice_multiply_fusion
  231.6 1.0 copy-done.4
  232.5 0.2 copy-done.5
  232.8 1.7 fusion.8
  234.5 3.2 %copy.76 = bf16[32,32,1024]{2,1,0:T(8,128)(2,1)} copy(bf16[32,32,1024]{2,1,0:T(8,128)(2,1)} %all-gather.9.cloned.1.call-done) | data formatting | bytes 4194304
  (25 shorter events, 0.2 us)
Async XLA Ops:
  7.2 1.6 copy-start
  7.2 24.6 %copy-start.1 = (f32[1,6,32,1024]{3,2,1,0:T(8,128)S(1)}, f32[1,6,32,1024]{3,2,1,0:T(8,128)}, u32[]{:S(2)}) copy-start(f32[1,6,32,1024]{3,2,1,0:T(8,128)} %param.11) | copy-start | bytes 2359300
  7.2 154.8 %all-gather.5.cloned.1.call-start = ((), (), s32[]{:S(2)}) async-start(), calls=%async_computation.6 | async-start | bytes 2359296 | tf_op jit(solution)/shard_map/all_gather | solution.py:47
  32.7 11.0 %copy-start.6 = (s32[32,1]{0,1:T(1,128)S(1)}, s32[32,1]{0,1:T(1,128)}, u32[]{:S(2)}) copy-start(s32[32,1]{0,1:T(1,128)} %param.7) | copy-start | bytes 388
  35.7 27.1 %all-to-all-start.3 = ((bf16[8,6,2,32,128]{4,2,3,1,0:T(2,128)(2,1)}), bf16[8,6,2,32,128]{4,2,3,1,0:T(2,128)(2,1)}, u32[]{:S(2)}, u32[]{:S(2)}) async-start(bf16[8,6,2,32,128]{4,2,3,1,0:T(2,128)(2,1)} %copy.62), calls=%async_computation.3 | async-start | bytes 1572864 | tf_op jit(solution)/shard_map/all_to_all | solution.py:51
  43.7 120.7 %all-gather.7.cloned.1.call-start = ((), (), s32[]{:S(2)}) async-start(), calls=%async_computation.7 | async-start | bytes 2359296 | tf_op jit(solution)/shard_map/all_gather | solution.py:57
  86.7 75.3 %copy-start.2 = (bf16[32,32,128]{2,1,0:T(8,128)(2,1)S(1)}, bf16[32,32,128]{2,1,0:T(8,128)(2,1)}, u32[]{:S(2)}) copy-start(bf16[32,32,128]{2,1,0:T(8,128)(2,1)} %all_to_all.30) | copy-start | bytes 786436
  86.7 147.8 %all-gather.9.cloned.1.call-start = ((), (), s32[]{:S(2)}) async-start(), calls=%async_computation.8 | async-start | bytes 2359296 | tf_op jit(solution)/shard_map/all_gather | solution.py:81
  182.8 2.5 %copy-start.3 = (bf16[8,1024,128]{2,1,0:T(8,128)(2,1)S(1)}, bf16[8,1024,128]{2,1,0:T(8,128)(2,1)}, u32[]{:S(2)}) copy-start(bf16[8,1024,128]{2,1,0:T(8,128)(2,1)} %all-gather.5.cloned.1.call-done) | copy-start | bytes 6291460
  186.9 20.6 %all-to-all-start.1 = ((bf16[32,2,32,128]{3,2,1,0:T(8,128)(2,1)}), bf16[32,2,32,128]{3,2,1,0:T(8,128)(2,1)S(1)}, u32[]{:S(2)}, u32[]{:S(2)}) async-start(bf16[32,2,32,128]{3,2,1,0:T(8,128)(2,1)} %pad_maximum_fusion), calls=%async_computation.1 | async-start | bytes 1048576 | tf_op jit(solution)/shard_map/all_to_all | solution.py:90
  211.2 19.7 %all-to-all-start.2 = ((bf16[8,6,2,32,128]{4,3,1,2,0:T(8,128)(2,1)}), bf16[8,6,2,32,128]{4,3,1,2,0:T(8,128)(2,1)S(1)}, u32[]{:S(2)}, u32[]{:S(2)}) async-start(bf16[8,6,2,32,128]{4,3,1,2,0:T(8,128)(2,1)} %copy_select_fusion), calls=%async_computation.2 | async-start | bytes 1572864 | tf_op jit(solution)/shard_map/all_to_all | solution.py:92
  231.4 1.1 copy-start.4
  231.4 1.4 copy-start.5
Sparse Core Ops, SparseCore 0:
  30.6 31.3 all-gather.4
  86.9 26.8 all-gather.6
  182.9 27.1 all-gather.8

commit v2 on v0

v2 whole, which is shorter than its diff:
```python
import jax
import jax.numpy as jnp
from jax import lax
from jax.experimental import pallas as pl
from jax.experimental.pallas import tpu as pltpu
from jax.sharding import PartitionSpec as P

decay_rate = 0.9
bf16 = jnp.bfloat16
f32 = jnp.float32

BS = 1024
NB = 32
CAP = 6
ROWS = 32
NW = 8
PART = 128
PARTNERS = [(k, o) for k in range(4) for o in range(2)]
VMEM = pl.BlockSpec(memory_space=pltpu.VMEM)
SMEM = pl.BlockSpec(memory_space=pltpu.SMEM)


def partner(worker, k, other):
    core = worker % 2
    core = 1 - core if other else core
    return (worker // 2 + k) % 4 * 2 + core


def send(value, k, other):
    return lax.ppermute(value, "worker", [(w, partner(w, k, other)) for w in range(NW)])


def exchange(pieces):
    return [p if j == 0 else send(p, *PARTNERS[j]) for j, p in enumerate(pieces)]


def gather(piece):
    along = [piece] + [send(piece, k, 0) for k in range(1, 4)]
    out = []
    for p in along:
        out += [p, send(p, 0, 1)]
    return out


def sources(worker):
    return [partner(worker, 4 - k, other) for k, other in PARTNERS]


def dests(worker):
    return [partner(worker, k, other) for k, other in PARTNERS]


def call(kernel, outs, args, in_specs=None, out_specs=None, flops=0, nbytes=2 << 20):
    return pl.pallas_call(
        kernel,
        out_shape=outs,
        in_specs=in_specs or [VMEM] * len(args),
        out_specs=out_specs or jax.tree.map(lambda _: VMEM, outs),
        compiler_params=pltpu.CompilerParams(vmem_limit_bytes=20 << 20),
        cost_estimate=pl.CostEstimate(flops=flops, bytes_accessed=nbytes, transcendentals=0),
    )(*args)


def shape(dims, kind=bf16):
    return jax.ShapeDtypeStruct(dims, kind)


def pack_roots(owners, left, right, *outs):
    holder, outs = outs[-1], outs[:-1]
    worker, shard = lax.axis_index("worker"), lax.axis_index("shard")
    for i in range(NW * CAP):
        holder[i] = -1

    def name(b, carry):
        who = owners[b]
        taken = lax.fori_loop(
            0, CAP, lambda c, n: n + (holder[who * CAP + c] >= 0).astype(jnp.int32), 0
        )
        holder[who * CAP + taken] = b
        return carry

    lax.fori_loop(0, NB, name, 0)
    row = lax.broadcasted_iota(jnp.int32, (ROWS, PART), 0)
    lane = lax.broadcasted_iota(jnp.int32, (ROWS, PART), 1)
    near = shard // 4
    on_diag = lane == row + shard % 4 * ROWS
    diag_rows = []
    for c in range(CAP):
        total = jnp.zeros((1, PART), f32)
        for n, ref in enumerate((left, right)):
            block = ref[c, :, pl.ds(pl.multiple_of(near * PART, PART), PART)]
            d = jnp.sum(jnp.where(on_diag, block, 0.0), axis=0, keepdims=True)
            high = d.astype(bf16).astype(f32)
            for m, v in enumerate((high, d - high)):
                to = (2 * n + m) * ROWS
                total = total + pltpu.roll(v, (to + PART - shard % 4 * ROWS) % PART, 1)
        diag_rows.append(total)
    diag_tile = jnp.concatenate(diag_rows + [jnp.zeros((16 - CAP, PART), f32)], axis=0).astype(bf16)
    for out, to in zip(outs, dests(worker)):
        cols = pl.ds(pl.multiple_of(to * PART, PART), PART)
        mask = on_diag & (to == near)
        for c in range(CAP):
            for n, ref in enumerate((left, right)):
                at = (2 * c + n) * ROWS
                out[at : at + ROWS, :] = jnp.where(mask, 0.0, ref[c, :, cols]).astype(bf16)
        out[2 * CAP * ROWS :, :] = diag_tile


def pick_roots(holder, *refs):
    pieces, (out_left, out_right) = refs[:NW], refs[NW:]
    worker = lax.axis_index("worker")
    for piece, source in zip(pieces, sources(worker)):
        diag_tile = piece[2 * CAP * ROWS :, :].astype(f32)
        for c in range(CAP):
            block = holder[source * CAP + c]

            @pl.when(block >= 0)
            def _():
                out_left[block] = piece[2 * c * ROWS : (2 * c + 1) * ROWS, :]
                out_right[block, :ROWS, :] = piece[(2 * c + 1) * ROWS : (2 * c + 2) * ROWS, :]
                out_right[block, ROWS:, :] = jnp.broadcast_to(
                    diag_tile[c : c + 1], (16, PART)
                ).astype(bf16)


def make_grams(*refs):
    pieces, out = refs[:NW], refs[NW]
    worker = lax.axis_index("worker")
    mine = pl.ds(pl.multiple_of(worker * PART, PART), PART)
    total = jnp.zeros((BS, PART), f32)
    for piece, source in zip(pieces, sources(worker)):
        total = total + lax.dot_general(
            piece[...], piece[mine, :], (((1,), (1,)), ((), ())), preferred_element_type=f32
        )
        block = lax.dot_general(
            piece[...], pieces[0][...], (((0,), (0,)), ((), ())), preferred_element_type=f32
        )
        out[pl.ds(source * 4, 4), ROWS:, :] = block.astype(bf16).reshape(4, ROWS, PART)
    out[:, :ROWS, :] = total.astype(bf16).reshape(NB, ROWS, PART)


def make_image(right, *refs):
    pieces, out = refs[:NW], refs[NW]
    worker = lax.axis_index("worker")
    lane = lax.broadcasted_iota(jnp.int32, (1, PART), 1)
    diag = jnp.zeros((1, PART), f32)
    for q in range(4):
        d = right[worker * 4 + q, ROWS:, :].astype(f32)[:1]
        both = pltpu.roll(d, 64, 1) + pltpu.roll(d, 32, 1)
        diag = diag + pltpu.roll(jnp.where(lane < ROWS, both, 0.0), q * ROWS, 1)
    total = pieces[0][...].astype(f32) * diag
    for piece, source in zip(pieces, sources(worker)):
        block = right[pl.ds(source * 4, 4), :ROWS, :].reshape(PART, PART)
        total = total + jnp.dot(piece[...], block, preferred_element_type=f32)
    out[...] = total.astype(bf16)


def make_result(right, image, *refs):
    pieces, out = refs[:NW], refs[NW]
    worker = lax.axis_index("worker")
    diag_rows = right[:, ROWS:, :].astype(f32)[:, :1, :]
    row = lax.broadcasted_iota(jnp.int32, (NB, ROWS, PART), 1)
    lane = lax.broadcasted_iota(jnp.int32, (NB, ROWS, PART), 2)
    spread = jnp.where((lane == row) | (lane == row + ROWS), diag_rows, 0.0)
    spread = spread.astype(bf16).reshape(BS, PART)
    diag = jnp.dot(spread, jnp.ones((PART, PART), bf16), preferred_element_type=f32)
    total = image[...].astype(f32) * diag
    for piece, source in zip(pieces, sources(worker)):
        block = image[pl.ds(pl.multiple_of(source * PART, PART), PART), :]
        total = total + jnp.dot(piece[...], block, preferred_element_type=f32)
    out[...] = total.astype(bf16).reshape(NB, ROWS, PART)


def pack_grams(holder, grams, *outs):
    worker = lax.axis_index("worker")
    for out, to in zip(outs, dests(worker)):
        for c in range(CAP):
            block = holder[to * CAP + c]
            out[c] = grams[jnp.maximum(block, 0)]


def update(holder, left, right, *refs):
    pieces, outs = refs[:NW], refs[NW:]
    worker = lax.axis_index("worker")
    for c in range(CAP):
        filled = holder[worker * CAP + c] >= 0

        @pl.when(filled)
        def _():
            for piece, source in zip(pieces, sources(worker)):
                cols = pl.ds(pl.multiple_of(source * PART, PART), PART)
                for n, (old, new) in enumerate(zip((left, right), outs)):
                    gram = piece[c, n * ROWS : (n + 1) * ROWS, :].astype(f32)
                    new[c, :, cols] = decay_rate * old[c, :, cols] + (1.0 - decay_rate) * gram

        @pl.when(jnp.logical_not(filled))
        def _():
            for old, new in zip((left, right), outs):
                new[c] = old[c]


def assemble(*refs):
    pieces, out = refs[:NW], refs[NW]
    worker = lax.axis_index("worker")
    for piece, source in zip(pieces, sources(worker)):
        out[:, :, pl.ds(pl.multiple_of(source * PART, PART), PART)] = piece[...]


def over_shard(value):
    return lax.all_to_all(value, "shard", 0, 0, tiled=True)


def body(grads, owners, left, right, left_root, right_root):
    worker = lax.axis_index("worker")
    with jax.named_scope("roots"):
        *packed, holder = call(
            pack_roots,
            [shape((2 * CAP * ROWS + 16, PART))] * NW + [shape((NW * CAP,), jnp.int32)],
            (owners[:, 0], left_root[0], right_root[0]),
            [SMEM, VMEM, VMEM],
            [VMEM] * NW + [SMEM],
        )
        packed = exchange(packed)
    with jax.named_scope("gradients"):
        mine = lax.dynamic_slice_in_dim(grads, worker * PART, PART, 2)
        mine = over_shard(mine).reshape(BS, PART)
        columns = gather(mine)
    with jax.named_scope("roots"):
        root_l, root_r = call(
            pick_roots,
            [shape((NB, ROWS, PART)), shape((NB, ROWS + 16, PART))],
            (holder, *packed),
            [SMEM] + [VMEM] * NW,
        )
        root_l = over_shard(root_l).reshape(BS, PART)
        root_l = gather(root_l)
        root_r = over_shard(root_r)
    with jax.named_scope("grams"):
        grams = call(
            make_grams, shape((NB, 2 * ROWS, PART)), tuple(columns), flops=4 * BS * BS * PART
        )
        grams = over_shard(grams)
        grams = call(
            pack_grams,
            [shape((CAP, 2 * ROWS, PART))] * NW,
            (holder, grams),
            [SMEM, VMEM],
        )
        grams = exchange(grams)
    with jax.named_scope("precondition"):
        image = call(
            make_image, shape((BS, PART)), (root_r, *columns), flops=2 * BS * BS * PART
        )
        result = call(
            make_result,
            shape((NB, ROWS, PART)),
            (root_r, image, *root_l),
            flops=2 * BS * BS * PART,
        )
        result = gather(over_shard(result))
        precond = call(assemble, shape((NB, ROWS, BS)), tuple(result), nbytes=4 << 20)
    with jax.named_scope("factors"):
        factor = shape((CAP, ROWS, BS), f32)
        new_left, new_right = call(
            update,
            [factor, factor],
            (holder, left[0], right[0], *grams),
            [SMEM] + [VMEM] * (2 + NW),
        )
    return new_left[None], new_right[None], precond


def solution(mesh):
    factor = P("worker", None, "shard", None)
    return jax.shard_map(
        body,
        mesh=mesh,
        in_specs=(P(None, "shard", None), P(), factor, factor, factor, factor),
        out_specs=(factor, factor, P(None, "shard", None)),
        check_vma=False,
    )
```

time: 324 us -> 178 us (0.55)
  waiting for transfers between devices: 250 us -> 44 us
  starting transfers between devices: 0.3 us -> 79.6 us
  matrix products: 49.8 us -> 0 us
  blocking collectives: 0 us -> 19 us
  Pallas kernels: 0 us -> 18.2 us
  between operations: 13.8 us -> 0.81 us
  local copies, waits for them, and re-layouts: 4.89 us -> 15.3 us
  other arithmetic: 4.96 us -> 0 us
    all_gather x3 -> x0, waiting for transfers between devices: 250 us -> none  [the longest x1 123 us: body(): piece = lax.all_gather(local_g, 'shard', axis=1, tiled=True)]
    dot_general x5 -> x0, matrix products: 49.8 us -> none  [the longest x1 14.6 us: body(): jnp.einsum('cri,cji->crj', root_left, lax.all_gather(image_b, 'shard', ax...]
    ppermute x0 -> x35, starting transfers between devices: none -> 45.5 us  [send(): lax.ppermute(value, 'worker', [(w, partner(w, k, other)) for w in range(N...]
    all_to_all x0 -> x4, starting transfers between devices: none -> 34.1 us  [over_shard(): return lax.all_to_all(value, 'shard', 0, 0, tiled=True)]
    ppermute x0 -> x35, waiting for transfers between devices: none -> 27.8 us  [send(): lax.ppermute(value, 'worker', [(w, partner(w, k, other)) for w in range(N...]
    all_to_all x0 -> x1, blocking collectives: none -> 19 us  [over_shard(): return lax.all_to_all(value, 'shard', 0, 0, tiled=True)]
    pallas_call x0 -> x8, Pallas kernels: none -> 18.2 us  [call(): pl.pallas_call(kernel, out_shape=outs, in_specs=in_specs or [VMEM] * len(...]
    all_to_all x0 -> x4, waiting for transfers between devices: none -> 16.2 us  [over_shard(): return lax.all_to_all(value, 'shard', 0, 0, tiled=True)]
  transfers between devices with their start and end apart: 3 -> 39, of which waited for: 3 -> 12; matrix products, arithmetic and copies ran while one was open for 6% -> 0% of each run, Pallas kernels for 0% -> 7%
where the time goes in v2:
time: 178 us; the launch traced here: 177 us
  starting transfers between devices  79.6 us (45%)
  waiting for transfers between devices  44 us (25%)
  blocking collectives  19 us (11%)
  Pallas kernels  18.2 us (10%)
  local copies, waits for them, and re-layouts  15.3 us (9%)
    ppermute x35, starting transfers between devices, send(): lax.ppermute(value, 'worker', [(w, partner(w, k, other)) for w in range(N...  45.5 us
    all_to_all x4, starting transfers between devices, over_shard(): return lax.all_to_all(value, 'shard', 0, 0, tiled=True)  34.1 us
    ppermute x35, waiting for transfers between devices, send(): lax.ppermute(value, 'worker', [(w, partner(w, k, other)) for w in range(N...  27.8 us
    all_to_all x1, blocking collectives, over_shard(): return lax.all_to_all(value, 'shard', 0, 0, tiled=True)  19 us
    pallas_call x8, Pallas kernels, call(): pl.pallas_call(kernel, out_shape=outs, in_specs=in_specs or [VMEM] * len(...  18.2 us
    all_to_all x4, waiting for transfers between devices, over_shard(): return lax.all_to_all(value, 'shard', 0, 0, tiled=True)  16.2 us
    unnamed x30, local copies, waits for them, and re-layouts  14.6 us
  transfers between devices with their start and end apart: 39, of which 12 were waited for; matrix products, arithmetic and copies ran while one was open for 0% of the time, Pallas kernels for 7%

profile of v2, /device:TPU:1, one launch (start us, length us, event | category | flops | bytes accessed | tf_op | source)
XLA Modules:
  0.0 177.0 jit_solution(4675160285236114332)
XLA Ops:
  0.6 1.6 copy-done
  3.0 12.0 %all-to-all-start = ((bf16[32,32,128]{2,1,0:T(8,128)(2,1)}), bf16[32,32,128]{2,1,0:T(8,128)(2,1)S(1)}, u32[]{:S(2)}, u32[]{:S(2)}) async-start(bf16[32,32,128]{2,1,0:T(8,128)(2,1)} %constant_dynamic-slice_fusion), calls=%async_computation | async-start | bytes 524288 | tf_op jit(solution)/shard_map/gradients/all_to_all | solution.py:210
  15.1 1.1 copy-done.12
  16.2 1.1 copy-done.13
  18.0 3.2 %roots.2 = (bf16[400,128]{1,0:T(8,128)(2,1)S(1)}, bf16[400,128]{1,0:T(8,128)(2,1)S(1)}, bf16[400,128]{1,0:T(8,128)(2,1)S(1)}, bf16[400,128]{1,0:T(8,128)(2,1)S(1...) custom-call(s32[32]{0:T(128)S(1)} %bitcast.24, ...), custom_call_target="tpu_custom_call" | custom-call | bytes 2097152 | tf_op jit(solution)/shard_map/roots/pallas_call | solution.py:54
  21.2 1.0 collective-permute-start.14
  22.3 1.2 collective-permute-start.15
  23.5 1.5 collective-permute-start.16
  24.9 1.4 collective-permute-start.17
  26.4 1.9 %collective-permute-start.18 = (bf16[400,128]{1,0:T(8,128)(2,1)S(1)}, bf16[400,128]{1,0:T(8,128)(2,1)S(1)}, u32[]{:S(2)}, u32[]{:S(2)}) collective-permute-start(bf16[400,128]{1,0:T(8,128)(2,1)S(1)} %get-tuple-element.40), channel_id=1, source_target_pairs={{0,5},{1,4},{2,7},{3,6},{4,1},{5,0},{6,3},{7,2},{8,13},{9,12},{10,... | collective-permute-start | bytes 307208 | tf_op jit(solution)/shard_map/roots/ppermute | solution.py:30
  28.2 1.5 collective-permute-start.19
  30.4 2.9 %collective-permute-done.17.refs_4_ = bf16[400,128]{1,0:T(8,128)(2,1)S(1)} collective-permute-done((bf16[400,128]{1,0:T(8,128)(2,1)S(1)}, bf16[400,128]{1,0:T(8,128)(2,1)S(1)}, u32[]{:S(2)}, u32[]{:S(2)}) %collective-permute-start.17) | collective-permute-done | bytes 102432 | tf_op jit(solution)/shard_map/roots/ppermute | solution.py:30
  33.3 2.4 %collective-permute-done.18.refs_5_ = bf16[400,128]{1,0:T(8,128)(2,1)S(1)} collective-permute-done((bf16[400,128]{1,0:T(8,128)(2,1)S(1)}, bf16[400,128]{1,0:T(8,128)(2,1)S(1)}, u32[]{:S(2)}, u32[]{:S(2)}) %collective-permute-start.18) | collective-permute-done | bytes 102432 | tf_op jit(solution)/shard_map/roots/ppermute | solution.py:30
  35.7 1.1 collective-permute-done.20.refs_7_
  36.8 1.7 roots.3
  38.5 19.0 %all_to_all.25 = bf16[32,32,128]{2,1,0:T(8,128)(2,1)S(1)} all-to-all(bf16[32,32,128]{2,1,0:T(8,128)(2,1)S(1)} %get-tuple-element.44), channel_id=1, replica_groups=mesh['shard'=32,'worker'=8] {'shard'}, dimensions={0} | all-to-all | bytes 524288 | tf_op jit(solution)/shard_map/roots/all_to_all | solution.py:210
  57.5 6.5 %all-to-all-start.2 = ((bf16[32,48,128]{2,1,0:T(8,128)(2,1)}), bf16[32,48,128]{2,1,0:T(8,128)(2,1)S(1)}, u32[]{:S(2)}, u32[]{:S(2)}) async-start(bf16[32,48,128]{2,1,0:T(8,128)(2,1)} %get-tuple-element.43), calls=%async_computation.2 | async-start | bytes 786432 | tf_op jit(solution)/shard_map/roots/all_to_all | solution.py:210
  64.0 2.7 %collective-permute-start.5 = (bf16[1024,128]{1,0:T(8,128)(2,1)S(1)}, bf16[1024,128]{1,0:T(8,128)(2,1)S(1)}, u32[]{:S(2)}, u32[]{:S(2)}) collective-permute-start(bf16[1024,128]{1,0:T(8,128)(2,1)S(1)} %bitcast.9), channel_id=1, source_target_pairs={{0,6},{1,7},{2,0},{3,1},{4,2},{5,3},{6,4},{7,5},{8,14},{9,15},{10,... | collective-permute-start | bytes 786440 | tf_op jit(solution)/shard_map/gradients/ppermute | solution.py:30
  66.7 1.2 collective-permute-start.3
  67.9 2.2 %collective-permute-start = (bf16[1024,128]{1,0:T(8,128)(2,1)S(1)}, bf16[1024,128]{1,0:T(8,128)(2,1)S(1)}, u32[]{:S(2)}, u32[]{:S(2)}) collective-permute-start(bf16[1024,128]{1,0:T(8,128)(2,1)S(1)} %bitcast.12), channel_id=1, source_target_pairs={{0,1},{1,0},{2,3},{3,2},{4,5},{5,4},{6,7},{7,6},{8,9},{9,8},{10,11... | collective-permute-start | bytes 786440 | tf_op jit(solution)/shard_map/gradients/ppermute | solution.py:30
  70.1 3.0 %collective-permute-start.26 = (bf16[1024,128]{1,0:T(8,128)(2,1)S(1)}, bf16[1024,128]{1,0:T(8,128)(2,1)}, u32[]{:S(2)}, u32[]{:S(2)}) collective-permute-start(bf16[1024,128]{1,0:T(8,128)(2,1)S(1)} %bitcast.15), channel_id=1, source_target_pairs={{0,6},{1,7},{2,0},{3,1},{4,2},{5,3},{6,4},{7,5},{8,14},{9,15},{10,... | collective-permute-start | bytes 786440 | tf_op jit(solution)/shard_map/roots/ppermute | solution.py:30
  74.1 4.6 %collective-permute-start.22 = (bf16[1024,128]{1,0:T(8,128)(2,1)S(1)}, bf16[1024,128]{1,0:T(8,128)(2,1)}, u32[]{:S(2)}, u32[]{:S(2)}) collective-permute-start(bf16[1024,128]{1,0:T(8,128)(2,1)S(1)} %bitcast.17), channel_id=1, source_target_pairs={{0,2},{1,3},{2,4},{3,5},{4,6},{5,7},{6,0},{7,1},{8,10},{9,11},{10,... | collective-permute-start | bytes 786440 | tf_op jit(solution)/shard_map/roots/ppermute | solution.py:30
  78.7 5.4 %collective-permute-done.1.refs_2_ = bf16[1024,128]{1,0:T(8,128)(2,1)} collective-permute-done((bf16[1024,128]{1,0:T(8,128)(2,1)S(1)}, bf16[1024,128]{1,0:T(8,128)(2,1)}, u32[]{:S(2)}, u32[]{:S(2)}) %collective-permute-start.1) | collective-permute-done | bytes 262176 | tf_op jit(solution)/shard_map/gradients/ppermute | solution.py:30
  84.2 2.0 %collective-permute-start.6 = (bf16[1024,128]{1,0:T(8,128)(2,1)S(1)}, bf16[1024,128]{1,0:T(8,128)(2,1)S(1)}, u32[]{:S(2)}, u32[]{:S(2)}) collective-permute-start(bf16[1024,128]{1,0:T(8,128)(2,1)S(1)} %collective-permute-done.5.refs_6_), channel_id=1, source_target_pairs={{0,1},{1,0},{2,3},{3,2},{4,5},{5,4},{6,7},{7,6},{8,9},{9,8},{10,11... | collective-permute-start | bytes 786440 | tf_op jit(solution)/shard_map/gradients/ppermute | solution.py:30
  86.9 3.2 %collective-permute-start.2 = (bf16[1024,128]{1,0:T(8,128)(2,1)}, bf16[1024,128]{1,0:T(8,128)(2,1)}, u32[]{:S(2)}, u32[]{:S(2)}) collective-permute-start(bf16[1024,128]{1,0:T(8,128)(2,1)} %collective-permute-done.1.refs_2_), channel_id=1, source_target_pairs={{0,1},{1,0},{2,3},{3,2},{4,5},{5,4},{6,7},{7,6},{8,9},{9,8},{10,11... | collective-permute-start | bytes 786440 | tf_op jit(solution)/shard_map/gradients/ppermute | solution.py:30
  90.7 2.5 %collective-permute-done.22.refs_2_ = bf16[1024,128]{1,0:T(8,128)(2,1)} collective-permute-done((bf16[1024,128]{1,0:T(8,128)(2,1)S(1)}, bf16[1024,128]{1,0:T(8,128)(2,1)}, u32[]{:S(2)}, u32[]{:S(2)}) %collective-permute-start.22) | collective-permute-done | bytes 262176 | tf_op jit(solution)/shard_map/roots/ppermute | solution.py:30
  97.7 0.9 copy-done.8
  98.6 1.7 precondition.3.image
  100.4 2.9 %precondition.4 = bf16[32,32,128]{2,1,0:T(8,128)(2,1)} custom-call(bf16[32,48,128]{2,1,0:T(8,128)(2,1)S(1)} %all-to-all-done.2.right, bf16[1024,128]{1,0:T(8,128)(2,1)S(1)} %precondition.3.image, bf16[1024,128]{1,0:T(8,128)(2,1)S(1)} %bitcast.19, bf16[1024,128]{1,0:T(8,128)(2,1)} %collective-permute-done.21.refs_1_, ...), custom_call_target="tpu_custom_call" | custom-call | flops 268435456 | bytes 2097152 | tf_op jit(solution)/shard_map/precondition/pallas_call | solution.py:54
  103.3 9.2 %all-to-all-start.4 = ((bf16[32,32,128]{2,1,0:T(8,128)(2,1)}), bf16[32,32,128]{2,1,0:T(8,128)(2,1)S(1)}, u32[]{:S(2)}, u32[]{:S(2)}) async-start(bf16[32,32,128]{2,1,0:T(8,128)(2,1)} %precondition.4), calls=%async_computation.4 | async-start | bytes 524288 | tf_op jit(solution)/shard_map/precondition/all_to_all | solution.py:210
  113.5 0.9 copy-done.6
  115.4 3.1 %grams.2 = bf16[32,64,128]{2,1,0:T(8,128)(2,1)} custom-call(bf16[1024,128]{1,0:T(8,128)(2,1)S(1)} %bitcast.14, bf16[1024,128]{1,0:T(8,128)(2,1)S(1)} %copy-done.3, bf16[1024,128]{1,0:T(8,128)(2,1)} %collective-permute-done.1.refs_2_, bf16[1024,128]{1,0:T(8,128)(2,1)} %collective-permute-done.2.refs_3_, bf16[1024,128]{1,0:T(8,128)(2,1)S(1)} %collective-permute-done.3.refs_4_, ...), custom_call_target="tpu_custom_call" | custom-call | flops 536870912 | bytes 2097152 | tf_op jit(solution)/shard_map/grams/pallas_call | solution.py:54
  118.5 4.3 %all-to-all-done.4.refs_0_ = bf16[32,32,128]{2,1,0:T(8,128)(2,1)S(1)} async-done(((bf16[32,32,128]{2,1,0:T(8,128)(2,1)}), bf16[32,32,128]{2,1,0:T(8,128)(2,1)S(1)}, u32[]{:S(2)}, u32[]{:S(2)}) %all-to-all-start.4) | async-done | bytes 262176 | tf_op jit(solution)/shard_map/precondition/all_to_all | solution.py:210
  122.8 6.3 %all-to-all-start.1 = ((bf16[32,64,128]{2,1,0:T(8,128)(2,1)}), bf16[32,64,128]{2,1,0:T(8,128)(2,1)S(1)}, u32[]{:S(2)}, u32[]{:S(2)}) async-start(bf16[32,64,128]{2,1,0:T(8,128)(2,1)} %grams.2), calls=%async_computation.1 | async-start | bytes 1048576 | tf_op jit(solution)/shard_map/grams/all_to_all | solution.py:210
  129.6 1.2 collective-permute-start.31
  131.3 11.9 %all-to-all-done.1.grams = bf16[32,64,128]{2,1,0:T(8,128)(2,1)S(1)} async-done(((bf16[32,64,128]{2,1,0:T(8,128)(2,1)}), bf16[32,64,128]{2,1,0:T(8,128)(2,1)S(1)}, u32[]{:S(2)}, u32[]{:S(2)}) %all-to-all-start.1) | async-done | bytes 524320 | tf_op jit(solution)/shard_map/grams/all_to_all | solution.py:210
  143.9 4.1 %collective-permute-start.7 = (bf16[6,64,128]{2,1,0:T(8,128)(2,1)S(1)}, bf16[6,64,128]{2,1,0:T(8,128)(2,1)S(1)}, u32[]{:S(2)}, u32[]{:S(2)}) collective-permute-start(bf16[6,64,128]{2,1,0:T(8,128)(2,1)S(1)} %get-tuple-element.26), channel_id=1, source_target_pairs={{0,1},{1,0},{2,3},{3,2},{4,5},{5,4},{6,7},{7,6},{8,9},{9,8},{10,11... | collective-permute-start | bytes 294920 | tf_op jit(solution)/shard_map/grams/ppermute | solution.py:30
  148.0 1.2 collective-permute-start.9
  149.2 2.9 %collective-permute-start.10 = (bf16[6,64,128]{2,1,0:T(8,128)(2,1)S(1)}, bf16[6,64,128]{2,1,0:T(8,128)(2,1)S(1)}, u32[]{:S(2)}, u32[]{:S(2)}) collective-permute-start(bf16[6,64,128]{2,1,0:T(8,128)(2,1)S(1)} %get-tuple-element.29), channel_id=1, source_target_pairs={{0,4},{1,5},{2,6},{3,7},{4,0},{5,1},{6,2},{7,3},{8,12},{9,13},{10,... | collective-permute-start | bytes 294920 | tf_op jit(solution)/shard_map/grams/ppermute | solution.py:30
  153.6 1.3 collective-permute-start.34
  154.9 5.2 %collective-permute-done.9.refs_3_ = bf16[6,64,128]{2,1,0:T(8,128)(2,1)S(1)} collective-permute-done((bf16[6,64,128]{2,1,0:T(8,128)(2,1)S(1)}, bf16[6,64,128]{2,1,0:T(8,128)(2,1)S(1)}, u32[]{:S(2)}, u32[]{:S(2)}) %collective-permute-start.9) | collective-permute-done | bytes 98336 | tf_op jit(solution)/shard_map/grams/ppermute | solution.py:30
  160.6 4.2 %collective-permute-done.12.refs_6_ = bf16[6,64,128]{2,1,0:T(8,128)(2,1)S(1)} collective-permute-done((bf16[6,64,128]{2,1,0:T(8,128)(2,1)S(1)}, bf16[6,64,128]{2,1,0:T(8,128)(2,1)S(1)}, u32[]{:S(2)}, u32[]{:S(2)}) %collective-permute-start.12) | collective-permute-done | bytes 98336 | tf_op jit(solution)/shard_map/grams/ppermute | solution.py:30
  164.8 2.1 %collective-permute-start.13 = (bf16[6,64,128]{2,1,0:T(8,128)(2,1)S(1)}, bf16[6,64,128]{2,1,0:T(8,128)(2,1)S(1)}, u32[]{:S(2)}, u32[]{:S(2)}) collective-permute-start(bf16[6,64,128]{2,1,0:T(8,128)(2,1)S(1)} %get-tuple-element.32), channel_id=1, source_target_pairs={{0,7},{1,6},{2,1},{3,0},{4,3},{5,2},{6,5},{7,4},{8,15},{9,14},{10,... | collective-permute-start | bytes 294920 | tf_op jit(solution)/shard_map/grams/ppermute | solution.py:30
  166.9 2.9 %collective-permute-done.13.refs_7_ = bf16[6,64,128]{2,1,0:T(8,128)(2,1)S(1)} collective-permute-done((bf16[6,64,128]{2,1,0:T(8,128)(2,1)S(1)}, bf16[6,64,128]{2,1,0:T(8,128)(2,1)S(1)}, u32[]{:S(2)}, u32[]{:S(2)}) %collective-permute-start.13) | collective-permute-done | bytes 98336 | tf_op jit(solution)/shard_map/grams/ppermute | solution.py:30
  169.8 1.1 copy-done.10
  171.0 1.1 copy-done.11
  172.1 1.9 %factors.1 = (f32[6,32,1024]{2,1,0:T(8,128)}, f32[6,32,1024]{2,1,0:T(8,128)}) custom-call(s32[48]{0:T(128)S(1)} %get-tuple-element.24.holder, f32[6,32,1024]{2,1,0:T(8,128)S(1)} %bitcast.20, f32[6,32,1024]{2,1,0:T(8,128)S(1)} %bitcast.21, bf16[6,64,128]{2,1,0:T(8,128)(2,1)S(1)} %get-tuple-element.25.refs_0_, ...), custom_call_target="tpu_custom_call" | custom-call | bytes 2097152 | tf_op jit(solution)/shard_map/factors/pallas_call | solution.py:54
  174.1 2.9 %precondition.5 = bf16[32,32,1024]{2,1,0:T(8,128)(2,1)} custom-call(bf16[32,32,128]{2,1,0:T(8,128)(2,1)S(1)} %all-to-all-done.4.refs_0_, bf16[32,32,128]{2,1,0:T(8,128)(2,1)S(1)} %collective-permute-done.28.refs_1_, bf16[32,32,128]{2,1,0:T(8,128)(2,1)} %collective-permute-done.29.refs_2_, bf16[32,32,128]{2,1,0:T(8,128)(2,1)S(1)} %collective-permute-done.30.refs_3_, ...), custom_call_target="tpu_custom_call" | custom-call | bytes 4194304 | tf_op jit(solution)/shard_map/precondition/pallas_call | solution.py:54
  (70 shorter events, 14.5 us)
Async XLA Ops:
  0.6 1.6 copy-start
  3.0 35.5 %all-to-all-start = ((bf16[32,32,128]{2,1,0:T(8,128)(2,1)}), bf16[32,32,128]{2,1,0:T(8,128)(2,1)S(1)}, u32[]{:S(2)}, u32[]{:S(2)}) async-start(bf16[32,32,128]{2,1,0:T(8,128)(2,1)} %constant_dynamic-slice_fusion), calls=%async_computation | async-start | bytes 524288 | tf_op jit(solution)/shard_map/gradients/all_to_all | solution.py:210
  15.0 1.1 copy-start.12
  16.2 1.1 copy-start.13
  21.2 7.0 %collective-permute-start.14 = (bf16[400,128]{1,0:T(8,128)(2,1)S(1)}, bf16[400,128]{1,0:T(8,128)(2,1)S(1)}, u32[]{:S(2)}, u32[]{:S(2)}) collective-permute-start(bf16[400,128]{1,0:T(8,128)(2,1)S(1)} %get-tuple-element.36), channel_id=1, source_target_pairs={{0,1},{1,0},{2,3},{3,2},{4,5},{5,4},{6,7},{7,6},{8,9},{9,8},{10,11... | collective-permute-start | bytes 307208 | tf_op jit(solution)/shard_map/roots/ppermute | solution.py:30
  22.3 7.5 %collective-permute-start.15 = (bf16[400,128]{1,0:T(8,128)(2,1)S(1)}, bf16[400,128]{1,0:T(8,128)(2,1)S(1)}, u32[]{:S(2)}, u32[]{:S(2)}) collective-permute-start(bf16[400,128]{1,0:T(8,128)(2,1)S(1)} %get-tuple-element.37), channel_id=1, source_target_pairs={{0,2},{1,3},{2,4},{3,5},{4,6},{5,7},{6,0},{7,1},{8,10},{9,11},{10,... | collective-permute-start | bytes 307208 | tf_op jit(solution)/shard_map/roots/ppermute | solution.py:30
  23.5 6.9 %collective-permute-start.16 = (bf16[400,128]{1,0:T(8,128)(2,1)S(1)}, bf16[400,128]{1,0:T(8,128)(2,1)S(1)}, u32[]{:S(2)}, u32[]{:S(2)}) collective-permute-start(bf16[400,128]{1,0:T(8,128)(2,1)S(1)} %get-tuple-element.38), channel_id=1, source_target_pairs={{0,3},{1,2},{2,5},{3,4},{4,7},{5,6},{6,1},{7,0},{8,11},{9,10},{10,... | collective-permute-start | bytes 307208 | tf_op jit(solution)/shard_map/roots/ppermute | solution.py:30
  24.9 8.4 %collective-permute-start.17 = (bf16[400,128]{1,0:T(8,128)(2,1)S(1)}, bf16[400,128]{1,0:T(8,128)(2,1)S(1)}, u32[]{:S(2)}, u32[]{:S(2)}) collective-permute-start(bf16[400,128]{1,0:T(8,128)(2,1)S(1)} %get-tuple-element.39), channel_id=1, source_target_pairs={{0,4},{1,5},{2,6},{3,7},{4,0},{5,1},{6,2},{7,3},{8,12},{9,13},{10,... | collective-permute-start | bytes 307208 | tf_op jit(solution)/shard_map/roots/ppermute | solution.py:30
  26.4 9.3 %collective-permute-start.18 = (bf16[400,128]{1,0:T(8,128)(2,1)S(1)}, bf16[400,128]{1,0:T(8,128)(2,1)S(1)}, u32[]{:S(2)}, u32[]{:S(2)}) collective-permute-start(bf16[400,128]{1,0:T(8,128)(2,1)S(1)} %get-tuple-element.40), channel_id=1, source_target_pairs={{0,5},{1,4},{2,7},{3,6},{4,1},{5,0},{6,3},{7,2},{8,13},{9,12},{10,... | collective-permute-start | bytes 307208 | tf_op jit(solution)/shard_map/roots/ppermute | solution.py:30
  28.2 7.4 %collective-permute-start.19 = (bf16[400,128]{1,0:T(8,128)(2,1)S(1)}, bf16[400,128]{1,0:T(8,128)(2,1)S(1)}, u32[]{:S(2)}, u32[]{:S(2)}) collective-permute-start(bf16[400,128]{1,0:T(8,128)(2,1)S(1)} %get-tuple-element.41), channel_id=1, source_target_pairs={{0,6},{1,7},{2,0},{3,1},{4,2},{5,3},{6,4},{7,5},{8,14},{9,15},{10,... | collective-permute-start | bytes 307208 | tf_op jit(solution)/shard_map/roots/ppermute | solution.py:30
  29.7 7.1 %collective-permute-start.20 = (bf16[400,128]{1,0:T(8,128)(2,1)S(1)}, bf16[400,128]{1,0:T(8,128)(2,1)S(1)}, u32[]{:S(2)}, u32[]{:S(2)}) collective-permute-start(bf16[400,128]{1,0:T(8,128)(2,1)S(1)} %get-tuple-element.42), channel_id=1, source_target_pairs={{0,7},{1,6},{2,1},{3,0},{4,3},{5,2},{6,5},{7,4},{8,15},{9,14},{10,... | collective-permute-start | bytes 307208 | tf_op jit(solution)/shard_map/roots/ppermute | solution.py:30
  57.5 38.3 %all-to-all-start.2 = ((bf16[32,48,128]{2,1,0:T(8,128)(2,1)}), bf16[32,48,128]{2,1,0:T(8,128)(2,1)S(1)}, u32[]{:S(2)}, u32[]{:S(2)}) async-start(bf16[32,48,128]{2,1,0:T(8,128)(2,1)} %get-tuple-element.43), calls=%async_computation.2 | async-start | bytes 786432 | tf_op jit(solution)/shard_map/roots/all_to_all | solution.py:210
  64.0 9.0 %collective-permute-start.5 = (bf16[1024,128]{1,0:T(8,128)(2,1)S(1)}, bf16[1024,128]{1,0:T(8,128)(2,1)S(1)}, u32[]{:S(2)}, u32[]{:S(2)}) collective-permute-start(bf16[1024,128]{1,0:T(8,128)(2,1)S(1)} %bitcast.9), channel_id=1, source_target_pairs={{0,6},{1,7},{2,0},{3,1},{4,2},{5,3},{6,4},{7,5},{8,14},{9,15},{10,... | collective-permute-start | bytes 786440 | tf_op jit(solution)/shard_map/gradients/ppermute | solution.py:30
  66.7 7.4 %collective-permute-start.3 = (bf16[1024,128]{1,0:T(8,128)(2,1)S(1)}, bf16[1024,128]{1,0:T(8,128)(2,1)S(1)}, u32[]{:S(2)}, u32[]{:S(2)}) collective-permute-start(bf16[1024,128]{1,0:T(8,128)(2,1)S(1)} %bitcast.10), channel_id=1, source_target_pairs={{0,4},{1,5},{2,6},{3,7},{4,0},{5,1},{6,2},{7,3},{8,12},{9,13},{10,... | collective-permute-start | bytes 786440 | tf_op jit(solution)/shard_map/gradients/ppermute | solution.py:30
  67.9 16.3 %collective-permute-start.1 = (bf16[1024,128]{1,0:T(8,128)(2,1)S(1)}, bf16[1024,128]{1,0:T(8,128)(2,1)}, u32[]{:S(2)}, u32[]{:S(2)}) collective-permute-start(bf16[1024,128]{1,0:T(8,128)(2,1)S(1)} %bitcast.11), channel_id=1, source_target_pairs={{0,2},{1,3},{2,4},{3,5},{4,6},{5,7},{6,0},{7,1},{8,10},{9,11},{10,... | collective-permute-start | bytes 786440 | tf_op jit(solution)/shard_map/gradients/ppermute | solution.py:30
  67.9 18.3 %collective-permute-start = (bf16[1024,128]{1,0:T(8,128)(2,1)S(1)}, bf16[1024,128]{1,0:T(8,128)(2,1)S(1)}, u32[]{:S(2)}, u32[]{:S(2)}) collective-permute-start(bf16[1024,128]{1,0:T(8,128)(2,1)S(1)} %bitcast.12), channel_id=1, source_target_pairs={{0,1},{1,0},{2,3},{3,2},{4,5},{5,4},{6,7},{7,6},{8,9},{9,8},{10,11... | collective-permute-start | bytes 786440 | tf_op jit(solution)/shard_map/gradients/ppermute | solution.py:30
  70.1 16.8 %collective-permute-start.26 = (bf16[1024,128]{1,0:T(8,128)(2,1)S(1)}, bf16[1024,128]{1,0:T(8,128)(2,1)}, u32[]{:S(2)}, u32[]{:S(2)}) collective-permute-start(bf16[1024,128]{1,0:T(8,128)(2,1)S(1)} %bitcast.15), channel_id=1, source_target_pairs={{0,6},{1,7},{2,0},{3,1},{4,2},{5,3},{6,4},{7,5},{8,14},{9,15},{10,... | collective-permute-start | bytes 786440 | tf_op jit(solution)/shard_map/roots/ppermute | solution.py:30
  73.0 17.0 %collective-permute-start.24 = (bf16[1024,128]{1,0:T(8,128)(2,1)S(1)}, bf16[1024,128]{1,0:T(8,128)(2,1)}, u32[]{:S(2)}, u32[]{:S(2)}) collective-permute-start(bf16[1024,128]{1,0:T(8,128)(2,1)S(1)} %bitcast.16), channel_id=1, source_target_pairs={{0,4},{1,5},{2,6},{3,7},{4,0},{5,1},{6,2},{7,3},{8,12},{9,13},{10,... | collective-permute-start | bytes 786440 | tf_op jit(solution)/shard_map/roots/ppermute | solution.py:30
  74.1 19.1 %collective-permute-start.22 = (bf16[1024,128]{1,0:T(8,128)(2,1)S(1)}, bf16[1024,128]{1,0:T(8,128)(2,1)}, u32[]{:S(2)}, u32[]{:S(2)}) collective-permute-start(bf16[1024,128]{1,0:T(8,128)(2,1)S(1)} %bitcast.17), channel_id=1, source_target_pairs={{0,2},{1,3},{2,4},{3,5},{4,6},{5,7},{6,0},{7,1},{8,10},{9,11},{10,... | collective-permute-start | bytes 786440 | tf_op jit(solution)/shard_map/roots/ppermute | solution.py:30
  84.2 9.7 %collective-permute-start.6 = (bf16[1024,128]{1,0:T(8,128)(2,1)S(1)}, bf16[1024,128]{1,0:T(8,128)(2,1)S(1)}, u32[]{:S(2)}, u32[]{:S(2)}) collective-permute-start(bf16[1024,128]{1,0:T(8,128)(2,1)S(1)} %collective-permute-done.5.refs_6_), channel_id=1, source_target_pairs={{0,1},{1,0},{2,3},{3,2},{4,5},{5,4},{6,7},{7,6},{8,9},{9,8},{10,11... | collective-permute-start | bytes 786440 | tf_op jit(solution)/shard_map/gradients/ppermute | solution.py:30
  86.9 7.7 %collective-permute-start.4 = (bf16[1024,128]{1,0:T(8,128)(2,1)S(1)}, bf16[1024,128]{1,0:T(8,128)(2,1)S(1)}, u32[]{:S(2)}, u32[]{:S(2)}) collective-permute-start(bf16[1024,128]{1,0:T(8,128)(2,1)S(1)} %collective-permute-done.3.refs_4_), channel_id=1, source_target_pairs={{0,1},{1,0},{2,3},{3,2},{4,5},{5,4},{6,7},{7,6},{8,9},{9,8},{10,11... | collective-permute-start | bytes 786440 | tf_op jit(solution)/shard_map/gradients/ppermute | solution.py:30
  86.9 8.9 %collective-permute-start.2 = (bf16[1024,128]{1,0:T(8,128)(2,1)}, bf16[1024,128]{1,0:T(8,128)(2,1)}, u32[]{:S(2)}, u32[]{:S(2)}) collective-permute-start(bf16[1024,128]{1,0:T(8,128)(2,1)} %collective-permute-done.1.refs_2_), channel_id=1, source_target_pairs={{0,1},{1,0},{2,3},{3,2},{4,5},{5,4},{6,7},{7,6},{8,9},{9,8},{10,11... | collective-permute-start | bytes 786440 | tf_op jit(solution)/shard_map/gradients/ppermute | solution.py:30
  90.1 10.3 %collective-permute-start.21 = (bf16[1024,128]{1,0:T(8,128)(2,1)S(1)}, bf16[1024,128]{1,0:T(8,128)(2,1)}, u32[]{:S(2)}, u32[]{:S(2)}) collective-permute-start(bf16[1024,128]{1,0:T(8,128)(2,1)S(1)} %bitcast.18), channel_id=1, source_target_pairs={{0,1},{1,0},{2,3},{3,2},{4,5},{5,4},{6,7},{7,6},{8,9},{9,8},{10,11... | collective-permute-start | bytes 786440 | tf_op jit(solution)/shard_map/roots/ppermute | solution.py:30
  93.2 7.1 %collective-permute-start.27 = (bf16[1024,128]{1,0:T(8,128)(2,1)}, bf16[1024,128]{1,0:T(8,128)(2,1)}, u32[]{:S(2)}, u32[]{:S(2)}) collective-permute-start(bf16[1024,128]{1,0:T(8,128)(2,1)} %collective-permute-done.26.refs_6_), channel_id=1, source_target_pairs={{0,1},{1,0},{2,3},{3,2},{4,5},{5,4},{6,7},{7,6},{8,9},{9,8},{10,11... | collective-permute-start | bytes 786440 | tf_op jit(solution)/shard_map/roots/ppermute | solution.py:30
  94.5 5.8 %collective-permute-start.25 = (bf16[1024,128]{1,0:T(8,128)(2,1)}, bf16[1024,128]{1,0:T(8,128)(2,1)}, u32[]{:S(2)}, u32[]{:S(2)}) collective-permute-start(bf16[1024,128]{1,0:T(8,128)(2,1)} %collective-permute-done.24.refs_4_), channel_id=1, source_target_pairs={{0,1},{1,0},{2,3},{3,2},{4,5},{5,4},{6,7},{7,6},{8,9},{9,8},{10,11... | collective-permute-start | bytes 786440 | tf_op jit(solution)/shard_map/roots/ppermute | solution.py:30
  95.3 5.1 %collective-permute-start.23 = (bf16[1024,128]{1,0:T(8,128)(2,1)}, bf16[1024,128]{1,0:T(8,128)(2,1)}, u32[]{:S(2)}, u32[]{:S(2)}) collective-permute-start(bf16[1024,128]{1,0:T(8,128)(2,1)} %collective-permute-done.22.refs_2_), channel_id=1, source_target_pairs={{0,1},{1,0},{2,3},{3,2},{4,5},{5,4},{6,7},{7,6},{8,9},{9,8},{10,11... | collective-permute-start | bytes 786440 | tf_op jit(solution)/shard_map/roots/ppermute | solution.py:30
  95.8 1.0 copy-start.2
  96.7 0.9 copy-start.5
  97.7 0.9 copy-start.8
  103.3 19.6 %all-to-all-start.4 = ((bf16[32,32,128]{2,1,0:T(8,128)(2,1)}), bf16[32,32,128]{2,1,0:T(8,128)(2,1)S(1)}, u32[]{:S(2)}, u32[]{:S(2)}) async-start(bf16[32,32,128]{2,1,0:T(8,128)(2,1)} %precondition.4), calls=%async_computation.4 | async-start | bytes 524288 | tf_op jit(solution)/shard_map/precondition/all_to_all | solution.py:210
  112.5 1.0 copy-start.3
  122.8 20.4 %all-to-all-start.1 = ((bf16[32,64,128]{2,1,0:T(8,128)(2,1)}), bf16[32,64,128]{2,1,0:T(8,128)(2,1)S(1)}, u32[]{:S(2)}, u32[]{:S(2)}) async-start(bf16[32,64,128]{2,1,0:T(8,128)(2,1)} %grams.2), calls=%async_computation.1 | async-start | bytes 1048576 | tf_op jit(solution)/shard_map/grams/all_to_all | solution.py:210
  129.2 18.8 %collective-permute-start.33 = (bf16[32,32,128]{2,1,0:T(8,128)(2,1)S(1)}, bf16[32,32,128]{2,1,0:T(8,128)(2,1)S(1)}, u32[]{:S(2)}, u32[]{:S(2)}) collective-permute-start(bf16[32,32,128]{2,1,0:T(8,128)(2,1)S(1)} %all-to-all-done.4.refs_0_), channel_id=1, source_target_pairs={{0,6},{1,7},{2,0},{3,1},{4,2},{5,3},{6,4},{7,5},{8,14},{9,15},{10,... | collective-permute-start | bytes 786440 | tf_op jit(solution)/shard_map/precondition/ppermute | solution.py:30
  129.6 19.6 %collective-permute-start.31 = (bf16[32,32,128]{2,1,0:T(8,128)(2,1)S(1)}, bf16[32,32,128]{2,1,0:T(8,128)(2,1)S(1)}, u32[]{:S(2)}, u32[]{:S(2)}) collective-permute-start(bf16[32,32,128]{2,1,0:T(8,128)(2,1)S(1)} %all-to-all-done.4.refs_0_), channel_id=1, source_target_pairs={{0,4},{1,5},{2,6},{3,7},{4,0},{5,1},{6,2},{7,3},{8,12},{9,13},{10,... | collective-permute-start | bytes 786440 | tf_op jit(solution)/shard_map/precondition/ppermute | solution.py:30
  130.8 21.3 %collective-permute-start.29 = (bf16[32,32,128]{2,1,0:T(8,128)(2,1)S(1)}, bf16[32,32,128]{2,1,0:T(8,128)(2,1)}, u32[]{:S(2)}, u32[]{:S(2)}) collective-permute-start(bf16[32,32,128]{2,1,0:T(8,128)(2,1)S(1)} %all-to-all-done.4.refs_0_), channel_id=1, source_target_pairs={{0,2},{1,3},{2,4},{3,5},{4,6},{5,7},{6,0},{7,1},{8,10},{9,11},{10,... | collective-permute-start | bytes 786440 | tf_op jit(solution)/shard_map/precondition/ppermute | solution.py:30
  143.9 8.6 %collective-permute-start.7 = (bf16[6,64,128]{2,1,0:T(8,128)(2,1)S(1)}, bf16[6,64,128]{2,1,0:T(8,128)(2,1)S(1)}, u32[]{:S(2)}, u32[]{:S(2)}) collective-permute-start(bf16[6,64,128]{2,1,0:T(8,128)(2,1)S(1)} %get-tuple-element.26), channel_id=1, source_target_pairs={{0,1},{1,0},{2,3},{3,2},{4,5},{5,4},{6,7},{7,6},{8,9},{9,8},{10,11... | collective-permute-start | bytes 294920 | tf_op jit(solution)/shard_map/grams/ppermute | solution.py:30
  148.0 5.6 %collective-permute-start.8 = (bf16[6,64,128]{2,1,0:T(8,128)(2,1)S(1)}, bf16[6,64,128]{2,1,0:T(8,128)(2,1)S(1)}, u32[]{:S(2)}, u32[]{:S(2)}) collective-permute-start(bf16[6,64,128]{2,1,0:T(8,128)(2,1)S(1)} %get-tuple-element.27), channel_id=1, source_target_pairs={{0,2},{1,3},{2,4},{3,5},{4,6},{5,7},{6,0},{7,1},{8,10},{9,11},{10,... | collective-permute-start | bytes 294920 | tf_op jit(solution)/shard_map/grams/ppermute | solution.py:30
  148.0 12.1 %collective-permute-start.9 = (bf16[6,64,128]{2,1,0:T(8,128)(2,1)S(1)}, bf16[6,64,128]{2,1,0:T(8,128)(2,1)S(1)}, u32[]{:S(2)}, u32[]{:S(2)}) collective-permute-start(bf16[6,64,128]{2,1,0:T(8,128)(2,1)S(1)} %get-tuple-element.28), channel_id=1, source_target_pairs={{0,3},{1,2},{2,5},{3,4},{4,7},{5,6},{6,1},{7,0},{8,11},{9,10},{10,... | collective-permute-start | bytes 294920 | tf_op jit(solution)/shard_map/grams/ppermute | solution.py:30
  149.2 11.1 %collective-permute-start.10 = (bf16[6,64,128]{2,1,0:T(8,128)(2,1)S(1)}, bf16[6,64,128]{2,1,0:T(8,128)(2,1)S(1)}, u32[]{:S(2)}, u32[]{:S(2)}) collective-permute-start(bf16[6,64,128]{2,1,0:T(8,128)(2,1)S(1)} %get-tuple-element.29), channel_id=1, source_target_pairs={{0,4},{1,5},{2,6},{3,7},{4,0},{5,1},{6,2},{7,3},{8,12},{9,13},{10,... | collective-permute-start | bytes 294920 | tf_op jit(solution)/shard_map/grams/ppermute | solution.py:30
  152.1 8.5 %collective-permute-start.11 = (bf16[6,64,128]{2,1,0:T(8,128)(2,1)S(1)}, bf16[6,64,128]{2,1,0:T(8,128)(2,1)S(1)}, u32[]{:S(2)}, u32[]{:S(2)}) collective-permute-start(bf16[6,64,128]{2,1,0:T(8,128)(2,1)S(1)} %get-tuple-element.30), channel_id=1, source_target_pairs={{0,5},{1,4},{2,7},{3,6},{4,1},{5,0},{6,3},{7,2},{8,13},{9,12},{10,... | collective-permute-start | bytes 294920 | tf_op jit(solution)/shard_map/grams/ppermute | solution.py:30
  152.5 21.5 %collective-permute-start.28 = (bf16[32,32,128]{2,1,0:T(8,128)(2,1)S(1)}, bf16[32,32,128]{2,1,0:T(8,128)(2,1)S(1)}, u32[]{:S(2)}, u32[]{:S(2)}) collective-permute-start(bf16[32,32,128]{2,1,0:T(8,128)(2,1)S(1)} %all-to-all-done.4.refs_0_), channel_id=1, source_target_pairs={{0,1},{1,0},{2,3},{3,2},{4,5},{5,4},{6,7},{7,6},{8,9},{9,8},{10,11... | collective-permute-start | bytes 786440 | tf_op jit(solution)/shard_map/precondition/ppermute | solution.py:30
  153.6 20.5 %collective-permute-start.34 = (bf16[32,32,128]{2,1,0:T(8,128)(2,1)S(1)}, bf16[32,32,128]{2,1,0:T(8,128)(2,1)S(1)}, u32[]{:S(2)}, u32[]{:S(2)}) collective-permute-start(bf16[32,32,128]{2,1,0:T(8,128)(2,1)S(1)} %collective-permute-done.33.refs_6_), channel_id=1, source_target_pairs={{0,1},{1,0},{2,3},{3,2},{4,5},{5,4},{6,7},{7,6},{8,9},{9,8},{10,11... | collective-permute-start | bytes 786440 | tf_op jit(solution)/shard_map/precondition/ppermute | solution.py:30
  160.1 14.0 %collective-permute-start.32 = (bf16[32,32,128]{2,1,0:T(8,128)(2,1)S(1)}, bf16[32,32,128]{2,1,0:T(8,128)(2,1)S(1)}, u32[]{:S(2)}, u32[]{:S(2)}) collective-permute-start(bf16[32,32,128]{2,1,0:T(8,128)(2,1)S(1)} %collective-permute-done.31.refs_4_), channel_id=1, source_target_pairs={{0,1},{1,0},{2,3},{3,2},{4,5},{5,4},{6,7},{7,6},{8,9},{9,8},{10,11... | collective-permute-start | bytes 786440 | tf_op jit(solution)/shard_map/precondition/ppermute | solution.py:30
  160.3 13.8 %collective-permute-start.30 = (bf16[32,32,128]{2,1,0:T(8,128)(2,1)}, bf16[32,32,128]{2,1,0:T(8,128)(2,1)S(1)}, u32[]{:S(2)}, u32[]{:S(2)}) collective-permute-start(bf16[32,32,128]{2,1,0:T(8,128)(2,1)} %collective-permute-done.29.refs_2_), channel_id=1, source_target_pairs={{0,1},{1,0},{2,3},{3,2},{4,5},{5,4},{6,7},{7,6},{8,9},{9,8},{10,11... | collective-permute-start | bytes 786440 | tf_op jit(solution)/shard_map/precondition/ppermute | solution.py:30
  160.6 4.2 %collective-permute-start.12 = (bf16[6,64,128]{2,1,0:T(8,128)(2,1)S(1)}, bf16[6,64,128]{2,1,0:T(8,128)(2,1)S(1)}, u32[]{:S(2)}, u32[]{:S(2)}) collective-permute-start(bf16[6,64,128]{2,1,0:T(8,128)(2,1)S(1)} %get-tuple-element.31), channel_id=1, source_target_pairs={{0,6},{1,7},{2,0},{3,1},{4,2},{5,3},{6,4},{7,5},{8,14},{9,15},{10,... | collective-permute-start | bytes 294920 | tf_op jit(solution)/shard_map/grams/ppermute | solution.py:30
  164.8 5.0 %collective-permute-start.13 = (bf16[6,64,128]{2,1,0:T(8,128)(2,1)S(1)}, bf16[6,64,128]{2,1,0:T(8,128)(2,1)S(1)}, u32[]{:S(2)}, u32[]{:S(2)}) collective-permute-start(bf16[6,64,128]{2,1,0:T(8,128)(2,1)S(1)} %get-tuple-element.32), channel_id=1, source_target_pairs={{0,7},{1,6},{2,1},{3,0},{4,3},{5,2},{6,5},{7,4},{8,15},{9,14},{10,... | collective-permute-start | bytes 294920 | tf_op jit(solution)/shard_map/grams/ppermute | solution.py:30
  169.8 1.1 copy-start.10
  171.0 1.1 copy-start.11
  (6 other events, 4.7 us)

commit v3 on v2

v3 whole, which is shorter than its diff:
```python
import jax
import jax.numpy as jnp
from jax import lax
from jax.experimental import pallas as pl
from jax.experimental.pallas import tpu as pltpu
from jax.sharding import PartitionSpec as P

decay_rate = 0.9
bf16 = jnp.bfloat16
f32 = jnp.float32

BS = 1024
NB = 32
CAP = 6
ROWS = 32
NW = 8
HALF = ROWS // 2
PART = 128
PARTNERS = [(k, o) for k in range(4) for o in range(2)]
ANY = pl.BlockSpec(memory_space=pl.ANY)
HBM = pl.BlockSpec(memory_space=pltpu.HBM)
VMEM = pl.BlockSpec(memory_space=pltpu.VMEM)
SMEM = pl.BlockSpec(memory_space=pltpu.SMEM)


def partner(worker, k, other):
    core = worker % 2
    core = 1 - core if other else core
    return (worker // 2 + k) % 4 * 2 + core


def send(value, k, other):
    return lax.ppermute(value, "worker", [(w, partner(w, k, other)) for w in range(NW)])


def exchange(pieces):
    return [p if j == 0 else send(p, *PARTNERS[j]) for j, p in enumerate(pieces)]


def gather(piece, own):
    out = [piece, send(own, 0, 1)]
    for p in [send(piece, k, 0) for k in range(1, 4)]:
        out += [p, send(p, 0, 1)]
    return out


def sources(worker):
    return [partner(worker, 4 - k, other) for k, other in PARTNERS]


def dests(worker):
    return [partner(worker, k, other) for k, other in PARTNERS]


def call(kernel, outs, args, in_specs=None, out_specs=None, scratch=(), flops=0, nbytes=2 << 20, vmem=16):
    return pl.pallas_call(
        kernel,
        out_shape=outs,
        in_specs=in_specs or [VMEM] * len(args),
        out_specs=out_specs or jax.tree.map(lambda _: VMEM, outs),
        scratch_shapes=scratch,
        compiler_params=pltpu.CompilerParams(vmem_limit_bytes=vmem << 20),
        cost_estimate=pl.CostEstimate(flops=flops, bytes_accessed=nbytes, transcendentals=0),
    )(*args)


def shape(dims, kind=bf16):
    return jax.ShapeDtypeStruct(dims, kind)


def pack_roots(owners, left_hbm, right_hbm, grads, *refs):
    outs, (columns, holder, left, right, taken, sems, cut) = refs[:NW], refs[NW:]
    shard, worker = lax.axis_index("shard"), lax.axis_index("worker")
    copies = [
        [
            pltpu.make_async_copy(far.at[c], near.at[c], sems.at[n, c])
            for n, (far, near) in enumerate(((left_hbm, left), (right_hbm, right)))
        ]
        for c in range(CAP)
    ]
    for pair in copies:
        for copy in pair:
            copy.start()
    mine = pl.ds(pl.multiple_of(worker * PART, PART), PART)
    copy_columns = pltpu.make_async_copy(grads.at[:, :, mine], columns, cut)
    copy_columns.start()
    for i in range(NW * CAP):
        holder[i] = -1
    for i in range(NW):
        taken[i] = 0

    def name(b, carry):
        who = owners[b]
        slot = taken[who]
        holder[who * CAP + slot] = b
        taken[who] = slot + 1
        return carry

    lax.fori_loop(0, NB, name, 0)
    row = lax.broadcasted_iota(jnp.int32, (ROWS, PART), 0)
    lane = lax.broadcasted_iota(jnp.int32, (ROWS, PART), 1)
    near = shard // 4
    on_diag = lane == row + shard % 4 * ROWS
    diag_rows = []
    for c in range(CAP):
        for copy in copies[c]:
            copy.wait()
        total = jnp.zeros((1, PART), f32)
        for n, ref in enumerate((left, right)):
            block = ref[c, :, pl.ds(pl.multiple_of(near * PART, PART), PART)]
            d = jnp.sum(jnp.where(on_diag, block, 0.0), axis=0, keepdims=True)
            high = d.astype(bf16).astype(f32)
            for m, v in enumerate((high, d - high)):
                to = (2 * n + m) * ROWS
                total = total + pltpu.roll(v, (to + PART - shard % 4 * ROWS) % PART, 1)
            for out, to in zip(outs, dests(worker)):
                block = ref[c, :, pl.ds(pl.multiple_of(to * PART, PART), PART)]
                block = jnp.where(on_diag & (to == near), 0.0, block)
                out[(2 * c + n) * ROWS : (2 * c + n + 1) * ROWS, :] = block.astype(bf16)
        diag_rows.append(total)
    diag_tile = jnp.concatenate(diag_rows + [jnp.zeros((16 - CAP, PART), f32)], axis=0).astype(bf16)
    for out in outs:
        out[2 * CAP * ROWS :, :] = diag_tile
    copy_columns.wait()


def pick_roots(holder, *refs):
    pieces, out = refs[:NW], refs[NW]
    worker = lax.axis_index("worker")
    for piece, source in zip(pieces, sources(worker)):
        diag_tile = piece[2 * CAP * ROWS :, :].astype(f32)
        for c in range(CAP):
            block = holder[source * CAP + c]

            @pl.when(block >= 0)
            def _():
                out[block, : 2 * ROWS, :] = piece[2 * c * ROWS : 2 * (c + 1) * ROWS, :]
                out[block, 2 * ROWS :, :] = jnp.broadcast_to(
                    diag_tile[c : c + 1], (HALF, PART)
                ).astype(bf16)


def make_grams(roots, columns, out, image):
    worker = lax.axis_index("worker")
    mine = pl.ds(pl.multiple_of(worker * PART, PART), PART)
    own = columns[worker]
    lane = lax.broadcasted_iota(jnp.int32, (1, PART), 1)
    diag = jnp.zeros((1, PART), f32)
    for q in range(4):
        d = roots[worker * 4 + q, 2 * ROWS :, :].astype(f32)[:1]
        both = pltpu.roll(d, 64, 1) + pltpu.roll(d, 32, 1)
        diag = diag + pltpu.roll(jnp.where(lane < ROWS, both, 0.0), q * ROWS, 1)
    product = own.astype(f32) * diag
    gram = jnp.zeros((BS, PART), f32)
    for w in range(NW):
        gram = gram + lax.dot_general(
            columns[w], columns[w, mine, :], (((1,), (1,)), ((), ())), preferred_element_type=f32
        )
        block = roots[w * 4 : (w + 1) * 4, ROWS : 2 * ROWS, :].reshape(PART, PART)
        product = product + jnp.dot(columns[w], block, preferred_element_type=f32)
        block = lax.dot_general(
            columns[w], own, (((0,), (0,)), ((), ())), preferred_element_type=f32
        )
        out[w * 4 : (w + 1) * 4, ROWS:, :] = block.astype(bf16).reshape(4, ROWS, PART)
    out[:, :ROWS, :] = gram.astype(bf16).reshape(NB, ROWS, PART)
    image[...] = product.astype(bf16)


def make_result(after, roots, image, left, out):
    diag_rows = roots[:, 2 * ROWS :, :].astype(f32)[:, :1, :]
    row = lax.broadcasted_iota(jnp.int32, (NB, ROWS, PART), 1)
    lane = lax.broadcasted_iota(jnp.int32, (NB, ROWS, PART), 2)
    spread = jnp.where((lane == row) | (lane == row + ROWS), diag_rows, 0.0)
    spread = spread.astype(bf16).reshape(BS, PART)
    diag = jnp.dot(spread, jnp.ones((PART, PART), bf16), preferred_element_type=f32)
    total = image[...].astype(f32) * diag
    for w in range(NW):
        total = total + jnp.dot(
            left[w].reshape(BS, PART),
            image[w * PART : (w + 1) * PART, :],
            preferred_element_type=f32,
        )
    out[...] = total.astype(bf16).reshape(NB, ROWS, PART)


def pack_grams(holder, grams, *outs):
    worker = lax.axis_index("worker")
    for out, to in zip(outs, dests(worker)):
        for c in range(CAP):
            out[c] = grams[jnp.maximum(holder[to * CAP + c], 0)]


def update(holder, left, right, *refs):
    pieces, outs, held, sems, out_sems = refs[:NW], refs[NW : NW + 2], *refs[NW + 2 :]
    worker = lax.axis_index("worker")
    into = [
        [pltpu.make_async_copy(far.at[c], held.at[n, c], sems.at[n, c]) for c in range(CAP)]
        for n, far in enumerate((left, right))
    ]
    back = [
        [pltpu.make_async_copy(held.at[n, c], far.at[c], out_sems.at[n, c]) for c in range(CAP)]
        for n, far in enumerate(outs)
    ]
    for copies in into:
        for copy in copies:
            copy.start()
    for n in range(2):
        for c in range(CAP):
            into[n][c].wait()

            @pl.when(holder[worker * CAP + c] >= 0)
            def _():
                for piece, source in zip(pieces, sources(worker)):
                    cols = pl.ds(pl.multiple_of(source * PART, PART), PART)
                    gram = piece[c, n * ROWS : (n + 1) * ROWS, :].astype(f32)
                    held[n, c, :, cols] = (
                        decay_rate * held[n, c, :, cols] + (1.0 - decay_rate) * gram
                    )

            back[n][c].start()
    for copies in back:
        for copy in copies:
            copy.wait()


def assemble(*refs):
    pieces, out, sems = refs[:NW], refs[NW], refs[NW + 1]
    copies = []
    for j, source in enumerate(sources(lax.axis_index("worker"))):
        cols = pl.ds(pl.multiple_of(source * PART, PART), PART)
        copies.append(pltpu.make_async_copy(pieces[j], out.at[:, :, cols], sems.at[j]))
    for copy in copies:
        copy.start()
    for copy in copies:
        copy.wait()


def over_shard(value):
    return lax.all_to_all(value, "shard", 0, 0, tiled=True)


def over_worker(value):
    return lax.all_gather(value, "worker", axis=0, tiled=False)


def body(grads, owners, left, right, left_root, right_root):
    tile = shape((NB, ROWS, PART))
    with jax.named_scope("roots"):
        *packed, mine, holder = call(
            pack_roots,
            [shape((2 * CAP * ROWS + HALF, PART))] * NW + [tile, shape((NW * CAP,), jnp.int32)],
            (owners[:, 0], left_root[0], right_root[0], grads),
            [SMEM, HBM, HBM, HBM],
            [VMEM] * (NW + 1) + [SMEM],
            [
                pltpu.VMEM((CAP, ROWS, BS), f32),
                pltpu.VMEM((CAP, ROWS, BS), f32),
                pltpu.SMEM((NW,), jnp.int32),
                pltpu.SemaphoreType.DMA((2, CAP)),
                pltpu.SemaphoreType.DMA,
            ],
            vmem=61,
        )
        mine, packed = lax.optimization_barrier((over_shard(mine), exchange(packed)))
    with jax.named_scope("gradients"):
        columns = over_worker(mine.reshape(BS, PART))
    with jax.named_scope("roots"):
        roots = call(
            pick_roots,
            shape((NB, 2 * ROWS + HALF, PART)),
            (holder, *packed),
            [SMEM] + [VMEM] * NW,
        )
        roots = over_shard(roots)
        root_l = over_worker(roots[:, :ROWS])
    with jax.named_scope("grams"):
        grams, image = call(
            make_grams,
            [shape((NB, 2 * ROWS, PART)), shape((BS, PART))],
            (roots, columns),
            flops=6 * BS * BS * PART,
        )
        grams = over_shard(grams)
        packed = call(
            pack_grams,
            [shape((CAP, 2 * ROWS, PART))] * NW,
            (holder, grams),
            [SMEM, VMEM],
        )
    with jax.named_scope("precondition"):
        result = call(
            make_result,
            tile,
            (packed[0], roots, image, root_l),
            [ANY] + [VMEM] * 3,
            flops=2 * BS * BS * PART,
        )
        result, packed = lax.optimization_barrier((over_shard(result), exchange(packed)))
    with jax.named_scope("factors"):
        factor = shape((CAP, ROWS, BS), f32)
        new_left, new_right = call(
            update,
            [factor, factor],
            (holder, left[0], right[0], *packed),
            [SMEM, HBM, HBM] + [VMEM] * NW,
            [HBM, HBM],
            [
                pltpu.VMEM((2, CAP, ROWS, BS), f32),
                pltpu.SemaphoreType.DMA((2, CAP)),
                pltpu.SemaphoreType.DMA((2, CAP)),
            ],
            nbytes=20 << 20,
            vmem=48,
        )
        own, new_left = lax.optimization_barrier((result, new_left))
    with jax.named_scope("precondition"):
        precond = call(
            assemble,
            shape((NB, ROWS, BS)),
            tuple(gather(result, own)),
            [VMEM] * NW,
            HBM,
            [pltpu.SemaphoreType.DMA((NW,))],
            nbytes=4 << 20,
        )
    return new_left[None], new_right[None], precond


def solution(mesh):
    factor = P("worker", None, "shard", None)
    return jax.shard_map(
        body,
        mesh=mesh,
        in_specs=(P(None, "shard", None), P(), factor, factor, factor, factor),
        out_specs=(factor, factor, P(None, "shard", None)),
        check_vma=False,
    )
```

time: 178 us -> 153 us (0.86)
  blocking collectives: 19 us -> 49.2 us
  starting transfers between devices: 79.6 us -> 50.7 us
  waiting for transfers between devices: 44 us -> 18.7 us
  between operations: 0.81 us -> 14.2 us
  local copies, waits for them, and re-layouts: 15.3 us -> 6.16 us
  Pallas kernels: 18.2 us -> 13.8 us
    all_to_all x1 -> x2, blocking collectives: 19 us -> 49.2 us  [over_shard(): return lax.all_to_all(value, 'shard', 0, 0, tiled=True)]
    ppermute x35 -> x21, starting transfers between devices: 45.5 us -> 29 us  [send(): lax.ppermute(value, 'worker', [(w, partner(w, k, other)) for w in range(N...]
    all_to_all x4 -> x2, waiting for transfers between devices: 16.2 us -> 0.01 us  [over_shard(): return lax.all_to_all(value, 'shard', 0, 0, tiled=True)]
    all_to_all x4 -> x2, starting transfers between devices: 34.1 us -> 21.6 us  [over_shard(): return lax.all_to_all(value, 'shard', 0, 0, tiled=True)]
    ppermute x35 -> x21, waiting for transfers between devices: 27.8 us -> 15.7 us  [send(): lax.ppermute(value, 'worker', [(w, partner(w, k, other)) for w in range(N...]
    unnamed x30 -> x16, local copies, waits for them, and re-layouts: 14.6 us -> 5.44 us
    pallas_call x8 -> x7, Pallas kernels: 18.2 us -> 13.8 us  [call(): pl.pallas_call(kernel, out_shape=outs, in_specs=in_specs or [VMEM] * len(...]
    all_gather x0 -> x2, waiting for transfers between devices: none -> 2.95 us  [over_worker(): return lax.all_gather(value, 'worker', axis=0, tiled=False)]
  transfers between devices with their start and end apart: 39 -> 25, of which waited for: 12 -> 9; matrix products, arithmetic and copies ran while one was open for 0% -> 0% of each run, Pallas kernels for 7% -> 5%
where the time goes in v3:
time: 153 us
  starting transfers between devices  50.7 us (33%)
  blocking collectives  49.2 us (32%)
  waiting for transfers between devices  18.7 us (12%)
  between operations  14.2 us (9%)
  Pallas kernels  13.8 us (9%)
  local copies, waits for them, and re-layouts  6.16 us (4%)
    all_to_all x2, blocking collectives, over_shard(): return lax.all_to_all(value, 'shard', 0, 0, tiled=True)  49.2 us
    ppermute x21, starting transfers between devices, send(): lax.ppermute(value, 'worker', [(w, partner(w, k, other)) for w in range(N...  29 us
    all_to_all x2, starting transfers between devices, over_shard(): return lax.all_to_all(value, 'shard', 0, 0, tiled=True)  21.6 us
    ppermute x21, waiting for transfers between devices, send(): lax.ppermute(value, 'worker', [(w, partner(w, k, other)) for w in range(N...  15.7 us
    pallas_call x7, Pallas kernels, call(): pl.pallas_call(kernel, out_shape=outs, in_specs=in_specs or [VMEM] * len(...  13.8 us
    unnamed x16, local copies, waits for them, and re-layouts  5.44 us
  transfers between devices with their start and end apart: 25, of which 9 were waited for; matrix products, arithmetic and copies ran while one was open for 0% of the time, Pallas kernels for 5%

profile of v3, /device:TPU:1, one launch (start us, length us, event | category | flops | bytes accessed | tf_op | source)
XLA Modules:
  0.0 152.8 jit_solution(9450168517336356307)
XLA Ops:
  7.2 3.5 %roots.2 = (bf16[400,128]{1,0:T(8,128)(2,1)}, bf16[400,128]{1,0:T(8,128)(2,1)}, bf16[400,128]{1,0:T(8,128)(2,1)}, bf16[400,128]{1,0:T(8,128)(2,1)}, bf16[400,128...) custom-call(s32[32]{0:T(128)} %bitcast.15, ...), custom_call_target="tpu_custom_call" | custom-call | bytes 2097152 | tf_op jit(solution)/shard_map/roots/pallas_call | solution.py:56
  10.7 12.0 %all-to-all-start = ((bf16[32,32,128]{2,1,0:T(8,128)(2,1)}), bf16[32,32,128]{2,1,0:T(8,128)(2,1)S(1)}, u32[]{:S(2)}, u32[]{:S(2)}) async-start(bf16[32,32,128]{2,1,0:T(8,128)(2,1)} %get-tuple-element.46), calls=%async_computation | async-start | bytes 524288 | tf_op jit(solution)/shard_map/roots/all_to_all | solution.py:239
  22.7 0.0 all-gather.4.cloned.1.call-start
  22.8 1.0 collective-permute-start
  23.8 1.2 collective-permute-start.1
  25.0 1.5 collective-permute-start.2
  26.5 1.4 collective-permute-start.3
  27.9 1.9 %collective-permute-start.4 = (bf16[400,128]{1,0:T(8,128)(2,1)}, bf16[400,128]{1,0:T(8,128)(2,1)S(1)}, u32[]{:S(2)}, u32[]{:S(2)}) collective-permute-start(bf16[400,128]{1,0:T(8,128)(2,1)} %get-tuple-element.52), channel_id=1, source_target_pairs={{0,5},{1,4},{2,7},{3,6},{4,1},{5,0},{6,3},{7,2},{8,13},{9,12},{10,... | collective-permute-start | bytes 307208 | tf_op jit(solution)/shard_map/roots/ppermute | solution.py:33
  29.8 1.5 collective-permute-start.5
  31.3 0.9 collective-permute-start.6
  32.2 0.2 collective-permute-done.2.refs_3_
  32.3 2.7 %collective-permute-done.3.refs_4_ = bf16[400,128]{1,0:T(8,128)(2,1)S(1)} collective-permute-done((bf16[400,128]{1,0:T(8,128)(2,1)}, bf16[400,128]{1,0:T(8,128)(2,1)S(1)}, u32[]{:S(2)}, u32[]{:S(2)}) %collective-permute-start.3) | collective-permute-done | bytes 102432 | tf_op jit(solution)/shard_map/roots/ppermute | solution.py:33
  35.0 2.4 %collective-permute-done.4.refs_5_ = bf16[400,128]{1,0:T(8,128)(2,1)S(1)} collective-permute-done((bf16[400,128]{1,0:T(8,128)(2,1)}, bf16[400,128]{1,0:T(8,128)(2,1)S(1)}, u32[]{:S(2)}, u32[]{:S(2)}) %collective-permute-start.4) | collective-permute-done | bytes 102432 | tf_op jit(solution)/shard_map/roots/ppermute | solution.py:33
  37.4 1.1 collective-permute-done.6.refs_7_
  38.5 0.7 copy-done.7
  39.2 0.0 all-gather.4.cloned.1.call-update
  39.3 0.0 all-gather.6.cloned.1.call-start
  39.3 0.9 copy-done.3
  40.2 0.7 copy-done.4
  40.9 1.0 roots.3
  41.9 26.3 %all_to_all.20.roots = bf16[32,80,128]{2,1,0:T(8,128)(2,1)S(1)} all-to-all(bf16[32,80,128]{2,1,0:T(8,128)(2,1)S(1)} %roots.3), channel_id=1, replica_groups=mesh['shard'=32,'worker'=8] {'shard'}, dimensions={0} | all-to-all | bytes 1310720 | tf_op jit(solution)/shard_map/roots/all_to_all | solution.py:239
  68.1 0.7 slice.4
  68.9 0.0 all-gather.4.cloned.1.call-done.columns
  68.9 1.6 %copy-done.6 = bf16[8,1024,128]{2,1,0:T(8,128)(2,1)S(1)} copy-done((bf16[8,1024,128]{2,1,0:T(8,128)(2,1)S(1)}, bf16[8,1024,128]{2,1,0:T(8,128)(2,1)}, u32[]{:S(2)}) %copy-start.6) | copy-done | bytes 2097176
  70.5 1.8 %grams.2 = (bf16[32,64,128]{2,1,0:T(8,128)(2,1)S(1)}, bf16[1024,128]{1,0:T(8,128)(2,1)S(1)}) custom-call(bf16[32,80,128]{2,1,0:T(8,128)(2,1)S(1)} %all_to_all.20.roots, bf16[8,1024,128]{2,1,0:T(8,128)(2,1)S(1)} %copy-done.6), custom_call_target="tpu_custom_call" | custom-call | flops 805306368 | bytes 2097152 | tf_op jit(solution)/shard_map/grams/pallas_call | solution.py:56
  72.3 22.9 %all_to_all.21.grams = bf16[32,64,128]{2,1,0:T(8,128)(2,1)S(1)} all-to-all(bf16[32,64,128]{2,1,0:T(8,128)(2,1)S(1)} %get-tuple-element.64), channel_id=1, replica_groups=mesh['shard'=32,'worker'=8] {'shard'}, dimensions={0} | all-to-all | bytes 1048576 | tf_op jit(solution)/shard_map/grams/all_to_all | solution.py:239
  95.2 0.7 grams.3
  95.9 2.9 %all-gather.6.cloned.1.call-done = bf16[256,32,128]{2,1,0:T(8,128)(2,1)} async-done(((bf16[32,32,128]{2,1,0:T(8,128)(2,1)}), bf16[256,32,128]{2,1,0:T(8,128)(2,1)}) %all-gather.6.cloned.1.call-update) | async-done | bytes 2097168 | tf_op jit(solution)/shard_map/roots/all_gather | solution.py:243
  98.8 1.6 %copy-done = bf16[256,32,128]{2,1,0:T(8,128)(2,1)S(1)} copy-done((bf16[256,32,128]{2,1,0:T(8,128)(2,1)S(1)}, bf16[256,32,128]{2,1,0:T(8,128)(2,1)}, u32[]{:S(2)}) %copy-start) | copy-done | bytes 2097176
  100.4 1.5 precondition.2
  101.9 9.6 %all-to-all-start.3 = ((bf16[32,32,128]{2,1,0:T(8,128)(2,1)}), bf16[32,32,128]{2,1,0:T(8,128)(2,1)S(1)}, u32[]{:S(2)}, u32[]{:S(2)}) async-start(bf16[32,32,128]{2,1,0:T(8,128)(2,1)} %precondition.2), calls=%async_computation.3 | async-start | bytes 524288 | tf_op jit(solution)/shard_map/precondition/all_to_all | solution.py:239
  111.5 0.6 collective-permute-start.7
  112.1 1.7 %collective-permute-start.9 = (bf16[6,64,128]{2,1,0:T(8,128)(2,1)S(1)}, bf16[6,64,128]{2,1,0:T(8,128)(2,1)S(1)}, u32[]{:S(2)}, u32[]{:S(2)}) collective-permute-start(bf16[6,64,128]{2,1,0:T(8,128)(2,1)S(1)} %get-tuple-element.69), channel_id=1, source_target_pairs={{0,3},{1,2},{2,5},{3,4},{4,7},{5,6},{6,1},{7,0},{8,11},{9,10},{10,... | collective-permute-start | bytes 294920 | tf_op jit(solution)/shard_map/precondition/ppermute | solution.py:33
  113.8 2.4 %collective-permute-start.10 = (bf16[6,64,128]{2,1,0:T(8,128)(2,1)S(1)}, bf16[6,64,128]{2,1,0:T(8,128)(2,1)S(1)}, u32[]{:S(2)}, u32[]{:S(2)}) collective-permute-start(bf16[6,64,128]{2,1,0:T(8,128)(2,1)S(1)} %get-tuple-element.70), channel_id=1, source_target_pairs={{0,4},{1,5},{2,6},{3,7},{4,0},{5,1},{6,2},{7,3},{8,12},{9,13},{10,... | collective-permute-start | bytes 294920 | tf_op jit(solution)/shard_map/precondition/ppermute | solution.py:33
  116.2 0.9 collective-permute-start.11
  117.1 1.3 collective-permute-start.12
  118.3 1.7 %collective-permute-start.13 = (bf16[6,64,128]{2,1,0:T(8,128)(2,1)S(1)}, bf16[6,64,128]{2,1,0:T(8,128)(2,1)S(1)}, u32[]{:S(2)}, u32[]{:S(2)}) collective-permute-start(bf16[6,64,128]{2,1,0:T(8,128)(2,1)S(1)} %get-tuple-element.73), channel_id=1, source_target_pairs={{0,7},{1,6},{2,1},{3,0},{4,3},{5,2},{6,5},{7,4},{8,15},{9,14},{10,... | collective-permute-start | bytes 294920 | tf_op jit(solution)/shard_map/precondition/ppermute | solution.py:33
  120.0 4.3 %collective-permute-done.9.refs_3_ = bf16[6,64,128]{2,1,0:T(8,128)(2,1)S(1)} collective-permute-done((bf16[6,64,128]{2,1,0:T(8,128)(2,1)S(1)}, bf16[6,64,128]{2,1,0:T(8,128)(2,1)S(1)}, u32[]{:S(2)}, u32[]{:S(2)}) %collective-permute-start.9) | collective-permute-done | bytes 98336 | tf_op jit(solution)/shard_map/precondition/ppermute | solution.py:33
  124.4 0.7 collective-permute-done.13.refs_7_
  125.1 2.5 %collective-permute-start.19 = (bf16[32,32,128]{2,1,0:T(8,128)(2,1)S(1)}, bf16[32,32,128]{2,1,0:T(8,128)(2,1)S(1)}, u32[]{:S(2)}, u32[]{:S(2)}) collective-permute-start(bf16[32,32,128]{2,1,0:T(8,128)(2,1)S(1)} %all-to-all-done.3.refs_0_), channel_id=1, source_target_pairs={{0,6},{1,7},{2,0},{3,1},{4,2},{5,3},{6,4},{7,5},{8,14},{9,15},{10,... | collective-permute-start | bytes 786440 | tf_op jit(solution)/shard_map/precondition/ppermute | solution.py:33
  127.6 1.1 collective-permute-start.17
  128.7 4.1 %factors.1 = (f32[6,32,1024]{2,1,0:T(8,128)}, f32[6,32,1024]{2,1,0:T(8,128)}) custom-call(s32[48]{0:T(128)S(1)} %copy-done.5, f32[6,32,1024]{2,1,0:T(8,128)S(1)} %bitcast.10, f32[6,32,1024]{2,1,0:T(8,128)S(1)} %bitcast.11, bf16[6,64,128]{2,1,0:T(8,128)(2,1)S(1)} %get-tuple-element.75.after.refs_0_, bf16[6,64,128]{2,1,0:T(8,128)(2,1)S(1)} %collective-permute-done.7.refs_1_, ...), custom_call_target="tpu_custom_call" | custom-call | bytes 20971520 | tf_op jit(solution)/shard_map/factors/pallas_call | solution.py:56
  132.8 1.2 collective-permute-start.14
  134.1 5.7 %collective-permute-start.20 = (bf16[32,32,128]{2,1,0:T(8,128)(2,1)S(1)}, bf16[32,32,128]{2,1,0:T(8,128)(2,1)S(1)}, u32[]{:S(2)}, u32[]{:S(2)}) collective-permute-start(bf16[32,32,128]{2,1,0:T(8,128)(2,1)S(1)} %collective-permute-done.19.refs_6_), channel_id=1, source_target_pairs={{0,1},{1,0},{2,3},{3,2},{4,5},{5,4},{6,7},{7,6},{8,9},{9,8},{10,11... | collective-permute-start | bytes 786440 | tf_op jit(solution)/shard_map/precondition/ppermute | solution.py:33
  139.8 3.2 %collective-permute-done.15.refs_2_ = bf16[32,32,128]{2,1,0:T(8,128)(2,1)S(1)} collective-permute-done((bf16[32,32,128]{2,1,0:T(8,128)(2,1)S(1)}, bf16[32,32,128]{2,1,0:T(8,128)(2,1)S(1)}, u32[]{:S(2)}, u32[]{:S(2)}) %collective-permute-start.15) | collective-permute-done | bytes 262176 | tf_op jit(solution)/shard_map/precondition/ppermute | solution.py:33
  143.0 0.5 collective-permute-start.16
  143.5 1.1 collective-permute-done.16.refs_3_
  144.6 1.4 precondition.3
  (30 shorter events, 0.1 us)
Async XLA Ops:
  10.7 27.9 %all-to-all-start = ((bf16[32,32,128]{2,1,0:T(8,128)(2,1)}), bf16[32,32,128]{2,1,0:T(8,128)(2,1)S(1)}, u32[]{:S(2)}, u32[]{:S(2)}) async-start(bf16[32,32,128]{2,1,0:T(8,128)(2,1)} %get-tuple-element.46), calls=%async_computation | async-start | bytes 524288 | tf_op jit(solution)/shard_map/roots/all_to_all | solution.py:239
  22.7 46.2 %all-gather.4.cloned.1.call-start = ((), (), s32[]{:S(2)}) async-start(), calls=%async_computation.4 | async-start | bytes 2359296 | tf_op jit(solution)/shard_map/gradients/all_gather | solution.py:243
  22.8 7.0 %collective-permute-start = (bf16[400,128]{1,0:T(8,128)(2,1)}, bf16[400,128]{1,0:T(8,128)(2,1)S(1)}, u32[]{:S(2)}, u32[]{:S(2)}) collective-permute-start(bf16[400,128]{1,0:T(8,128)(2,1)} %get-tuple-element.48), channel_id=1, source_target_pairs={{0,1},{1,0},{2,3},{3,2},{4,5},{5,4},{6,7},{7,6},{8,9},{9,8},{10,11... | collective-permute-start | bytes 307208 | tf_op jit(solution)/shard_map/roots/ppermute | solution.py:33
  23.8 7.5 %collective-permute-start.1 = (bf16[400,128]{1,0:T(8,128)(2,1)}, bf16[400,128]{1,0:T(8,128)(2,1)S(1)}, u32[]{:S(2)}, u32[]{:S(2)}) collective-permute-start(bf16[400,128]{1,0:T(8,128)(2,1)} %get-tuple-element.49), channel_id=1, source_target_pairs={{0,2},{1,3},{2,4},{3,5},{4,6},{5,7},{6,0},{7,1},{8,10},{9,11},{10,... | collective-permute-start | bytes 307208 | tf_op jit(solution)/shard_map/roots/ppermute | solution.py:33
  25.0 7.3 %collective-permute-start.2 = (bf16[400,128]{1,0:T(8,128)(2,1)}, bf16[400,128]{1,0:T(8,128)(2,1)S(1)}, u32[]{:S(2)}, u32[]{:S(2)}) collective-permute-start(bf16[400,128]{1,0:T(8,128)(2,1)} %get-tuple-element.50), channel_id=1, source_target_pairs={{0,3},{1,2},{2,5},{3,4},{4,7},{5,6},{6,1},{7,0},{8,11},{9,10},{10,... | collective-permute-start | bytes 307208 | tf_op jit(solution)/shard_map/roots/ppermute | solution.py:33
  26.5 8.6 %collective-permute-start.3 = (bf16[400,128]{1,0:T(8,128)(2,1)}, bf16[400,128]{1,0:T(8,128)(2,1)S(1)}, u32[]{:S(2)}, u32[]{:S(2)}) collective-permute-start(bf16[400,128]{1,0:T(8,128)(2,1)} %get-tuple-element.51), channel_id=1, source_target_pairs={{0,4},{1,5},{2,6},{3,7},{4,0},{5,1},{6,2},{7,3},{8,12},{9,13},{10,... | collective-permute-start | bytes 307208 | tf_op jit(solution)/shard_map/roots/ppermute | solution.py:33
  27.9 9.5 %collective-permute-start.4 = (bf16[400,128]{1,0:T(8,128)(2,1)}, bf16[400,128]{1,0:T(8,128)(2,1)S(1)}, u32[]{:S(2)}, u32[]{:S(2)}) collective-permute-start(bf16[400,128]{1,0:T(8,128)(2,1)} %get-tuple-element.52), channel_id=1, source_target_pairs={{0,5},{1,4},{2,7},{3,6},{4,1},{5,0},{6,3},{7,2},{8,13},{9,12},{10,... | collective-permute-start | bytes 307208 | tf_op jit(solution)/shard_map/roots/ppermute | solution.py:33
  29.8 7.6 %collective-permute-start.5 = (bf16[400,128]{1,0:T(8,128)(2,1)}, bf16[400,128]{1,0:T(8,128)(2,1)S(1)}, u32[]{:S(2)}, u32[]{:S(2)}) collective-permute-start(bf16[400,128]{1,0:T(8,128)(2,1)} %get-tuple-element.53), channel_id=1, source_target_pairs={{0,6},{1,7},{2,0},{3,1},{4,2},{5,3},{6,4},{7,5},{8,14},{9,15},{10,... | collective-permute-start | bytes 307208 | tf_op jit(solution)/shard_map/roots/ppermute | solution.py:33
  31.3 7.3 %collective-permute-start.6 = (bf16[400,128]{1,0:T(8,128)(2,1)}, bf16[400,128]{1,0:T(8,128)(2,1)S(1)}, u32[]{:S(2)}, u32[]{:S(2)}) collective-permute-start(bf16[400,128]{1,0:T(8,128)(2,1)} %get-tuple-element.54), channel_id=1, source_target_pairs={{0,7},{1,6},{2,1},{3,0},{4,3},{5,2},{6,5},{7,4},{8,15},{9,14},{10,... | collective-permute-start | bytes 307208 | tf_op jit(solution)/shard_map/roots/ppermute | solution.py:33
  38.5 0.7 copy-start.7
  39.3 59.6 %all-gather.6.cloned.1.call-start = ((), (), s32[]{:S(2)}) async-start(), calls=%async_computation.5 | async-start | bytes 2359296 | tf_op jit(solution)/shard_map/roots/all_gather | solution.py:243
  39.3 0.9 copy-start.3
  40.2 0.7 copy-start.4
  68.9 26.4 %copy-start.5 = (s32[48]{0:T(128)S(1)}, s32[48]{0:T(128)}, u32[]{:S(2)}) copy-start(s32[48]{0:T(128)} %get-tuple-element.45.holder) | copy-start | bytes 580
  68.9 1.6 %copy-start.6 = (bf16[8,1024,128]{2,1,0:T(8,128)(2,1)S(1)}, bf16[8,1024,128]{2,1,0:T(8,128)(2,1)}, u32[]{:S(2)}) copy-start(bf16[8,1024,128]{2,1,0:T(8,128)(2,1)} %all-gather.4.cloned.1.call-done.columns) | copy-start | bytes 6291460
  72.3 56.4 %copy-start.1 = (f32[1,6,32,1024]{3,2,1,0:T(8,128)S(1)}, f32[1,6,32,1024]{3,2,1,0:T(8,128)}, u32[]{:S(2)}) copy-start(f32[1,6,32,1024]{3,2,1,0:T(8,128)} %param.8) | copy-start | bytes 2359300
  72.3 56.4 %copy-start.2 = (f32[1,6,32,1024]{3,2,1,0:T(8,128)S(1)}, f32[1,6,32,1024]{3,2,1,0:T(8,128)}, u32[]{:S(2)}) copy-start(f32[1,6,32,1024]{3,2,1,0:T(8,128)} %param.9) | copy-start | bytes 2359300
  98.8 1.6 %copy-start = (bf16[256,32,128]{2,1,0:T(8,128)(2,1)S(1)}, bf16[256,32,128]{2,1,0:T(8,128)(2,1)}, u32[]{:S(2)}) copy-start(bf16[256,32,128]{2,1,0:T(8,128)(2,1)} %all-gather.6.cloned.1.call-done) | copy-start | bytes 6291460
  101.9 23.2 %all-to-all-start.3 = ((bf16[32,32,128]{2,1,0:T(8,128)(2,1)}), bf16[32,32,128]{2,1,0:T(8,128)(2,1)S(1)}, u32[]{:S(2)}, u32[]{:S(2)}) async-start(bf16[32,32,128]{2,1,0:T(8,128)(2,1)} %precondition.2), calls=%async_computation.3 | async-start | bytes 524288 | tf_op jit(solution)/shard_map/precondition/all_to_all | solution.py:239
  111.5 5.6 %collective-permute-start.7 = (bf16[6,64,128]{2,1,0:T(8,128)(2,1)S(1)}, bf16[6,64,128]{2,1,0:T(8,128)(2,1)S(1)}, u32[]{:S(2)}, u32[]{:S(2)}) collective-permute-start(bf16[6,64,128]{2,1,0:T(8,128)(2,1)S(1)} %get-tuple-element.67), channel_id=1, source_target_pairs={{0,1},{1,0},{2,3},{3,2},{4,5},{5,4},{6,7},{7,6},{8,9},{9,8},{10,11... | collective-permute-start | bytes 294920 | tf_op jit(solution)/shard_map/precondition/ppermute | solution.py:33
  112.1 6.2 %collective-permute-start.8 = (bf16[6,64,128]{2,1,0:T(8,128)(2,1)S(1)}, bf16[6,64,128]{2,1,0:T(8,128)(2,1)S(1)}, u32[]{:S(2)}, u32[]{:S(2)}) collective-permute-start(bf16[6,64,128]{2,1,0:T(8,128)(2,1)S(1)} %get-tuple-element.68), channel_id=1, source_target_pairs={{0,2},{1,3},{2,4},{3,5},{4,6},{5,7},{6,0},{7,1},{8,10},{9,11},{10,... | collective-permute-start | bytes 294920 | tf_op jit(solution)/shard_map/precondition/ppermute | solution.py:33
  112.1 12.3 %collective-permute-start.9 = (bf16[6,64,128]{2,1,0:T(8,128)(2,1)S(1)}, bf16[6,64,128]{2,1,0:T(8,128)(2,1)S(1)}, u32[]{:S(2)}, u32[]{:S(2)}) collective-permute-start(bf16[6,64,128]{2,1,0:T(8,128)(2,1)S(1)} %get-tuple-element.69), channel_id=1, source_target_pairs={{0,3},{1,2},{2,5},{3,4},{4,7},{5,6},{6,1},{7,0},{8,11},{9,10},{10,... | collective-permute-start | bytes 294920 | tf_op jit(solution)/shard_map/precondition/ppermute | solution.py:33
  113.8 10.6 %collective-permute-start.10 = (bf16[6,64,128]{2,1,0:T(8,128)(2,1)S(1)}, bf16[6,64,128]{2,1,0:T(8,128)(2,1)S(1)}, u32[]{:S(2)}, u32[]{:S(2)}) collective-permute-start(bf16[6,64,128]{2,1,0:T(8,128)(2,1)S(1)} %get-tuple-element.70), channel_id=1, source_target_pairs={{0,4},{1,5},{2,6},{3,7},{4,0},{5,1},{6,2},{7,3},{8,12},{9,13},{10,... | collective-permute-start | bytes 294920 | tf_op jit(solution)/shard_map/precondition/ppermute | solution.py:33
  116.2 8.2 %collective-permute-start.11 = (bf16[6,64,128]{2,1,0:T(8,128)(2,1)S(1)}, bf16[6,64,128]{2,1,0:T(8,128)(2,1)S(1)}, u32[]{:S(2)}, u32[]{:S(2)}) collective-permute-start(bf16[6,64,128]{2,1,0:T(8,128)(2,1)S(1)} %get-tuple-element.71), channel_id=1, source_target_pairs={{0,5},{1,4},{2,7},{3,6},{4,1},{5,0},{6,3},{7,2},{8,13},{9,12},{10,... | collective-permute-start | bytes 294920 | tf_op jit(solution)/shard_map/precondition/ppermute | solution.py:33
  117.1 7.3 %collective-permute-start.12 = (bf16[6,64,128]{2,1,0:T(8,128)(2,1)S(1)}, bf16[6,64,128]{2,1,0:T(8,128)(2,1)S(1)}, u32[]{:S(2)}, u32[]{:S(2)}) collective-permute-start(bf16[6,64,128]{2,1,0:T(8,128)(2,1)S(1)} %get-tuple-element.72), channel_id=1, source_target_pairs={{0,6},{1,7},{2,0},{3,1},{4,2},{5,3},{6,4},{7,5},{8,14},{9,15},{10,... | collective-permute-start | bytes 294920 | tf_op jit(solution)/shard_map/precondition/ppermute | solution.py:33
  118.3 6.7 %collective-permute-start.13 = (bf16[6,64,128]{2,1,0:T(8,128)(2,1)S(1)}, bf16[6,64,128]{2,1,0:T(8,128)(2,1)S(1)}, u32[]{:S(2)}, u32[]{:S(2)}) collective-permute-start(bf16[6,64,128]{2,1,0:T(8,128)(2,1)S(1)} %get-tuple-element.73), channel_id=1, source_target_pairs={{0,7},{1,6},{2,1},{3,0},{4,3},{5,2},{6,5},{7,4},{8,15},{9,14},{10,... | collective-permute-start | bytes 294920 | tf_op jit(solution)/shard_map/precondition/ppermute | solution.py:33
  125.1 9.0 %collective-permute-start.19 = (bf16[32,32,128]{2,1,0:T(8,128)(2,1)S(1)}, bf16[32,32,128]{2,1,0:T(8,128)(2,1)S(1)}, u32[]{:S(2)}, u32[]{:S(2)}) collective-permute-start(bf16[32,32,128]{2,1,0:T(8,128)(2,1)S(1)} %all-to-all-done.3.refs_0_), channel_id=1, source_target_pairs={{0,6},{1,7},{2,0},{3,1},{4,2},{5,3},{6,4},{7,5},{8,14},{9,15},{10,... | collective-permute-start | bytes 786440 | tf_op jit(solution)/shard_map/precondition/ppermute | solution.py:33
  127.6 12.2 %collective-permute-start.17 = (bf16[32,32,128]{2,1,0:T(8,128)(2,1)S(1)}, bf16[32,32,128]{2,1,0:T(8,128)(2,1)S(1)}, u32[]{:S(2)}, u32[]{:S(2)}) collective-permute-start(bf16[32,32,128]{2,1,0:T(8,128)(2,1)S(1)} %all-to-all-done.3.refs_0_), channel_id=1, source_target_pairs={{0,4},{1,5},{2,6},{3,7},{4,0},{5,1},{6,2},{7,3},{8,12},{9,13},{10,... | collective-permute-start | bytes 786440 | tf_op jit(solution)/shard_map/precondition/ppermute | solution.py:33
  128.7 14.2 %collective-permute-start.15 = (bf16[32,32,128]{2,1,0:T(8,128)(2,1)S(1)}, bf16[32,32,128]{2,1,0:T(8,128)(2,1)S(1)}, u32[]{:S(2)}, u32[]{:S(2)}) collective-permute-start(bf16[32,32,128]{2,1,0:T(8,128)(2,1)S(1)} %all-to-all-done.3.refs_0_), channel_id=1, source_target_pairs={{0,2},{1,3},{2,4},{3,5},{4,6},{5,7},{6,0},{7,1},{8,10},{9,11},{10,... | collective-permute-start | bytes 786440 | tf_op jit(solution)/shard_map/precondition/ppermute | solution.py:33
  132.8 10.6 %collective-permute-start.14 = (bf16[32,32,128]{2,1,0:T(8,128)(2,1)S(1)}, bf16[32,32,128]{2,1,0:T(8,128)(2,1)S(1)}, u32[]{:S(2)}, u32[]{:S(2)}) collective-permute-start(bf16[32,32,128]{2,1,0:T(8,128)(2,1)S(1)} %all-to-all-done.3.refs_0_), channel_id=1, source_target_pairs={{0,1},{1,0},{2,3},{3,2},{4,5},{5,4},{6,7},{7,6},{8,9},{9,8},{10,11... | collective-permute-start | bytes 786440 | tf_op jit(solution)/shard_map/precondition/ppermute | solution.py:33
  134.1 9.4 %collective-permute-start.20 = (bf16[32,32,128]{2,1,0:T(8,128)(2,1)S(1)}, bf16[32,32,128]{2,1,0:T(8,128)(2,1)S(1)}, u32[]{:S(2)}, u32[]{:S(2)}) collective-permute-start(bf16[32,32,128]{2,1,0:T(8,128)(2,1)S(1)} %collective-permute-done.19.refs_6_), channel_id=1, source_target_pairs={{0,1},{1,0},{2,3},{3,2},{4,5},{5,4},{6,7},{7,6},{8,9},{9,8},{10,11... | collective-permute-start | bytes 786440 | tf_op jit(solution)/shard_map/precondition/ppermute | solution.py:33
  139.8 3.7 %collective-permute-start.18 = (bf16[32,32,128]{2,1,0:T(8,128)(2,1)S(1)}, bf16[32,32,128]{2,1,0:T(8,128)(2,1)S(1)}, u32[]{:S(2)}, u32[]{:S(2)}) collective-permute-start(bf16[32,32,128]{2,1,0:T(8,128)(2,1)S(1)} %collective-permute-done.17.refs_4_), channel_id=1, source_target_pairs={{0,1},{1,0},{2,3},{3,2},{4,5},{5,4},{6,7},{7,6},{8,9},{9,8},{10,11... | collective-permute-start | bytes 786440 | tf_op jit(solution)/shard_map/precondition/ppermute | solution.py:33
  143.0 1.7 %collective-permute-start.16 = (bf16[32,32,128]{2,1,0:T(8,128)(2,1)S(1)}, bf16[32,32,128]{2,1,0:T(8,128)(2,1)S(1)}, u32[]{:S(2)}, u32[]{:S(2)}) collective-permute-start(bf16[32,32,128]{2,1,0:T(8,128)(2,1)S(1)} %collective-permute-done.15.refs_2_), channel_id=1, source_target_pairs={{0,1},{1,0},{2,3},{3,2},{4,5},{5,4},{6,7},{7,6},{8,9},{9,8},{10,11... | collective-permute-start | bytes 786440 | tf_op jit(solution)/shard_map/precondition/ppermute | solution.py:33
Sparse Core Ops, SparseCore 0:
  39.4 28.9 all-gather.3
  70.8 28.0 all-gather.5

commit v4 on v3

--- a/solution.py
+++ b/solution.py
@@ -37,7 +37,8 @@
     return [p if j == 0 else send(p, *PARTNERS[j]) for j, p in enumerate(pieces)]
 
 
-def gather(piece, own):
+def gather(piece, own=None):
+    own = piece if own is None else own
     out = [piece, send(own, 0, 1)]
     for p in [send(piece, k, 0) for k in range(1, 4)]:
         out += [p, send(p, 0, 1)]
@@ -140,10 +141,11 @@
                 ).astype(bf16)
 
 
-def make_grams(roots, columns, out, image):
+def make_grams(roots, *refs):
+    pieces, (out, image) = refs[:NW], refs[NW:]
     worker = lax.axis_index("worker")
     mine = pl.ds(pl.multiple_of(worker * PART, PART), PART)
-    own = columns[worker]
+    own = pieces[0][...]
     lane = lax.broadcasted_iota(jnp.int32, (1, PART), 1)
     diag = jnp.zeros((1, PART), f32)
     for q in range(4):
@@ -152,21 +154,21 @@
         diag = diag + pltpu.roll(jnp.where(lane < ROWS, both, 0.0), q * ROWS, 1)
     product = own.astype(f32) * diag
     gram = jnp.zeros((BS, PART), f32)
-    for w in range(NW):
+    for piece, source in zip(pieces, sources(worker)):
+        columns = piece[...]
         gram = gram + lax.dot_general(
-            columns[w], columns[w, mine, :], (((1,), (1,)), ((), ())), preferred_element_type=f32
-        )
-        block = roots[w * 4 : (w + 1) * 4, ROWS : 2 * ROWS, :].reshape(PART, PART)
-        product = product + jnp.dot(columns[w], block, preferred_element_type=f32)
-        block = lax.dot_general(
-            columns[w], own, (((0,), (0,)), ((), ())), preferred_element_type=f32
-        )
-        out[w * 4 : (w + 1) * 4, ROWS:, :] = block.astype(bf16).reshape(4, ROWS, PART)
+            columns, piece[mine, :], (((1,), (1,)), ((), ())), preferred_element_type=f32
+        )
+        block = roots[pl.ds(source * 4, 4), ROWS : 2 * ROWS, :].reshape(PART, PART)
+        product = product + jnp.dot(columns, block, preferred_element_type=f32)
+        block = lax.dot_general(columns, own, (((0,), (0,)), ((), ())), preferred_element_type=f32)
+        out[pl.ds(source * 4, 4), ROWS:, :] = block.astype(bf16).reshape(4, ROWS, PART)
     out[:, :ROWS, :] = gram.astype(bf16).reshape(NB, ROWS, PART)
     image[...] = product.astype(bf16)
 
 
-def make_result(after, roots, image, left, out):
+def make_result(roots, image, *refs):
+    pieces, out = refs[:NW], refs[NW]
     diag_rows = roots[:, 2 * ROWS :, :].astype(f32)[:, :1, :]
     row = lax.broadcasted_iota(jnp.int32, (NB, ROWS, PART), 1)
     lane = lax.broadcasted_iota(jnp.int32, (NB, ROWS, PART), 2)
@@ -174,12 +176,9 @@
     spread = spread.astype(bf16).reshape(BS, PART)
     diag = jnp.dot(spread, jnp.ones((PART, PART), bf16), preferred_element_type=f32)
     total = image[...].astype(f32) * diag
-    for w in range(NW):
-        total = total + jnp.dot(
-            left[w].reshape(BS, PART),
-            image[w * PART : (w + 1) * PART, :],
-            preferred_element_type=f32,
-        )
+    for piece, source in zip(pieces, sources(lax.axis_index("worker"))):
+        block = image[pl.ds(pl.multiple_of(source * PART, PART), PART), :]
+        total = total + jnp.dot(piece[...], block, preferred_element_type=f32)
     out[...] = total.astype(bf16).reshape(NB, ROWS, PART)
 
 
@@ -239,10 +238,6 @@
     return lax.all_to_all(value, "shard", 0, 0, tiled=True)
 
 
-def over_worker(value):
-    return lax.all_gather(value, "worker", axis=0, tiled=False)
-
-
 def body(grads, owners, left, right, left_root, right_root):
     tile = shape((NB, ROWS, PART))
     with jax.named_scope("roots"):
@@ -263,7 +258,7 @@
         )
         mine, packed = lax.optimization_barrier((over_shard(mine), exchange(packed)))
     with jax.named_scope("gradients"):
-        columns = over_worker(mine.reshape(BS, PART))
+        columns = gather(mine.reshape(BS, PART))
     with jax.named_scope("roots"):
         roots = call(
             pick_roots,
@@ -271,16 +266,16 @@
             (holder, *packed),
             [SMEM] + [VMEM] * NW,
         )
-        roots = over_shard(roots)
-        root_l = over_worker(roots[:, :ROWS])
+        roots, columns = lax.optimization_barrier((over_shard(roots), columns))
+        root_l = gather(roots[:, :ROWS].reshape(BS, PART))
     with jax.named_scope("grams"):
         grams, image = call(
             make_grams,
             [shape((NB, 2 * ROWS, PART)), shape((BS, PART))],
-            (roots, columns),
+            (roots, *columns),
             flops=6 * BS * BS * PART,
         )
-        grams = over_shard(grams)
+        grams, root_l = lax.optimization_barrier((over_shard(grams), root_l))
         packed = call(
             pack_grams,
             [shape((CAP, 2 * ROWS, PART))] * NW,
@@ -291,8 +286,7 @@
         result = call(
             make_result,
             tile,
-            (packed[0], roots, image, root_l),
-            [ANY] + [VMEM] * 3,
+            (roots, image, *root_l),
             flops=2 * BS * BS * PART,
         )
         result, packed = lax.optimization_barrier((over_shard(result), exchange(packed)))
@@ -310,7 +304,7 @@
                 pltpu.SemaphoreType.DMA((2, CAP)),
             ],
             nbytes=20 << 20,
-            vmem=48,
+            vmem=61,
         )
         own, new_left = lax.optimization_barrier((result, new_left))
     with jax.named_scope("precondition"):

time: 153 us -> 141 us (0.922)
  blocking collectives: 49.2 us -> 0 us
  starting transfers between devices: 50.7 us -> 90.8 us
  between operations: 14.2 us -> 1.02 us
  waiting for transfers between devices: 18.7 us -> 31.3 us
  local copies, waits for them, and re-layouts: 6.16 us -> 2.15 us
    all_to_all x2 -> x0, blocking collectives: 49.2 us -> none  [over_shard(): return lax.all_to_all(value, 'shard', 0, 0, tiled=True)]
    ppermute x21 -> x35, starting transfers between devices: 29 us -> 50.8 us  [send(): lax.ppermute(value, 'worker', [(w, partner(w, k, other)) for w in range(N...]
    all_to_all x2 -> x4, starting transfers between devices: 21.6 us -> 40 us  [over_shard(): return lax.all_to_all(value, 'shard', 0, 0, tiled=True)]
    ppermute x21 -> x35, waiting for transfers between devices: 15.7 us -> 31.3 us  [send(): lax.ppermute(value, 'worker', [(w, partner(w, k, other)) for w in range(N...]
    unnamed x16 -> x22, local copies, waits for them, and re-layouts: 5.44 us -> 2.13 us
    all_gather x2 -> x0, waiting for transfers between devices: 2.95 us -> none  [over_worker(): return lax.all_gather(value, 'worker', axis=0, tiled=False)]
  transfers between devices with their start and end apart: 25 -> 39, of which waited for: 9 -> 14; matrix products, arithmetic and copies ran while one was open for 0% -> 0% of each run, Pallas kernels for 5% -> 3%
where the time goes in v4:
time: 141 us; the launch traced here: 140 us
  starting transfers between devices  90.8 us (64%)
  waiting for transfers between devices  31.3 us (22%)
  Pallas kernels  15.1 us (11%)
  local copies, waits for them, and re-layouts  2.15 us (2%)
    ppermute x35, starting transfers between devices, send(): lax.ppermute(value, 'worker', [(w, partner(w, k, other)) for w in range(N...  50.8 us
    all_to_all x4, starting transfers between devices, over_shard(): return lax.all_to_all(value, 'shard', 0, 0, tiled=True)  40 us
    ppermute x35, waiting for transfers between devices, send(): lax.ppermute(value, 'worker', [(w, partner(w, k, other)) for w in range(N...  31.3 us
    pallas_call x7, Pallas kernels, call(): pl.pallas_call(kernel, out_shape=outs, in_specs=in_specs or [VMEM] * len(...  15.1 us
  transfers between devices with their start and end apart: 39, of which 14 were waited for; matrix products, arithmetic and copies ran while one was open for 0% of the time, Pallas kernels for 3%

profile of v4, /device:TPU:1, one launch (start us, length us, event | category | flops | bytes accessed | tf_op | source)
XLA Modules:
  0.0 140.4 jit_solution(6508854365575074131)
XLA Ops:
  0.6 3.5 %roots.2 = (bf16[400,128]{1,0:T(8,128)(2,1)}, bf16[400,128]{1,0:T(8,128)(2,1)}, bf16[400,128]{1,0:T(8,128)(2,1)}, bf16[400,128]{1,0:T(8,128)(2,1)}, bf16[400,128...) custom-call(s32[32]{0:T(128)} %bitcast.23, ...), custom_call_target="tpu_custom_call" | custom-call | bytes 2097152 | tf_op jit(solution)/shard_map/roots/pallas_call | solution.py:57
  4.1 12.0 %all-to-all-start = ((bf16[32,32,128]{2,1,0:T(8,128)(2,1)}), bf16[32,32,128]{2,1,0:T(8,128)(2,1)S(1)}, u32[]{:S(2)}, u32[]{:S(2)}) async-start(bf16[32,32,128]{2,1,0:T(8,128)(2,1)} %get-tuple-element.64), calls=%async_computation | async-start | bytes 524288 | tf_op jit(solution)/shard_map/roots/all_to_all | solution.py:238
  16.2 1.0 collective-permute-start
  17.2 1.2 collective-permute-start.1
  18.4 1.5 %collective-permute-start.2 = (bf16[400,128]{1,0:T(8,128)(2,1)}, bf16[400,128]{1,0:T(8,128)(2,1)S(1)}, u32[]{:S(2)}, u32[]{:S(2)}) collective-permute-start(bf16[400,128]{1,0:T(8,128)(2,1)} %get-tuple-element.68), channel_id=1, source_target_pairs={{0,3},{1,2},{2,5},{3,4},{4,7},{5,6},{6,1},{7,0},{8,11},{9,10},{10,... | collective-permute-start | bytes 307208 | tf_op jit(solution)/shard_map/roots/ppermute | solution.py:33
  19.9 1.4 %collective-permute-start.3 = (bf16[400,128]{1,0:T(8,128)(2,1)}, bf16[400,128]{1,0:T(8,128)(2,1)S(1)}, u32[]{:S(2)}, u32[]{:S(2)}) collective-permute-start(bf16[400,128]{1,0:T(8,128)(2,1)} %get-tuple-element.69), channel_id=1, source_target_pairs={{0,4},{1,5},{2,6},{3,7},{4,0},{5,1},{6,2},{7,3},{8,12},{9,13},{10,... | collective-permute-start | bytes 307208 | tf_op jit(solution)/shard_map/roots/ppermute | solution.py:33
  21.3 1.9 %collective-permute-start.4 = (bf16[400,128]{1,0:T(8,128)(2,1)}, bf16[400,128]{1,0:T(8,128)(2,1)S(1)}, u32[]{:S(2)}, u32[]{:S(2)}) collective-permute-start(bf16[400,128]{1,0:T(8,128)(2,1)} %get-tuple-element.70), channel_id=1, source_target_pairs={{0,5},{1,4},{2,7},{3,6},{4,1},{5,0},{6,3},{7,2},{8,13},{9,12},{10,... | collective-permute-start | bytes 307208 | tf_op jit(solution)/shard_map/roots/ppermute | solution.py:33
  23.2 1.5 %collective-permute-start.5 = (bf16[400,128]{1,0:T(8,128)(2,1)}, bf16[400,128]{1,0:T(8,128)(2,1)S(1)}, u32[]{:S(2)}, u32[]{:S(2)}) collective-permute-start(bf16[400,128]{1,0:T(8,128)(2,1)} %get-tuple-element.71), channel_id=1, source_target_pairs={{0,6},{1,7},{2,0},{3,1},{4,2},{5,3},{6,4},{7,5},{8,14},{9,15},{10,... | collective-permute-start | bytes 307208 | tf_op jit(solution)/shard_map/roots/ppermute | solution.py:33
  24.7 0.9 collective-permute-start.6
  25.7 2.7 %collective-permute-done.3.refs_4_ = bf16[400,128]{1,0:T(8,128)(2,1)S(1)} collective-permute-done((bf16[400,128]{1,0:T(8,128)(2,1)}, bf16[400,128]{1,0:T(8,128)(2,1)S(1)}, u32[]{:S(2)}, u32[]{:S(2)}) %collective-permute-start.3) | collective-permute-done | bytes 102432 | tf_op jit(solution)/shard_map/roots/ppermute | solution.py:33
  28.5 2.4 %collective-permute-done.4.refs_5_ = bf16[400,128]{1,0:T(8,128)(2,1)S(1)} collective-permute-done((bf16[400,128]{1,0:T(8,128)(2,1)}, bf16[400,128]{1,0:T(8,128)(2,1)S(1)}, u32[]{:S(2)}, u32[]{:S(2)}) %collective-permute-start.4) | collective-permute-done | bytes 102432 | tf_op jit(solution)/shard_map/roots/ppermute | solution.py:33
  30.8 1.1 collective-permute-done.6.refs_7_
  31.9 0.9 copy-done
  33.4 1.8 %roots.3 = bf16[32,80,128]{2,1,0:T(8,128)(2,1)} custom-call(s32[48]{0:T(128)S(1)} %copy-done.2, bf16[400,128]{1,0:T(8,128)(2,1)S(1)} %copy-done, bf16[400,128]{1,0:T(8,128)(2,1)S(1)} %collective-permute-done.refs_1_, bf16[400,128]{1,0:T(8,128)(2,1)S(1)} %collective-permute-done.1.refs_2_, bf16[400,128]{1,0:T(8,128)(2,1)S(1)} %collective-permute-done.2.refs_3_, ...), custom_call_target="tpu_custom_call" | custom-call | bytes 2097152 | tf_op jit(solution)/shard_map/roots/pallas_call | solution.py:57
  35.2 9.5 %all-to-all-start.1 = ((bf16[32,80,128]{2,1,0:T(8,128)(2,1)}), bf16[32,80,128]{2,1,0:T(8,128)(2,1)S(1)}, u32[]{:S(2)}, u32[]{:S(2)}) async-start(bf16[32,80,128]{2,1,0:T(8,128)(2,1)} %roots.3), calls=%async_computation.1 | async-start | bytes 1310720 | tf_op jit(solution)/shard_map/roots/all_to_all | solution.py:238
  44.7 2.7 %collective-permute-start.12 = (bf16[1024,128]{1,0:T(8,128)(2,1)S(1)}, bf16[1024,128]{1,0:T(8,128)(2,1)S(1)}, u32[]{:S(2)}, u32[]{:S(2)}) collective-permute-start(bf16[1024,128]{1,0:T(8,128)(2,1)S(1)} %bitcast.14), channel_id=1, source_target_pairs={{0,6},{1,7},{2,0},{3,1},{4,2},{5,3},{6,4},{7,5},{8,14},{9,15},{10,... | collective-permute-start | bytes 786440 | tf_op jit(solution)/shard_map/gradients/ppermute | solution.py:33
  47.4 1.2 collective-permute-start.10
  48.6 1.2 collective-permute-start.7
  49.9 3.0 %collective-permute-done.12.refs_6_ = bf16[1024,128]{1,0:T(8,128)(2,1)S(1)} collective-permute-done((bf16[1024,128]{1,0:T(8,128)(2,1)S(1)}, bf16[1024,128]{1,0:T(8,128)(2,1)S(1)}, u32[]{:S(2)}, u32[]{:S(2)}) %collective-permute-start.12) | collective-permute-done | bytes 262176 | tf_op jit(solution)/shard_map/gradients/ppermute | solution.py:33
  52.9 6.7 %collective-permute-start.13 = (bf16[1024,128]{1,0:T(8,128)(2,1)S(1)}, bf16[1024,128]{1,0:T(8,128)(2,1)S(1)}, u32[]{:S(2)}, u32[]{:S(2)}) collective-permute-start(bf16[1024,128]{1,0:T(8,128)(2,1)S(1)} %collective-permute-done.12.refs_6_), channel_id=1, source_target_pairs={{0,1},{1,0},{2,3},{3,2},{4,5},{5,4},{6,7},{7,6},{8,9},{9,8},{10,11... | collective-permute-start | bytes 786440 | tf_op jit(solution)/shard_map/gradients/ppermute | solution.py:33
  59.6 3.2 %collective-permute-done.8.refs_2_ = bf16[1024,128]{1,0:T(8,128)(2,1)S(1)} collective-permute-done((bf16[1024,128]{1,0:T(8,128)(2,1)S(1)}, bf16[1024,128]{1,0:T(8,128)(2,1)S(1)}, u32[]{:S(2)}, u32[]{:S(2)}) %collective-permute-start.8) | collective-permute-done | bytes 262176 | tf_op jit(solution)/shard_map/gradients/ppermute | solution.py:33
  63.2 1.1 collective-permute-done.9.refs_3_
  64.4 2.6 %grams.2 = (bf16[32,64,128]{2,1,0:T(8,128)(2,1)}, bf16[1024,128]{1,0:T(8,128)(2,1)S(1)}) custom-call(bf16[32,80,128]{2,1,0:T(8,128)(2,1)S(1)} %all-to-all-done.1.roots, bf16[1024,128]{1,0:T(8,128)(2,1)S(1)} %bitcast.18, bf16[1024,128]{1,0:T(8,128)(2,1)S(1)} %collective-permute-done.7.refs_1_, bf16[1024,128]{1,0:T(8,128)(2,1)S(1)} %collective-permute-done.8.refs_2_, ...), custom_call_target="tpu_custom_call" | custom-call | flops 805306368 | bytes 2097152 | tf_op jit(solution)/shard_map/grams/pallas_call | solution.py:57
  67.0 9.2 %all-to-all-start.2 = ((bf16[32,64,128]{2,1,0:T(8,128)(2,1)}), bf16[32,64,128]{2,1,0:T(8,128)(2,1)S(1)}, u32[]{:S(2)}, u32[]{:S(2)}) async-start(bf16[32,64,128]{2,1,0:T(8,128)(2,1)} %get-tuple-element.92), calls=%async_computation.2 | async-start | bytes 1048576 | tf_op jit(solution)/shard_map/grams/all_to_all | solution.py:238
  76.8 1.1 collective-permute-start.17
  78.5 1.5 %collective-permute-start.14 = (bf16[1024,128]{1,0:T(8,128)(2,1)S(1)}, bf16[1024,128]{1,0:T(8,128)(2,1)S(1)}, u32[]{:S(2)}, u32[]{:S(2)}) collective-permute-start(bf16[1024,128]{1,0:T(8,128)(2,1)S(1)} %bitcast.12), channel_id=1, source_target_pairs={{0,1},{1,0},{2,3},{3,2},{4,5},{5,4},{6,7},{7,6},{8,9},{9,8},{10,11... | collective-permute-start | bytes 786440 | tf_op jit(solution)/shard_map/roots/ppermute | solution.py:33
  80.0 3.6 %collective-permute-done.19.refs_6_ = bf16[1024,128]{1,0:T(8,128)(2,1)S(1)} collective-permute-done((bf16[1024,128]{1,0:T(8,128)(2,1)S(1)}, bf16[1024,128]{1,0:T(8,128)(2,1)S(1)}, u32[]{:S(2)}, u32[]{:S(2)}) %collective-permute-start.19) | collective-permute-done | bytes 262176 | tf_op jit(solution)/shard_map/roots/ppermute | solution.py:33
  83.6 2.7 %collective-permute-start.20 = (bf16[1024,128]{1,0:T(8,128)(2,1)S(1)}, bf16[1024,128]{1,0:T(8,128)(2,1)S(1)}, u32[]{:S(2)}, u32[]{:S(2)}) collective-permute-start(bf16[1024,128]{1,0:T(8,128)(2,1)S(1)} %collective-permute-done.19.refs_6_), channel_id=1, source_target_pairs={{0,1},{1,0},{2,3},{3,2},{4,5},{5,4},{6,7},{7,6},{8,9},{9,8},{10,11... | collective-permute-start | bytes 786440 | tf_op jit(solution)/shard_map/roots/ppermute | solution.py:33
  86.2 2.3 %collective-permute-start.18 = (bf16[1024,128]{1,0:T(8,128)(2,1)S(1)}, bf16[1024,128]{1,0:T(8,128)(2,1)S(1)}, u32[]{:S(2)}, u32[]{:S(2)}) collective-permute-start(bf16[1024,128]{1,0:T(8,128)(2,1)S(1)} %collective-permute-done.17.refs_4_), channel_id=1, source_target_pairs={{0,1},{1,0},{2,3},{3,2},{4,5},{5,4},{6,7},{7,6},{8,9},{9,8},{10,11... | collective-permute-start | bytes 786440 | tf_op jit(solution)/shard_map/roots/ppermute | solution.py:33
  88.5 3.6 %collective-permute-done.15.refs_2_ = bf16[1024,128]{1,0:T(8,128)(2,1)S(1)} collective-permute-done((bf16[1024,128]{1,0:T(8,128)(2,1)S(1)}, bf16[1024,128]{1,0:T(8,128)(2,1)S(1)}, u32[]{:S(2)}, u32[]{:S(2)}) %collective-permute-start.15) | collective-permute-done | bytes 262176 | tf_op jit(solution)/shard_map/roots/ppermute | solution.py:33
  92.7 1.1 collective-permute-done.16.refs_3_
  93.8 1.5 %precondition.2 = bf16[32,32,128]{2,1,0:T(8,128)(2,1)} custom-call(bf16[32,80,128]{2,1,0:T(8,128)(2,1)S(1)} %all-to-all-done.1.roots, bf16[1024,128]{1,0:T(8,128)(2,1)S(1)} %get-tuple-element.91.image, bf16[1024,128]{1,0:T(8,128)(2,1)S(1)} %bitcast.13, bf16[1024,128]{1,0:T(8,128)(2,1)S(1)} %collective-permute-done.14.refs_1_, ...), custom_call_target="tpu_custom_call" | custom-call | flops 268435456 | bytes 2097152 | tf_op jit(solution)/shard_map/precondition/pallas_call | solution.py:57
  95.3 9.2 %all-to-all-start.3 = ((bf16[32,32,128]{2,1,0:T(8,128)(2,1)}), bf16[32,32,128]{2,1,0:T(8,128)(2,1)S(1)}, u32[]{:S(2)}, u32[]{:S(2)}) async-start(bf16[32,32,128]{2,1,0:T(8,128)(2,1)} %precondition.2), calls=%async_computation.3 | async-start | bytes 524288 | tf_op jit(solution)/shard_map/precondition/all_to_all | solution.py:238
  105.9 0.7 collective-permute-start.21
  106.5 1.0 collective-permute-start.23
  107.5 3.1 %collective-permute-start.24 = (bf16[6,64,128]{2,1,0:T(8,128)(2,1)S(1)}, bf16[6,64,128]{2,1,0:T(8,128)(2,1)S(1)}, u32[]{:S(2)}, u32[]{:S(2)}) collective-permute-start(bf16[6,64,128]{2,1,0:T(8,128)(2,1)S(1)} %get-tuple-element.106), channel_id=1, source_target_pairs={{0,4},{1,5},{2,6},{3,7},{4,0},{5,1},{6,2},{7,3},{8,12},{9,13},{10,... | collective-permute-start | bytes 294920 | tf_op jit(solution)/shard_map/precondition/ppermute | solution.py:33
  110.8 1.9 %collective-permute-start.26 = (bf16[6,64,128]{2,1,0:T(8,128)(2,1)S(1)}, bf16[6,64,128]{2,1,0:T(8,128)(2,1)S(1)}, u32[]{:S(2)}, u32[]{:S(2)}) collective-permute-start(bf16[6,64,128]{2,1,0:T(8,128)(2,1)S(1)} %get-tuple-element.108), channel_id=1, source_target_pairs={{0,6},{1,7},{2,0},{3,1},{4,2},{5,3},{6,4},{7,5},{8,14},{9,15},{10,... | collective-permute-start | bytes 294920 | tf_op jit(solution)/shard_map/precondition/ppermute | solution.py:33
  112.8 1.6 %collective-permute-start.27 = (bf16[6,64,128]{2,1,0:T(8,128)(2,1)S(1)}, bf16[6,64,128]{2,1,0:T(8,128)(2,1)S(1)}, u32[]{:S(2)}, u32[]{:S(2)}) collective-permute-start(bf16[6,64,128]{2,1,0:T(8,128)(2,1)S(1)} %get-tuple-element.109), channel_id=1, source_target_pairs={{0,7},{1,6},{2,1},{3,0},{4,3},{5,2},{6,5},{7,4},{8,15},{9,14},{10,... | collective-permute-start | bytes 294920 | tf_op jit(solution)/shard_map/precondition/ppermute | solution.py:33
  114.4 4.2 %collective-permute-done.23.refs_3_ = bf16[6,64,128]{2,1,0:T(8,128)(2,1)S(1)} collective-permute-done((bf16[6,64,128]{2,1,0:T(8,128)(2,1)S(1)}, bf16[6,64,128]{2,1,0:T(8,128)(2,1)S(1)}, u32[]{:S(2)}, u32[]{:S(2)}) %collective-permute-start.23) | collective-permute-done | bytes 98336 | tf_op jit(solution)/shard_map/precondition/ppermute | solution.py:33
  118.6 0.7 collective-permute-done.27.refs_7_
  119.3 2.5 %collective-permute-start.33 = (bf16[32,32,128]{2,1,0:T(8,128)(2,1)S(1)}, bf16[32,32,128]{2,1,0:T(8,128)(2,1)S(1)}, u32[]{:S(2)}, u32[]{:S(2)}) collective-permute-start(bf16[32,32,128]{2,1,0:T(8,128)(2,1)S(1)} %all-to-all-done.3.refs_0_), channel_id=1, source_target_pairs={{0,6},{1,7},{2,0},{3,1},{4,2},{5,3},{6,4},{7,5},{8,14},{9,15},{10,... | collective-permute-start | bytes 786440 | tf_op jit(solution)/shard_map/precondition/ppermute | solution.py:33
  121.8 0.9 collective-permute-start.31
  122.8 3.7 %factors.1 = (f32[6,32,1024]{2,1,0:T(8,128)}, f32[6,32,1024]{2,1,0:T(8,128)}) custom-call(s32[48]{0:T(128)} %get-tuple-element.63.holder, f32[6,32,1024]{2,1,0:T(8,128)} %bitcast.19, f32[6,32,1024]{2,1,0:T(8,128)} %bitcast.20, bf16[6,64,128]{2,1,0:T(8,128)(2,1)} %copy-done.1, bf16[6,64,128]{2,1,0:T(8,128)(2,1)} %copy-done.4, bf16[6,64,128]{2,1,0:T(8,128)(2,1)} %copy-done.5, ...), custom_call_target="tpu_custom_call" | custom-call | bytes 20971520 | tf_op jit(solution)/shard_map/factors/pallas_call | solution.py:57
  126.5 1.0 collective-permute-start.28
  127.5 6.5 %collective-permute-start.34 = (bf16[32,32,128]{2,1,0:T(8,128)(2,1)S(1)}, bf16[32,32,128]{2,1,0:T(8,128)(2,1)S(1)}, u32[]{:S(2)}, u32[]{:S(2)}) collective-permute-start(bf16[32,32,128]{2,1,0:T(8,128)(2,1)S(1)} %collective-permute-done.33.refs_6_), channel_id=1, source_target_pairs={{0,1},{1,0},{2,3},{3,2},{4,5},{5,4},{6,7},{7,6},{8,9},{9,8},{10,11... | collective-permute-start | bytes 786440 | tf_op jit(solution)/shard_map/precondition/ppermute | solution.py:33
  134.0 3.2 %collective-permute-done.29.refs_2_ = bf16[32,32,128]{2,1,0:T(8,128)(2,1)S(1)} collective-permute-done((bf16[32,32,128]{2,1,0:T(8,128)(2,1)S(1)}, bf16[32,32,128]{2,1,0:T(8,128)(2,1)S(1)}, u32[]{:S(2)}, u32[]{:S(2)}) %collective-permute-start.29) | collective-permute-done | bytes 262176 | tf_op jit(solution)/shard_map/precondition/ppermute | solution.py:33
  137.7 1.1 collective-permute-done.30.refs_3_
  138.8 1.4 precondition.3
  (60 shorter events, 5.0 us)
Async XLA Ops:
  4.1 27.8 %all-to-all-start = ((bf16[32,32,128]{2,1,0:T(8,128)(2,1)}), bf16[32,32,128]{2,1,0:T(8,128)(2,1)S(1)}, u32[]{:S(2)}, u32[]{:S(2)}) async-start(bf16[32,32,128]{2,1,0:T(8,128)(2,1)} %get-tuple-element.64), calls=%async_computation | async-start | bytes 524288 | tf_op jit(solution)/shard_map/roots/all_to_all | solution.py:238
  16.2 7.0 %collective-permute-start = (bf16[400,128]{1,0:T(8,128)(2,1)}, bf16[400,128]{1,0:T(8,128)(2,1)S(1)}, u32[]{:S(2)}, u32[]{:S(2)}) collective-permute-start(bf16[400,128]{1,0:T(8,128)(2,1)} %get-tuple-element.66), channel_id=1, source_target_pairs={{0,1},{1,0},{2,3},{3,2},{4,5},{5,4},{6,7},{7,6},{8,9},{9,8},{10,11... | collective-permute-start | bytes 307208 | tf_op jit(solution)/shard_map/roots/ppermute | solution.py:33
  17.2 7.5 %collective-permute-start.1 = (bf16[400,128]{1,0:T(8,128)(2,1)}, bf16[400,128]{1,0:T(8,128)(2,1)S(1)}, u32[]{:S(2)}, u32[]{:S(2)}) collective-permute-start(bf16[400,128]{1,0:T(8,128)(2,1)} %get-tuple-element.67), channel_id=1, source_target_pairs={{0,2},{1,3},{2,4},{3,5},{4,6},{5,7},{6,0},{7,1},{8,10},{9,11},{10,... | collective-permute-start | bytes 307208 | tf_op jit(solution)/shard_map/roots/ppermute | solution.py:33
  18.4 7.3 %collective-permute-start.2 = (bf16[400,128]{1,0:T(8,128)(2,1)}, bf16[400,128]{1,0:T(8,128)(2,1)S(1)}, u32[]{:S(2)}, u32[]{:S(2)}) collective-permute-start(bf16[400,128]{1,0:T(8,128)(2,1)} %get-tuple-element.68), channel_id=1, source_target_pairs={{0,3},{1,2},{2,5},{3,4},{4,7},{5,6},{6,1},{7,0},{8,11},{9,10},{10,... | collective-permute-start | bytes 307208 | tf_op jit(solution)/shard_map/roots/ppermute | solution.py:33
  19.9 8.6 %collective-permute-start.3 = (bf16[400,128]{1,0:T(8,128)(2,1)}, bf16[400,128]{1,0:T(8,128)(2,1)S(1)}, u32[]{:S(2)}, u32[]{:S(2)}) collective-permute-start(bf16[400,128]{1,0:T(8,128)(2,1)} %get-tuple-element.69), channel_id=1, source_target_pairs={{0,4},{1,5},{2,6},{3,7},{4,0},{5,1},{6,2},{7,3},{8,12},{9,13},{10,... | collective-permute-start | bytes 307208 | tf_op jit(solution)/shard_map/roots/ppermute | solution.py:33
  21.3 9.5 %collective-permute-start.4 = (bf16[400,128]{1,0:T(8,128)(2,1)}, bf16[400,128]{1,0:T(8,128)(2,1)S(1)}, u32[]{:S(2)}, u32[]{:S(2)}) collective-permute-start(bf16[400,128]{1,0:T(8,128)(2,1)} %get-tuple-element.70), channel_id=1, source_target_pairs={{0,5},{1,4},{2,7},{3,6},{4,1},{5,0},{6,3},{7,2},{8,13},{9,12},{10,... | collective-permute-start | bytes 307208 | tf_op jit(solution)/shard_map/roots/ppermute | solution.py:33
  23.2 7.6 %collective-permute-start.5 = (bf16[400,128]{1,0:T(8,128)(2,1)}, bf16[400,128]{1,0:T(8,128)(2,1)S(1)}, u32[]{:S(2)}, u32[]{:S(2)}) collective-permute-start(bf16[400,128]{1,0:T(8,128)(2,1)} %get-tuple-element.71), channel_id=1, source_target_pairs={{0,6},{1,7},{2,0},{3,1},{4,2},{5,3},{6,4},{7,5},{8,14},{9,15},{10,... | collective-permute-start | bytes 307208 | tf_op jit(solution)/shard_map/roots/ppermute | solution.py:33
  24.7 7.3 %collective-permute-start.6 = (bf16[400,128]{1,0:T(8,128)(2,1)}, bf16[400,128]{1,0:T(8,128)(2,1)S(1)}, u32[]{:S(2)}, u32[]{:S(2)}) collective-permute-start(bf16[400,128]{1,0:T(8,128)(2,1)} %get-tuple-element.72), channel_id=1, source_target_pairs={{0,7},{1,6},{2,1},{3,0},{4,3},{5,2},{6,5},{7,4},{8,15},{9,14},{10,... | collective-permute-start | bytes 307208 | tf_op jit(solution)/shard_map/roots/ppermute | solution.py:33
  31.9 0.9 copy-start
  35.2 29.2 %all-to-all-start.1 = ((bf16[32,80,128]{2,1,0:T(8,128)(2,1)}), bf16[32,80,128]{2,1,0:T(8,128)(2,1)S(1)}, u32[]{:S(2)}, u32[]{:S(2)}) async-start(bf16[32,80,128]{2,1,0:T(8,128)(2,1)} %roots.3), calls=%async_computation.1 | async-start | bytes 1310720 | tf_op jit(solution)/shard_map/roots/all_to_all | solution.py:238
  44.7 8.1 %collective-permute-start.12 = (bf16[1024,128]{1,0:T(8,128)(2,1)S(1)}, bf16[1024,128]{1,0:T(8,128)(2,1)S(1)}, u32[]{:S(2)}, u32[]{:S(2)}) collective-permute-start(bf16[1024,128]{1,0:T(8,128)(2,1)S(1)} %bitcast.14), channel_id=1, source_target_pairs={{0,6},{1,7},{2,0},{3,1},{4,2},{5,3},{6,4},{7,5},{8,14},{9,15},{10,... | collective-permute-start | bytes 786440 | tf_op jit(solution)/shard_map/gradients/ppermute | solution.py:33
  47.4 12.2 %collective-permute-start.10 = (bf16[1024,128]{1,0:T(8,128)(2,1)S(1)}, bf16[1024,128]{1,0:T(8,128)(2,1)S(1)}, u32[]{:S(2)}, u32[]{:S(2)}) collective-permute-start(bf16[1024,128]{1,0:T(8,128)(2,1)S(1)} %bitcast.15), channel_id=1, source_target_pairs={{0,4},{1,5},{2,6},{3,7},{4,0},{5,1},{6,2},{7,3},{8,12},{9,13},{10,... | collective-permute-start | bytes 786440 | tf_op jit(solution)/shard_map/gradients/ppermute | solution.py:33
  48.6 14.1 %collective-permute-start.8 = (bf16[1024,128]{1,0:T(8,128)(2,1)S(1)}, bf16[1024,128]{1,0:T(8,128)(2,1)S(1)}, u32[]{:S(2)}, u32[]{:S(2)}) collective-permute-start(bf16[1024,128]{1,0:T(8,128)(2,1)S(1)} %bitcast.16), channel_id=1, source_target_pairs={{0,2},{1,3},{2,4},{3,5},{4,6},{5,7},{6,0},{7,1},{8,10},{9,11},{10,... | collective-permute-start | bytes 786440 | tf_op jit(solution)/shard_map/gradients/ppermute | solution.py:33
  48.6 14.6 %collective-permute-start.7 = (bf16[1024,128]{1,0:T(8,128)(2,1)S(1)}, bf16[1024,128]{1,0:T(8,128)(2,1)S(1)}, u32[]{:S(2)}, u32[]{:S(2)}) collective-permute-start(bf16[1024,128]{1,0:T(8,128)(2,1)S(1)} %bitcast.17), channel_id=1, source_target_pairs={{0,1},{1,0},{2,3},{3,2},{4,5},{5,4},{6,7},{7,6},{8,9},{9,8},{10,11... | collective-permute-start | bytes 786440 | tf_op jit(solution)/shard_map/gradients/ppermute | solution.py:33
  52.9 10.4 %collective-permute-start.13 = (bf16[1024,128]{1,0:T(8,128)(2,1)S(1)}, bf16[1024,128]{1,0:T(8,128)(2,1)S(1)}, u32[]{:S(2)}, u32[]{:S(2)}) collective-permute-start(bf16[1024,128]{1,0:T(8,128)(2,1)S(1)} %collective-permute-done.12.refs_6_), channel_id=1, source_target_pairs={{0,1},{1,0},{2,3},{3,2},{4,5},{5,4},{6,7},{7,6},{8,9},{9,8},{10,11... | collective-permute-start | bytes 786440 | tf_op jit(solution)/shard_map/gradients/ppermute | solution.py:33
  59.6 3.7 %collective-permute-start.11 = (bf16[1024,128]{1,0:T(8,128)(2,1)S(1)}, bf16[1024,128]{1,0:T(8,128)(2,1)S(1)}, u32[]{:S(2)}, u32[]{:S(2)}) collective-permute-start(bf16[1024,128]{1,0:T(8,128)(2,1)S(1)} %collective-permute-done.10.refs_4_), channel_id=1, source_target_pairs={{0,1},{1,0},{2,3},{3,2},{4,5},{5,4},{6,7},{7,6},{8,9},{9,8},{10,11... | collective-permute-start | bytes 786440 | tf_op jit(solution)/shard_map/gradients/ppermute | solution.py:33
  62.7 1.7 %collective-permute-start.9 = (bf16[1024,128]{1,0:T(8,128)(2,1)S(1)}, bf16[1024,128]{1,0:T(8,128)(2,1)S(1)}, u32[]{:S(2)}, u32[]{:S(2)}) collective-permute-start(bf16[1024,128]{1,0:T(8,128)(2,1)S(1)} %collective-permute-done.8.refs_2_), channel_id=1, source_target_pairs={{0,1},{1,0},{2,3},{3,2},{4,5},{5,4},{6,7},{7,6},{8,9},{9,8},{10,11... | collective-permute-start | bytes 786440 | tf_op jit(solution)/shard_map/gradients/ppermute | solution.py:33
  67.0 26.8 %all-to-all-start.2 = ((bf16[32,64,128]{2,1,0:T(8,128)(2,1)}), bf16[32,64,128]{2,1,0:T(8,128)(2,1)S(1)}, u32[]{:S(2)}, u32[]{:S(2)}) async-start(bf16[32,64,128]{2,1,0:T(8,128)(2,1)} %get-tuple-element.92), calls=%async_computation.2 | async-start | bytes 1048576 | tf_op jit(solution)/shard_map/grams/all_to_all | solution.py:238
  76.3 28.3 %copy-start.3 = (s32[48]{0:T(128)S(1)}, s32[48]{0:T(128)}, u32[]{:S(2)}) copy-start(s32[48]{0:T(128)} %get-tuple-element.63.holder) | copy-start | bytes 580
  76.3 7.3 %collective-permute-start.19 = (bf16[1024,128]{1,0:T(8,128)(2,1)S(1)}, bf16[1024,128]{1,0:T(8,128)(2,1)S(1)}, u32[]{:S(2)}, u32[]{:S(2)}) collective-permute-start(bf16[1024,128]{1,0:T(8,128)(2,1)S(1)} %bitcast.9), channel_id=1, source_target_pairs={{0,6},{1,7},{2,0},{3,1},{4,2},{5,3},{6,4},{7,5},{8,14},{9,15},{10,... | collective-permute-start | bytes 786440 | tf_op jit(solution)/shard_map/roots/ppermute | solution.py:33
  76.8 9.4 %collective-permute-start.17 = (bf16[1024,128]{1,0:T(8,128)(2,1)S(1)}, bf16[1024,128]{1,0:T(8,128)(2,1)S(1)}, u32[]{:S(2)}, u32[]{:S(2)}) collective-permute-start(bf16[1024,128]{1,0:T(8,128)(2,1)S(1)} %bitcast.10), channel_id=1, source_target_pairs={{0,4},{1,5},{2,6},{3,7},{4,0},{5,1},{6,2},{7,3},{8,12},{9,13},{10,... | collective-permute-start | bytes 786440 | tf_op jit(solution)/shard_map/roots/ppermute | solution.py:33
  77.9 14.2 %collective-permute-start.15 = (bf16[1024,128]{1,0:T(8,128)(2,1)S(1)}, bf16[1024,128]{1,0:T(8,128)(2,1)S(1)}, u32[]{:S(2)}, u32[]{:S(2)}) collective-permute-start(bf16[1024,128]{1,0:T(8,128)(2,1)S(1)} %bitcast.11), channel_id=1, source_target_pairs={{0,2},{1,3},{2,4},{3,5},{4,6},{5,7},{6,0},{7,1},{8,10},{9,11},{10,... | collective-permute-start | bytes 786440 | tf_op jit(solution)/shard_map/roots/ppermute | solution.py:33
  78.5 14.2 %collective-permute-start.14 = (bf16[1024,128]{1,0:T(8,128)(2,1)S(1)}, bf16[1024,128]{1,0:T(8,128)(2,1)S(1)}, u32[]{:S(2)}, u32[]{:S(2)}) collective-permute-start(bf16[1024,128]{1,0:T(8,128)(2,1)S(1)} %bitcast.12), channel_id=1, source_target_pairs={{0,1},{1,0},{2,3},{3,2},{4,5},{5,4},{6,7},{7,6},{8,9},{9,8},{10,11... | collective-permute-start | bytes 786440 | tf_op jit(solution)/shard_map/roots/ppermute | solution.py:33
  83.6 9.1 %collective-permute-start.20 = (bf16[1024,128]{1,0:T(8,128)(2,1)S(1)}, bf16[1024,128]{1,0:T(8,128)(2,1)S(1)}, u32[]{:S(2)}, u32[]{:S(2)}) collective-permute-start(bf16[1024,128]{1,0:T(8,128)(2,1)S(1)} %collective-permute-done.19.refs_6_), channel_id=1, source_target_pairs={{0,1},{1,0},{2,3},{3,2},{4,5},{5,4},{6,7},{7,6},{8,9},{9,8},{10,11... | collective-permute-start | bytes 786440 | tf_op jit(solution)/shard_map/roots/ppermute | solution.py:33
  86.2 6.5 %collective-permute-start.18 = (bf16[1024,128]{1,0:T(8,128)(2,1)S(1)}, bf16[1024,128]{1,0:T(8,128)(2,1)S(1)}, u32[]{:S(2)}, u32[]{:S(2)}) collective-permute-start(bf16[1024,128]{1,0:T(8,128)(2,1)S(1)} %collective-permute-done.17.refs_4_), channel_id=1, source_target_pairs={{0,1},{1,0},{2,3},{3,2},{4,5},{5,4},{6,7},{7,6},{8,9},{9,8},{10,11... | collective-permute-start | bytes 786440 | tf_op jit(solution)/shard_map/roots/ppermute | solution.py:33
  92.2 1.7 %collective-permute-start.16 = (bf16[1024,128]{1,0:T(8,128)(2,1)S(1)}, bf16[1024,128]{1,0:T(8,128)(2,1)S(1)}, u32[]{:S(2)}, u32[]{:S(2)}) collective-permute-start(bf16[1024,128]{1,0:T(8,128)(2,1)S(1)} %collective-permute-done.15.refs_2_), channel_id=1, source_target_pairs={{0,1},{1,0},{2,3},{3,2},{4,5},{5,4},{6,7},{7,6},{8,9},{9,8},{10,11... | collective-permute-start | bytes 786440 | tf_op jit(solution)/shard_map/roots/ppermute | solution.py:33
  95.3 24.0 %all-to-all-start.3 = ((bf16[32,32,128]{2,1,0:T(8,128)(2,1)}), bf16[32,32,128]{2,1,0:T(8,128)(2,1)S(1)}, u32[]{:S(2)}, u32[]{:S(2)}) async-start(bf16[32,32,128]{2,1,0:T(8,128)(2,1)} %precondition.2), calls=%async_computation.3 | async-start | bytes 524288 | tf_op jit(solution)/shard_map/precondition/all_to_all | solution.py:238
  105.9 5.0 %collective-permute-start.21 = (bf16[6,64,128]{2,1,0:T(8,128)(2,1)S(1)}, bf16[6,64,128]{2,1,0:T(8,128)(2,1)S(1)}, u32[]{:S(2)}, u32[]{:S(2)}) collective-permute-start(bf16[6,64,128]{2,1,0:T(8,128)(2,1)S(1)} %get-tuple-element.103), channel_id=1, source_target_pairs={{0,1},{1,0},{2,3},{3,2},{4,5},{5,4},{6,7},{7,6},{8,9},{9,8},{10,11... | collective-permute-start | bytes 294920 | tf_op jit(solution)/shard_map/precondition/ppermute | solution.py:33
  106.5 6.3 %collective-permute-start.22 = (bf16[6,64,128]{2,1,0:T(8,128)(2,1)S(1)}, bf16[6,64,128]{2,1,0:T(8,128)(2,1)S(1)}, u32[]{:S(2)}, u32[]{:S(2)}) collective-permute-start(bf16[6,64,128]{2,1,0:T(8,128)(2,1)S(1)} %get-tuple-element.104), channel_id=1, source_target_pairs={{0,2},{1,3},{2,4},{3,5},{4,6},{5,7},{6,0},{7,1},{8,10},{9,11},{10,... | collective-permute-start | bytes 294920 | tf_op jit(solution)/shard_map/precondition/ppermute | solution.py:33
  106.5 12.0 %collective-permute-start.23 = (bf16[6,64,128]{2,1,0:T(8,128)(2,1)S(1)}, bf16[6,64,128]{2,1,0:T(8,128)(2,1)S(1)}, u32[]{:S(2)}, u32[]{:S(2)}) collective-permute-start(bf16[6,64,128]{2,1,0:T(8,128)(2,1)S(1)} %get-tuple-element.105), channel_id=1, source_target_pairs={{0,3},{1,2},{2,5},{3,4},{4,7},{5,6},{6,1},{7,0},{8,11},{9,10},{10,... | collective-permute-start | bytes 294920 | tf_op jit(solution)/shard_map/precondition/ppermute | solution.py:33
  107.5 11.1 %collective-permute-start.24 = (bf16[6,64,128]{2,1,0:T(8,128)(2,1)S(1)}, bf16[6,64,128]{2,1,0:T(8,128)(2,1)S(1)}, u32[]{:S(2)}, u32[]{:S(2)}) collective-permute-start(bf16[6,64,128]{2,1,0:T(8,128)(2,1)S(1)} %get-tuple-element.106), channel_id=1, source_target_pairs={{0,4},{1,5},{2,6},{3,7},{4,0},{5,1},{6,2},{7,3},{8,12},{9,13},{10,... | collective-permute-start | bytes 294920 | tf_op jit(solution)/shard_map/precondition/ppermute | solution.py:33
  110.6 8.0 %collective-permute-start.25 = (bf16[6,64,128]{2,1,0:T(8,128)(2,1)S(1)}, bf16[6,64,128]{2,1,0:T(8,128)(2,1)S(1)}, u32[]{:S(2)}, u32[]{:S(2)}) collective-permute-start(bf16[6,64,128]{2,1,0:T(8,128)(2,1)S(1)} %get-tuple-element.107), channel_id=1, source_target_pairs={{0,5},{1,4},{2,7},{3,6},{4,1},{5,0},{6,3},{7,2},{8,13},{9,12},{10,... | collective-permute-start | bytes 294920 | tf_op jit(solution)/shard_map/precondition/ppermute | solution.py:33
  110.8 11.9 %copy-start.4 = (bf16[6,64,128]{2,1,0:T(8,128)(2,1)}, bf16[6,64,128]{2,1,0:T(8,128)(2,1)S(1)}, u32[]{:S(2)}) copy-start(bf16[6,64,128]{2,1,0:T(8,128)(2,1)S(1)} %collective-permute-done.21.refs_1_) | copy-start | bytes 294916
  110.8 7.8 %collective-permute-start.26 = (bf16[6,64,128]{2,1,0:T(8,128)(2,1)S(1)}, bf16[6,64,128]{2,1,0:T(8,128)(2,1)S(1)}, u32[]{:S(2)}, u32[]{:S(2)}) collective-permute-start(bf16[6,64,128]{2,1,0:T(8,128)(2,1)S(1)} %get-tuple-element.108), channel_id=1, source_target_pairs={{0,6},{1,7},{2,0},{3,1},{4,2},{5,3},{6,4},{7,5},{8,14},{9,15},{10,... | collective-permute-start | bytes 294920 | tf_op jit(solution)/shard_map/precondition/ppermute | solution.py:33
  112.8 10.0 %copy-start.5 = (bf16[6,64,128]{2,1,0:T(8,128)(2,1)}, bf16[6,64,128]{2,1,0:T(8,128)(2,1)S(1)}, u32[]{:S(2)}) copy-start(bf16[6,64,128]{2,1,0:T(8,128)(2,1)S(1)} %collective-permute-done.22.refs_2_) | copy-start | bytes 294916
  112.8 6.5 %collective-permute-start.27 = (bf16[6,64,128]{2,1,0:T(8,128)(2,1)S(1)}, bf16[6,64,128]{2,1,0:T(8,128)(2,1)S(1)}, u32[]{:S(2)}, u32[]{:S(2)}) collective-permute-start(bf16[6,64,128]{2,1,0:T(8,128)(2,1)S(1)} %get-tuple-element.109), channel_id=1, source_target_pairs={{0,7},{1,6},{2,1},{3,0},{4,3},{5,2},{6,5},{7,4},{8,15},{9,14},{10,... | collective-permute-start | bytes 294920 | tf_op jit(solution)/shard_map/precondition/ppermute | solution.py:33
  118.6 4.2 %copy-start.6 = (bf16[6,64,128]{2,1,0:T(8,128)(2,1)}, bf16[6,64,128]{2,1,0:T(8,128)(2,1)S(1)}, u32[]{:S(2)}) copy-start(bf16[6,64,128]{2,1,0:T(8,128)(2,1)S(1)} %collective-permute-done.23.refs_3_) | copy-start | bytes 294916
  118.6 4.2 %copy-start.7 = (bf16[6,64,128]{2,1,0:T(8,128)(2,1)}, bf16[6,64,128]{2,1,0:T(8,128)(2,1)S(1)}, u32[]{:S(2)}) copy-start(bf16[6,64,128]{2,1,0:T(8,128)(2,1)S(1)} %collective-permute-done.24.refs_4_) | copy-start | bytes 294916
  118.6 4.2 %copy-start.8 = (bf16[6,64,128]{2,1,0:T(8,128)(2,1)}, bf16[6,64,128]{2,1,0:T(8,128)(2,1)S(1)}, u32[]{:S(2)}) copy-start(bf16[6,64,128]{2,1,0:T(8,128)(2,1)S(1)} %collective-permute-done.25.refs_5_) | copy-start | bytes 294916
  118.6 4.2 %copy-start.9 = (bf16[6,64,128]{2,1,0:T(8,128)(2,1)}, bf16[6,64,128]{2,1,0:T(8,128)(2,1)S(1)}, u32[]{:S(2)}) copy-start(bf16[6,64,128]{2,1,0:T(8,128)(2,1)S(1)} %collective-permute-done.26.refs_6_) | copy-start | bytes 294916
  119.3 3.5 %copy-start.10 = (bf16[6,64,128]{2,1,0:T(8,128)(2,1)}, bf16[6,64,128]{2,1,0:T(8,128)(2,1)S(1)}, u32[]{:S(2)}) copy-start(bf16[6,64,128]{2,1,0:T(8,128)(2,1)S(1)} %collective-permute-done.27.refs_7_) | copy-start | bytes 294916
  119.3 8.2 %collective-permute-start.33 = (bf16[32,32,128]{2,1,0:T(8,128)(2,1)S(1)}, bf16[32,32,128]{2,1,0:T(8,128)(2,1)S(1)}, u32[]{:S(2)}, u32[]{:S(2)}) collective-permute-start(bf16[32,32,128]{2,1,0:T(8,128)(2,1)S(1)} %all-to-all-done.3.refs_0_), channel_id=1, source_target_pairs={{0,6},{1,7},{2,0},{3,1},{4,2},{5,3},{6,4},{7,5},{8,14},{9,15},{10,... | collective-permute-start | bytes 786440 | tf_op jit(solution)/shard_map/precondition/ppermute | solution.py:33
  121.8 12.2 %collective-permute-start.31 = (bf16[32,32,128]{2,1,0:T(8,128)(2,1)S(1)}, bf16[32,32,128]{2,1,0:T(8,128)(2,1)S(1)}, u32[]{:S(2)}, u32[]{:S(2)}) collective-permute-start(bf16[32,32,128]{2,1,0:T(8,128)(2,1)S(1)} %all-to-all-done.3.refs_0_), channel_id=1, source_target_pairs={{0,4},{1,5},{2,6},{3,7},{4,0},{5,1},{6,2},{7,3},{8,12},{9,13},{10,... | collective-permute-start | bytes 786440 | tf_op jit(solution)/shard_map/precondition/ppermute | solution.py:33
  122.8 14.4 %collective-permute-start.29 = (bf16[32,32,128]{2,1,0:T(8,128)(2,1)S(1)}, bf16[32,32,128]{2,1,0:T(8,128)(2,1)S(1)}, u32[]{:S(2)}, u32[]{:S(2)}) collective-permute-start(bf16[32,32,128]{2,1,0:T(8,128)(2,1)S(1)} %all-to-all-done.3.refs_0_), channel_id=1, source_target_pairs={{0,2},{1,3},{2,4},{3,5},{4,6},{5,7},{6,0},{7,1},{8,10},{9,11},{10,... | collective-permute-start | bytes 786440 | tf_op jit(solution)/shard_map/precondition/ppermute | solution.py:33
  126.5 11.2 %collective-permute-start.28 = (bf16[32,32,128]{2,1,0:T(8,128)(2,1)S(1)}, bf16[32,32,128]{2,1,0:T(8,128)(2,1)S(1)}, u32[]{:S(2)}, u32[]{:S(2)}) collective-permute-start(bf16[32,32,128]{2,1,0:T(8,128)(2,1)S(1)} %all-to-all-done.3.refs_0_), channel_id=1, source_target_pairs={{0,1},{1,0},{2,3},{3,2},{4,5},{5,4},{6,7},{7,6},{8,9},{9,8},{10,11... | collective-permute-start | bytes 786440 | tf_op jit(solution)/shard_map/precondition/ppermute | solution.py:33
  127.5 10.2 %collective-permute-start.34 = (bf16[32,32,128]{2,1,0:T(8,128)(2,1)S(1)}, bf16[32,32,128]{2,1,0:T(8,128)(2,1)S(1)}, u32[]{:S(2)}, u32[]{:S(2)}) collective-permute-start(bf16[32,32,128]{2,1,0:T(8,128)(2,1)S(1)} %collective-permute-done.33.refs_6_), channel_id=1, source_target_pairs={{0,1},{1,0},{2,3},{3,2},{4,5},{5,4},{6,7},{7,6},{8,9},{9,8},{10,11... | collective-permute-start | bytes 786440 | tf_op jit(solution)/shard_map/precondition/ppermute | solution.py:33
  134.0 3.7 %collective-permute-start.32 = (bf16[32,32,128]{2,1,0:T(8,128)(2,1)S(1)}, bf16[32,32,128]{2,1,0:T(8,128)(2,1)S(1)}, u32[]{:S(2)}, u32[]{:S(2)}) collective-permute-start(bf16[32,32,128]{2,1,0:T(8,128)(2,1)S(1)} %collective-permute-done.31.refs_4_), channel_id=1, source_target_pairs={{0,1},{1,0},{2,3},{3,2},{4,5},{5,4},{6,7},{7,6},{8,9},{9,8},{10,11... | collective-permute-start | bytes 786440 | tf_op jit(solution)/shard_map/precondition/ppermute | solution.py:33
  137.2 1.7 %collective-permute-start.30 = (bf16[32,32,128]{2,1,0:T(8,128)(2,1)S(1)}, bf16[32,32,128]{2,1,0:T(8,128)(2,1)S(1)}, u32[]{:S(2)}, u32[]{:S(2)}) collective-permute-start(bf16[32,32,128]{2,1,0:T(8,128)(2,1)S(1)} %collective-permute-done.29.refs_2_), channel_id=1, source_target_pairs={{0,1},{1,0},{2,3},{3,2},{4,5},{5,4},{6,7},{7,6},{8,9},{9,8},{10,11... | collective-permute-start | bytes 786440 | tf_op jit(solution)/shard_map/precondition/ppermute | solution.py:33
  (2 other events, 1.2 us)

commit v5 on v4

--- a/solution.py
+++ b/solution.py
@@ -35,6 +35,15 @@
 
 def exchange(pieces):
     return [p if j == 0 else send(p, *PARTNERS[j]) for j, p in enumerate(pieces)]
+
+
+def outgoing(refs):
+    own, given, *pairs = refs
+    return [own, given] + [pair.at[o] for pair in pairs for o in range(2)]
+
+
+def incoming(refs):
+    return list(refs[:2]) + [ref.at[j % 2] for j, ref in enumerate(refs[2:])]
 
 
 def gather(piece, own=None):
@@ -83,8 +92,12 @@
         for copy in pair:
             copy.start()
     mine = pl.ds(pl.multiple_of(worker * PART, PART), PART)
-    copy_columns = pltpu.make_async_copy(grads.at[:, :, mine], columns, cut)
-    copy_columns.start()
+    column_copies = [
+        pltpu.make_async_copy(grads.at[4 * i : 4 * i + 4, :, mine], columns.at[4 * i : 4 * i + 4], cut.at[i])
+        for i in range(NB // 4)
+    ]
+    for copy in column_copies:
+        copy.start()
     for i in range(NW * CAP):
         holder[i] = -1
     for i in range(NW):
@@ -122,7 +135,8 @@
     diag_tile = jnp.concatenate(diag_rows + [jnp.zeros((16 - CAP, PART), f32)], axis=0).astype(bf16)
     for out in outs:
         out[2 * CAP * ROWS :, :] = diag_tile
-    copy_columns.wait()
+    for copy in column_copies:
+        copy.wait()
 
 
 def pick_roots(holder, *refs):
@@ -184,13 +198,13 @@
 
 def pack_grams(holder, grams, *outs):
     worker = lax.axis_index("worker")
-    for out, to in zip(outs, dests(worker)):
+    for out, to in zip(outgoing(outs), dests(worker)):
         for c in range(CAP):
             out[c] = grams[jnp.maximum(holder[to * CAP + c], 0)]
 
 
 def update(holder, left, right, *refs):
-    pieces, outs, held, sems, out_sems = refs[:NW], refs[NW : NW + 2], *refs[NW + 2 :]
+    pieces, outs, held, sems, out_sems = incoming(refs[:NW]), refs[NW : NW + 2], *refs[NW + 2 :]
     worker = lax.axis_index("worker")
     into = [
         [pltpu.make_async_copy(far.at[c], held.at[n, c], sems.at[n, c]) for c in range(CAP)]
@@ -252,7 +266,7 @@
                 pltpu.VMEM((CAP, ROWS, BS), f32),
                 pltpu.SMEM((NW,), jnp.int32),
                 pltpu.SemaphoreType.DMA((2, CAP)),
-                pltpu.SemaphoreType.DMA,
+                pltpu.SemaphoreType.DMA((NB // 4,)),
             ],
             vmem=61,
         )
@@ -265,8 +279,9 @@
             shape((NB, 2 * ROWS + HALF, PART)),
             (holder, *packed),
             [SMEM] + [VMEM] * NW,
-        )
-        roots, columns = lax.optimization_barrier((over_shard(roots), columns))
+            vmem=61,
+        )
+        roots = over_shard(roots)
         root_l = gather(roots[:, :ROWS].reshape(BS, PART))
     with jax.named_scope("grams"):
         grams, image = call(
@@ -278,7 +293,7 @@
         grams, root_l = lax.optimization_barrier((over_shard(grams), root_l))
         packed = call(
             pack_grams,
-            [shape((CAP, 2 * ROWS, PART))] * NW,
+            [shape((CAP, 2 * ROWS, PART))] * 2 + [shape((2, CAP, 2 * ROWS, PART))] * 3,
             (holder, grams),
             [SMEM, VMEM],
         )
@@ -289,7 +304,12 @@
             (roots, image, *root_l),
             flops=2 * BS * BS * PART,
         )
-        result, packed = lax.optimization_barrier((over_shard(result), exchange(packed)))
+        own, given, *pairs = packed
+        pairs = [send(pair, k, 0) for k, pair in enumerate(pairs, 1)]
+        result, pairs, given = lax.optimization_barrier((over_shard(result), pairs, given))
+        packed = [own, send(given, 0, 1)]
+        for pair in pairs:
+            packed += [pair, send(pair, 0, 1)]
     with jax.named_scope("factors"):
         factor = shape((CAP, ROWS, BS), f32)
         new_left, new_right = call(

time: 141 us -> 140 us (level)
  starting transfers between devices: 90.8 us -> 85.1 us
  waiting for transfers between devices: 31.3 us -> 35.8 us
    ppermute x35, starting transfers between devices: 50.8 us -> 45.1 us  [send(): lax.ppermute(value, 'worker', [(w, partner(w, k, other)) for w in range(N...]
    ppermute x35, waiting for transfers between devices: 31.3 us -> 35.8 us  [send(): lax.ppermute(value, 'worker', [(w, partner(w, k, other)) for w in range(N...]
  transfers between devices with their start and end apart: 39 -> 39, of which waited for: 14 -> 17; matrix products, arithmetic and copies ran while one was open for 0% -> 0% of each run, Pallas kernels for 3% -> 3%
where the time goes in v5:
time: 140 us
  starting transfers between devices  85.1 us (61%)
  waiting for transfers between devices  35.8 us (26%)
  Pallas kernels  16 us (11%)
  local copies, waits for them, and re-layouts  1.93 us (1%)
    ppermute x35, starting transfers between devices, send(): lax.ppermute(value, 'worker', [(w, partner(w, k, other)) for w in range(N...  45.1 us
    all_to_all x4, starting transfers between devices, over_shard(): return lax.all_to_all(value, 'shard', 0, 0, tiled=True)  40 us
    ppermute x35, waiting for transfers between devices, send(): lax.ppermute(value, 'worker', [(w, partner(w, k, other)) for w in range(N...  35.8 us
    pallas_call x7, Pallas kernels, call(): pl.pallas_call(kernel, out_shape=outs, in_specs=in_specs or [VMEM] * len(...  16 us
  transfers between devices with their start and end apart: 39, of which 17 were waited for; matrix products, arithmetic and copies ran while one was open for 0% of the time, Pallas kernels for 3%

profile of v5, /device:TPU:1, one launch (start us, length us, event | category | flops | bytes accessed | tf_op | source)
XLA Modules:
  0.0 139.9 jit_solution(15502462444679178421)
XLA Ops:
  0.6 3.6 %roots.2 = (bf16[400,128]{1,0:T(8,128)(2,1)}, bf16[400,128]{1,0:T(8,128)(2,1)}, bf16[400,128]{1,0:T(8,128)(2,1)}, bf16[400,128]{1,0:T(8,128)(2,1)}, bf16[400,128...) custom-call(s32[32]{0:T(128)} %bitcast.23, ...), custom_call_target="tpu_custom_call" | custom-call | bytes 2097152 | tf_op jit(solution)/shard_map/roots/pallas_call | solution.py:66
  4.2 12.0 %all-to-all-start = ((bf16[32,32,128]{2,1,0:T(8,128)(2,1)}), bf16[32,32,128]{2,1,0:T(8,128)(2,1)S(1)}, u32[]{:S(2)}, u32[]{:S(2)}) async-start(bf16[32,32,128]{2,1,0:T(8,128)(2,1)} %get-tuple-element.48), calls=%async_computation | async-start | bytes 524288 | tf_op jit(solution)/shard_map/roots/all_to_all | solution.py:252
  16.2 1.0 collective-permute-start
  17.3 1.2 collective-permute-start.1
  18.5 1.5 %collective-permute-start.2 = (bf16[400,128]{1,0:T(8,128)(2,1)}, bf16[400,128]{1,0:T(8,128)(2,1)S(1)}, u32[]{:S(2)}, u32[]{:S(2)}) collective-permute-start(bf16[400,128]{1,0:T(8,128)(2,1)} %get-tuple-element.52), channel_id=1, source_target_pairs={{0,3},{1,2},{2,5},{3,4},{4,7},{5,6},{6,1},{7,0},{8,11},{9,10},{10,... | collective-permute-start | bytes 307208 | tf_op jit(solution)/shard_map/roots/ppermute | solution.py:33
  20.0 1.4 %collective-permute-start.3 = (bf16[400,128]{1,0:T(8,128)(2,1)}, bf16[400,128]{1,0:T(8,128)(2,1)S(1)}, u32[]{:S(2)}, u32[]{:S(2)}) collective-permute-start(bf16[400,128]{1,0:T(8,128)(2,1)} %get-tuple-element.53), channel_id=1, source_target_pairs={{0,4},{1,5},{2,6},{3,7},{4,0},{5,1},{6,2},{7,3},{8,12},{9,13},{10,... | collective-permute-start | bytes 307208 | tf_op jit(solution)/shard_map/roots/ppermute | solution.py:33
  21.4 1.9 %collective-permute-start.4 = (bf16[400,128]{1,0:T(8,128)(2,1)}, bf16[400,128]{1,0:T(8,128)(2,1)S(1)}, u32[]{:S(2)}, u32[]{:S(2)}) collective-permute-start(bf16[400,128]{1,0:T(8,128)(2,1)} %get-tuple-element.54), channel_id=1, source_target_pairs={{0,5},{1,4},{2,7},{3,6},{4,1},{5,0},{6,3},{7,2},{8,13},{9,12},{10,... | collective-permute-start | bytes 307208 | tf_op jit(solution)/shard_map/roots/ppermute | solution.py:33
  23.3 1.5 %collective-permute-start.5 = (bf16[400,128]{1,0:T(8,128)(2,1)}, bf16[400,128]{1,0:T(8,128)(2,1)S(1)}, u32[]{:S(2)}, u32[]{:S(2)}) collective-permute-start(bf16[400,128]{1,0:T(8,128)(2,1)} %get-tuple-element.55), channel_id=1, source_target_pairs={{0,6},{1,7},{2,0},{3,1},{4,2},{5,3},{6,4},{7,5},{8,14},{9,15},{10,... | collective-permute-start | bytes 307208 | tf_op jit(solution)/shard_map/roots/ppermute | solution.py:33
  24.7 0.9 collective-permute-start.6
  25.8 2.7 %collective-permute-done.3.refs_4_ = bf16[400,128]{1,0:T(8,128)(2,1)S(1)} collective-permute-done((bf16[400,128]{1,0:T(8,128)(2,1)}, bf16[400,128]{1,0:T(8,128)(2,1)S(1)}, u32[]{:S(2)}, u32[]{:S(2)}) %collective-permute-start.3) | collective-permute-done | bytes 102432 | tf_op jit(solution)/shard_map/roots/ppermute | solution.py:33
  28.5 2.4 %collective-permute-done.4.refs_5_ = bf16[400,128]{1,0:T(8,128)(2,1)S(1)} collective-permute-done((bf16[400,128]{1,0:T(8,128)(2,1)}, bf16[400,128]{1,0:T(8,128)(2,1)S(1)}, u32[]{:S(2)}, u32[]{:S(2)}) %collective-permute-start.4) | collective-permute-done | bytes 102432 | tf_op jit(solution)/shard_map/roots/ppermute | solution.py:33
  30.9 1.1 collective-permute-done.6.refs_7_
  32.7 2.5 %roots.3 = bf16[32,80,128]{2,1,0:T(8,128)(2,1)} custom-call(s32[48]{0:T(128)} %get-tuple-element.47.holder, bf16[400,128]{1,0:T(8,128)(2,1)} %get-tuple-element.57.refs_0_, bf16[400,128]{1,0:T(8,128)(2,1)} %copy-done.8, bf16[400,128]{1,0:T(8,128)(2,1)} %copy-done.9, bf16[400,128]{1,0:T(8,128)(2,1)} %copy-done.10, bf16[400,128]{1,0:T(8,128)(2,1)} %copy-done.11, ...), custom_call_target="tpu_custom_call" | custom-call | bytes 2097152 | tf_op jit(solution)/shard_map/roots/pallas_call | solution.py:66
  35.2 9.5 %all-to-all-start.1 = ((bf16[32,80,128]{2,1,0:T(8,128)(2,1)}), bf16[32,80,128]{2,1,0:T(8,128)(2,1)S(1)}, u32[]{:S(2)}, u32[]{:S(2)}) async-start(bf16[32,80,128]{2,1,0:T(8,128)(2,1)} %roots.3), calls=%async_computation.1 | async-start | bytes 1310720 | tf_op jit(solution)/shard_map/roots/all_to_all | solution.py:252
  44.7 2.7 %collective-permute-start.12 = (bf16[1024,128]{1,0:T(8,128)(2,1)S(1)}, bf16[1024,128]{1,0:T(8,128)(2,1)S(1)}, u32[]{:S(2)}, u32[]{:S(2)}) collective-permute-start(bf16[1024,128]{1,0:T(8,128)(2,1)S(1)} %bitcast.14), channel_id=1, source_target_pairs={{0,6},{1,7},{2,0},{3,1},{4,2},{5,3},{6,4},{7,5},{8,14},{9,15},{10,... | collective-permute-start | bytes 786440 | tf_op jit(solution)/shard_map/gradients/ppermute | solution.py:33
  47.3 1.2 collective-permute-start.10
  48.6 1.2 collective-permute-start.7
  49.8 3.0 %collective-permute-done.12.refs_6_ = bf16[1024,128]{1,0:T(8,128)(2,1)S(1)} collective-permute-done((bf16[1024,128]{1,0:T(8,128)(2,1)S(1)}, bf16[1024,128]{1,0:T(8,128)(2,1)S(1)}, u32[]{:S(2)}, u32[]{:S(2)}) %collective-permute-start.12) | collective-permute-done | bytes 262176 | tf_op jit(solution)/shard_map/gradients/ppermute | solution.py:33
  52.8 6.7 %collective-permute-start.13 = (bf16[1024,128]{1,0:T(8,128)(2,1)S(1)}, bf16[1024,128]{1,0:T(8,128)(2,1)S(1)}, u32[]{:S(2)}, u32[]{:S(2)}) collective-permute-start(bf16[1024,128]{1,0:T(8,128)(2,1)S(1)} %collective-permute-done.12.refs_6_), channel_id=1, source_target_pairs={{0,1},{1,0},{2,3},{3,2},{4,5},{5,4},{6,7},{7,6},{8,9},{9,8},{10,11... | collective-permute-start | bytes 786440 | tf_op jit(solution)/shard_map/gradients/ppermute | solution.py:33
  59.5 3.2 %collective-permute-done.8.refs_2_ = bf16[1024,128]{1,0:T(8,128)(2,1)S(1)} collective-permute-done((bf16[1024,128]{1,0:T(8,128)(2,1)S(1)}, bf16[1024,128]{1,0:T(8,128)(2,1)S(1)}, u32[]{:S(2)}, u32[]{:S(2)}) %collective-permute-start.8) | collective-permute-done | bytes 262176 | tf_op jit(solution)/shard_map/gradients/ppermute | solution.py:33
  63.2 1.1 collective-permute-done.9.refs_3_
  64.3 2.6 %grams.2 = (bf16[32,64,128]{2,1,0:T(8,128)(2,1)}, bf16[1024,128]{1,0:T(8,128)(2,1)S(1)}) custom-call(bf16[32,80,128]{2,1,0:T(8,128)(2,1)S(1)} %all-to-all-done.1.roots, bf16[1024,128]{1,0:T(8,128)(2,1)S(1)} %bitcast.18, bf16[1024,128]{1,0:T(8,128)(2,1)S(1)} %collective-permute-done.7.refs_1_, bf16[1024,128]{1,0:T(8,128)(2,1)S(1)} %collective-permute-done.8.refs_2_, ...), custom_call_target="tpu_custom_call" | custom-call | flops 805306368 | bytes 2097152 | tf_op jit(solution)/shard_map/grams/pallas_call | solution.py:66
  67.0 9.2 %all-to-all-start.2 = ((bf16[32,64,128]{2,1,0:T(8,128)(2,1)}), bf16[32,64,128]{2,1,0:T(8,128)(2,1)S(1)}, u32[]{:S(2)}, u32[]{:S(2)}) async-start(bf16[32,64,128]{2,1,0:T(8,128)(2,1)} %get-tuple-element.67), calls=%async_computation.2 | async-start | bytes 1048576 | tf_op jit(solution)/shard_map/grams/all_to_all | solution.py:252
  76.8 1.1 collective-permute-start.17
  78.4 1.5 %collective-permute-start.14 = (bf16[1024,128]{1,0:T(8,128)(2,1)S(1)}, bf16[1024,128]{1,0:T(8,128)(2,1)S(1)}, u32[]{:S(2)}, u32[]{:S(2)}) collective-permute-start(bf16[1024,128]{1,0:T(8,128)(2,1)S(1)} %bitcast.12), channel_id=1, source_target_pairs={{0,1},{1,0},{2,3},{3,2},{4,5},{5,4},{6,7},{7,6},{8,9},{9,8},{10,11... | collective-permute-start | bytes 786440 | tf_op jit(solution)/shard_map/roots/ppermute | solution.py:33
  79.9 3.6 %collective-permute-done.19.refs_6_ = bf16[1024,128]{1,0:T(8,128)(2,1)S(1)} collective-permute-done((bf16[1024,128]{1,0:T(8,128)(2,1)S(1)}, bf16[1024,128]{1,0:T(8,128)(2,1)S(1)}, u32[]{:S(2)}, u32[]{:S(2)}) %collective-permute-start.19) | collective-permute-done | bytes 262176 | tf_op jit(solution)/shard_map/roots/ppermute | solution.py:33
  83.5 2.6 %collective-permute-start.20 = (bf16[1024,128]{1,0:T(8,128)(2,1)S(1)}, bf16[1024,128]{1,0:T(8,128)(2,1)S(1)}, u32[]{:S(2)}, u32[]{:S(2)}) collective-permute-start(bf16[1024,128]{1,0:T(8,128)(2,1)S(1)} %collective-permute-done.19.refs_6_), channel_id=1, source_target_pairs={{0,1},{1,0},{2,3},{3,2},{4,5},{5,4},{6,7},{7,6},{8,9},{9,8},{10,11... | collective-permute-start | bytes 786440 | tf_op jit(solution)/shard_map/roots/ppermute | solution.py:33
  86.2 2.3 %collective-permute-start.18 = (bf16[1024,128]{1,0:T(8,128)(2,1)S(1)}, bf16[1024,128]{1,0:T(8,128)(2,1)S(1)}, u32[]{:S(2)}, u32[]{:S(2)}) collective-permute-start(bf16[1024,128]{1,0:T(8,128)(2,1)S(1)} %collective-permute-done.17.refs_4_), channel_id=1, source_target_pairs={{0,1},{1,0},{2,3},{3,2},{4,5},{5,4},{6,7},{7,6},{8,9},{9,8},{10,11... | collective-permute-start | bytes 786440 | tf_op jit(solution)/shard_map/roots/ppermute | solution.py:33
  88.5 3.6 %collective-permute-done.15.refs_2_ = bf16[1024,128]{1,0:T(8,128)(2,1)S(1)} collective-permute-done((bf16[1024,128]{1,0:T(8,128)(2,1)S(1)}, bf16[1024,128]{1,0:T(8,128)(2,1)S(1)}, u32[]{:S(2)}, u32[]{:S(2)}) %collective-permute-start.15) | collective-permute-done | bytes 262176 | tf_op jit(solution)/shard_map/roots/ppermute | solution.py:33
  92.6 1.1 collective-permute-done.16.refs_3_
  93.8 1.5 %precondition.2 = bf16[32,32,128]{2,1,0:T(8,128)(2,1)} custom-call(bf16[32,80,128]{2,1,0:T(8,128)(2,1)S(1)} %all-to-all-done.1.roots, bf16[1024,128]{1,0:T(8,128)(2,1)S(1)} %get-tuple-element.66.image, bf16[1024,128]{1,0:T(8,128)(2,1)S(1)} %bitcast.13, bf16[1024,128]{1,0:T(8,128)(2,1)S(1)} %collective-permute-done.14.refs_1_, ...), custom_call_target="tpu_custom_call" | custom-call | flops 268435456 | bytes 2097152 | tf_op jit(solution)/shard_map/precondition/pallas_call | solution.py:66
  95.3 9.2 %all-to-all-start.3 = ((bf16[32,32,128]{2,1,0:T(8,128)(2,1)}), bf16[32,32,128]{2,1,0:T(8,128)(2,1)S(1)}, u32[]{:S(2)}, u32[]{:S(2)}) async-start(bf16[32,32,128]{2,1,0:T(8,128)(2,1)} %precondition.2), calls=%async_computation.3 | async-start | bytes 524288 | tf_op jit(solution)/shard_map/precondition/all_to_all | solution.py:252
  104.5 0.7 grams.3
  105.8 2.0 %collective-permute-start.22 = (bf16[2,6,64,128]{3,2,1,0:T(8,128)(2,1)S(1)}, bf16[2,6,64,128]{3,2,1,0:T(8,128)(2,1)S(1)}, u32[]{:S(2)}, u32[]{:S(2)}) collective-permute-start(bf16[2,6,64,128]{3,2,1,0:T(8,128)(2,1)S(1)} %get-tuple-element.78), channel_id=1, source_target_pairs={{0,4},{1,5},{2,6},{3,7},{4,0},{5,1},{6,2},{7,3},{8,12},{9,13},{10,... | collective-permute-start | bytes 589832 | tf_op jit(solution)/shard_map/precondition/ppermute | solution.py:33
  107.8 1.2 collective-permute-start.23
  109.0 4.5 %collective-permute-done.21.refs_2_ = bf16[2,6,64,128]{3,2,1,0:T(8,128)(2,1)S(1)} collective-permute-done((bf16[2,6,64,128]{3,2,1,0:T(8,128)(2,1)S(1)}, bf16[2,6,64,128]{3,2,1,0:T(8,128)(2,1)S(1)}, u32[]{:S(2)}, u32[]{:S(2)}) %collective-permute-start.21) | collective-permute-done | bytes 196640 | tf_op jit(solution)/shard_map/precondition/ppermute | solution.py:33
  113.5 2.9 %collective-permute-done.22.refs_4_ = bf16[2,6,64,128]{3,2,1,0:T(8,128)(2,1)S(1)} collective-permute-done((bf16[2,6,64,128]{3,2,1,0:T(8,128)(2,1)S(1)}, bf16[2,6,64,128]{3,2,1,0:T(8,128)(2,1)S(1)}, u32[]{:S(2)}, u32[]{:S(2)}) %collective-permute-start.22) | collective-permute-done | bytes 196640 | tf_op jit(solution)/shard_map/precondition/ppermute | solution.py:33
  116.4 1.2 collective-permute-done.23.refs_6_
  117.6 1.6 %collective-permute-start.25 = (bf16[2,6,64,128]{3,2,1,0:T(8,128)(2,1)S(1)}, bf16[2,6,64,128]{3,2,1,0:T(8,128)(2,1)S(1)}, u32[]{:S(2)}, u32[]{:S(2)}) collective-permute-start(bf16[2,6,64,128]{3,2,1,0:T(8,128)(2,1)S(1)} %collective-permute-done.21.refs_2_), channel_id=1, source_target_pairs={{0,1},{1,0},{2,3},{3,2},{4,5},{5,4},{6,7},{7,6},{8,9},{9,8},{10,11... | collective-permute-start | bytes 589832 | tf_op jit(solution)/shard_map/precondition/ppermute | solution.py:33
  119.3 2.3 %collective-permute-start.33 = (bf16[32,32,128]{2,1,0:T(8,128)(2,1)S(1)}, bf16[32,32,128]{2,1,0:T(8,128)(2,1)S(1)}, u32[]{:S(2)}, u32[]{:S(2)}) collective-permute-start(bf16[32,32,128]{2,1,0:T(8,128)(2,1)S(1)} %all-to-all-done.3.refs_0_), channel_id=1, source_target_pairs={{0,6},{1,7},{2,0},{3,1},{4,2},{5,3},{6,4},{7,5},{8,14},{9,15},{10,... | collective-permute-start | bytes 786440 | tf_op jit(solution)/shard_map/precondition/ppermute | solution.py:33
  122.2 1.0 collective-permute-start.26
  123.3 1.0 collective-permute-done.26.refs_5_
  125.3 3.8 %factors.1 = (f32[6,32,1024]{2,1,0:T(8,128)}, f32[6,32,1024]{2,1,0:T(8,128)}) custom-call(s32[48]{0:T(128)} %get-tuple-element.47.holder, f32[6,32,1024]{2,1,0:T(8,128)} %bitcast.19, f32[6,32,1024]{2,1,0:T(8,128)} %bitcast.20, bf16[6,64,128]{2,1,0:T(8,128)(2,1)} %copy-done, bf16[6,64,128]{2,1,0:T(8,128)(2,1)} %copy-done.15, ...), custom_call_target="tpu_custom_call" | custom-call | bytes 20971520 | tf_op jit(solution)/shard_map/factors/pallas_call | solution.py:66
  129.5 4.3 %collective-permute-start.34 = (bf16[32,32,128]{2,1,0:T(8,128)(2,1)S(1)}, bf16[32,32,128]{2,1,0:T(8,128)(2,1)S(1)}, u32[]{:S(2)}, u32[]{:S(2)}) collective-permute-start(bf16[32,32,128]{2,1,0:T(8,128)(2,1)S(1)} %collective-permute-done.33.refs_6_), channel_id=1, source_target_pairs={{0,1},{1,0},{2,3},{3,2},{4,5},{5,4},{6,7},{7,6},{8,9},{9,8},{10,11... | collective-permute-start | bytes 786440 | tf_op jit(solution)/shard_map/precondition/ppermute | solution.py:33
  133.8 2.5 %collective-permute-done.29.refs_2_ = bf16[32,32,128]{2,1,0:T(8,128)(2,1)S(1)} collective-permute-done((bf16[32,32,128]{2,1,0:T(8,128)(2,1)S(1)}, bf16[32,32,128]{2,1,0:T(8,128)(2,1)S(1)}, u32[]{:S(2)}, u32[]{:S(2)}) %collective-permute-start.29) | collective-permute-done | bytes 262176 | tf_op jit(solution)/shard_map/precondition/ppermute | solution.py:33
  136.3 0.8 collective-permute-start.30
  137.2 1.1 collective-permute-done.30.refs_3_
  138.3 1.4 precondition.3
  (70 shorter events, 5.7 us)
Async XLA Ops:
  4.2 27.8 %all-to-all-start = ((bf16[32,32,128]{2,1,0:T(8,128)(2,1)}), bf16[32,32,128]{2,1,0:T(8,128)(2,1)S(1)}, u32[]{:S(2)}, u32[]{:S(2)}) async-start(bf16[32,32,128]{2,1,0:T(8,128)(2,1)} %get-tuple-element.48), calls=%async_computation | async-start | bytes 524288 | tf_op jit(solution)/shard_map/roots/all_to_all | solution.py:252
  16.2 7.0 %collective-permute-start = (bf16[400,128]{1,0:T(8,128)(2,1)}, bf16[400,128]{1,0:T(8,128)(2,1)S(1)}, u32[]{:S(2)}, u32[]{:S(2)}) collective-permute-start(bf16[400,128]{1,0:T(8,128)(2,1)} %get-tuple-element.50), channel_id=1, source_target_pairs={{0,1},{1,0},{2,3},{3,2},{4,5},{5,4},{6,7},{7,6},{8,9},{9,8},{10,11... | collective-permute-start | bytes 307208 | tf_op jit(solution)/shard_map/roots/ppermute | solution.py:33
  17.3 7.5 %collective-permute-start.1 = (bf16[400,128]{1,0:T(8,128)(2,1)}, bf16[400,128]{1,0:T(8,128)(2,1)S(1)}, u32[]{:S(2)}, u32[]{:S(2)}) collective-permute-start(bf16[400,128]{1,0:T(8,128)(2,1)} %get-tuple-element.51), channel_id=1, source_target_pairs={{0,2},{1,3},{2,4},{3,5},{4,6},{5,7},{6,0},{7,1},{8,10},{9,11},{10,... | collective-permute-start | bytes 307208 | tf_op jit(solution)/shard_map/roots/ppermute | solution.py:33
  18.5 7.3 %collective-permute-start.2 = (bf16[400,128]{1,0:T(8,128)(2,1)}, bf16[400,128]{1,0:T(8,128)(2,1)S(1)}, u32[]{:S(2)}, u32[]{:S(2)}) collective-permute-start(bf16[400,128]{1,0:T(8,128)(2,1)} %get-tuple-element.52), channel_id=1, source_target_pairs={{0,3},{1,2},{2,5},{3,4},{4,7},{5,6},{6,1},{7,0},{8,11},{9,10},{10,... | collective-permute-start | bytes 307208 | tf_op jit(solution)/shard_map/roots/ppermute | solution.py:33
  20.0 8.6 %collective-permute-start.3 = (bf16[400,128]{1,0:T(8,128)(2,1)}, bf16[400,128]{1,0:T(8,128)(2,1)S(1)}, u32[]{:S(2)}, u32[]{:S(2)}) collective-permute-start(bf16[400,128]{1,0:T(8,128)(2,1)} %get-tuple-element.53), channel_id=1, source_target_pairs={{0,4},{1,5},{2,6},{3,7},{4,0},{5,1},{6,2},{7,3},{8,12},{9,13},{10,... | collective-permute-start | bytes 307208 | tf_op jit(solution)/shard_map/roots/ppermute | solution.py:33
  21.4 9.5 %collective-permute-start.4 = (bf16[400,128]{1,0:T(8,128)(2,1)}, bf16[400,128]{1,0:T(8,128)(2,1)S(1)}, u32[]{:S(2)}, u32[]{:S(2)}) collective-permute-start(bf16[400,128]{1,0:T(8,128)(2,1)} %get-tuple-element.54), channel_id=1, source_target_pairs={{0,5},{1,4},{2,7},{3,6},{4,1},{5,0},{6,3},{7,2},{8,13},{9,12},{10,... | collective-permute-start | bytes 307208 | tf_op jit(solution)/shard_map/roots/ppermute | solution.py:33
  23.3 8.7 %copy-start.8 = (bf16[400,128]{1,0:T(8,128)(2,1)}, bf16[400,128]{1,0:T(8,128)(2,1)S(1)}, u32[]{:S(2)}) copy-start(bf16[400,128]{1,0:T(8,128)(2,1)S(1)} %collective-permute-done.refs_1_) | copy-start | bytes 307204
  23.3 7.6 %collective-permute-start.5 = (bf16[400,128]{1,0:T(8,128)(2,1)}, bf16[400,128]{1,0:T(8,128)(2,1)S(1)}, u32[]{:S(2)}, u32[]{:S(2)}) collective-permute-start(bf16[400,128]{1,0:T(8,128)(2,1)} %get-tuple-element.55), channel_id=1, source_target_pairs={{0,6},{1,7},{2,0},{3,1},{4,2},{5,3},{6,4},{7,5},{8,14},{9,15},{10,... | collective-permute-start | bytes 307208 | tf_op jit(solution)/shard_map/roots/ppermute | solution.py:33
  24.7 7.3 %copy-start.9 = (bf16[400,128]{1,0:T(8,128)(2,1)}, bf16[400,128]{1,0:T(8,128)(2,1)S(1)}, u32[]{:S(2)}) copy-start(bf16[400,128]{1,0:T(8,128)(2,1)S(1)} %collective-permute-done.1.refs_2_) | copy-start | bytes 307204
  24.7 7.3 %collective-permute-start.6 = (bf16[400,128]{1,0:T(8,128)(2,1)}, bf16[400,128]{1,0:T(8,128)(2,1)S(1)}, u32[]{:S(2)}, u32[]{:S(2)}) collective-permute-start(bf16[400,128]{1,0:T(8,128)(2,1)} %get-tuple-element.56), channel_id=1, source_target_pairs={{0,7},{1,6},{2,1},{3,0},{4,3},{5,2},{6,5},{7,4},{8,15},{9,14},{10,... | collective-permute-start | bytes 307208 | tf_op jit(solution)/shard_map/roots/ppermute | solution.py:33
  25.8 6.2 %copy-start.10 = (bf16[400,128]{1,0:T(8,128)(2,1)}, bf16[400,128]{1,0:T(8,128)(2,1)S(1)}, u32[]{:S(2)}) copy-start(bf16[400,128]{1,0:T(8,128)(2,1)S(1)} %collective-permute-done.2.refs_3_) | copy-start | bytes 307204
  28.5 3.5 %copy-start.11 = (bf16[400,128]{1,0:T(8,128)(2,1)}, bf16[400,128]{1,0:T(8,128)(2,1)S(1)}, u32[]{:S(2)}) copy-start(bf16[400,128]{1,0:T(8,128)(2,1)S(1)} %collective-permute-done.3.refs_4_) | copy-start | bytes 307204
  35.2 29.2 %all-to-all-start.1 = ((bf16[32,80,128]{2,1,0:T(8,128)(2,1)}), bf16[32,80,128]{2,1,0:T(8,128)(2,1)S(1)}, u32[]{:S(2)}, u32[]{:S(2)}) async-start(bf16[32,80,128]{2,1,0:T(8,128)(2,1)} %roots.3), calls=%async_computation.1 | async-start | bytes 1310720 | tf_op jit(solution)/shard_map/roots/all_to_all | solution.py:252
  44.7 8.1 %collective-permute-start.12 = (bf16[1024,128]{1,0:T(8,128)(2,1)S(1)}, bf16[1024,128]{1,0:T(8,128)(2,1)S(1)}, u32[]{:S(2)}, u32[]{:S(2)}) collective-permute-start(bf16[1024,128]{1,0:T(8,128)(2,1)S(1)} %bitcast.14), channel_id=1, source_target_pairs={{0,6},{1,7},{2,0},{3,1},{4,2},{5,3},{6,4},{7,5},{8,14},{9,15},{10,... | collective-permute-start | bytes 786440 | tf_op jit(solution)/shard_map/gradients/ppermute | solution.py:33
  47.3 12.2 %collective-permute-start.10 = (bf16[1024,128]{1,0:T(8,128)(2,1)S(1)}, bf16[1024,128]{1,0:T(8,128)(2,1)S(1)}, u32[]{:S(2)}, u32[]{:S(2)}) collective-permute-start(bf16[1024,128]{1,0:T(8,128)(2,1)S(1)} %bitcast.15), channel_id=1, source_target_pairs={{0,4},{1,5},{2,6},{3,7},{4,0},{5,1},{6,2},{7,3},{8,12},{9,13},{10,... | collective-permute-start | bytes 786440 | tf_op jit(solution)/shard_map/gradients/ppermute | solution.py:33
  48.6 14.1 %collective-permute-start.8 = (bf16[1024,128]{1,0:T(8,128)(2,1)S(1)}, bf16[1024,128]{1,0:T(8,128)(2,1)S(1)}, u32[]{:S(2)}, u32[]{:S(2)}) collective-permute-start(bf16[1024,128]{1,0:T(8,128)(2,1)S(1)} %bitcast.16), channel_id=1, source_target_pairs={{0,2},{1,3},{2,4},{3,5},{4,6},{5,7},{6,0},{7,1},{8,10},{9,11},{10,... | collective-permute-start | bytes 786440 | tf_op jit(solution)/shard_map/gradients/ppermute | solution.py:33
  48.6 14.6 %collective-permute-start.7 = (bf16[1024,128]{1,0:T(8,128)(2,1)S(1)}, bf16[1024,128]{1,0:T(8,128)(2,1)S(1)}, u32[]{:S(2)}, u32[]{:S(2)}) collective-permute-start(bf16[1024,128]{1,0:T(8,128)(2,1)S(1)} %bitcast.17), channel_id=1, source_target_pairs={{0,1},{1,0},{2,3},{3,2},{4,5},{5,4},{6,7},{7,6},{8,9},{9,8},{10,11... | collective-permute-start | bytes 786440 | tf_op jit(solution)/shard_map/gradients/ppermute | solution.py:33
  52.8 10.4 %collective-permute-start.13 = (bf16[1024,128]{1,0:T(8,128)(2,1)S(1)}, bf16[1024,128]{1,0:T(8,128)(2,1)S(1)}, u32[]{:S(2)}, u32[]{:S(2)}) collective-permute-start(bf16[1024,128]{1,0:T(8,128)(2,1)S(1)} %collective-permute-done.12.refs_6_), channel_id=1, source_target_pairs={{0,1},{1,0},{2,3},{3,2},{4,5},{5,4},{6,7},{7,6},{8,9},{9,8},{10,11... | collective-permute-start | bytes 786440 | tf_op jit(solution)/shard_map/gradients/ppermute | solution.py:33
  59.5 3.7 %collective-permute-start.11 = (bf16[1024,128]{1,0:T(8,128)(2,1)S(1)}, bf16[1024,128]{1,0:T(8,128)(2,1)S(1)}, u32[]{:S(2)}, u32[]{:S(2)}) collective-permute-start(bf16[1024,128]{1,0:T(8,128)(2,1)S(1)} %collective-permute-done.10.refs_4_), channel_id=1, source_target_pairs={{0,1},{1,0},{2,3},{3,2},{4,5},{5,4},{6,7},{7,6},{8,9},{9,8},{10,11... | collective-permute-start | bytes 786440 | tf_op jit(solution)/shard_map/gradients/ppermute | solution.py:33
  62.7 1.7 %collective-permute-start.9 = (bf16[1024,128]{1,0:T(8,128)(2,1)S(1)}, bf16[1024,128]{1,0:T(8,128)(2,1)S(1)}, u32[]{:S(2)}, u32[]{:S(2)}) collective-permute-start(bf16[1024,128]{1,0:T(8,128)(2,1)S(1)} %collective-permute-done.8.refs_2_), channel_id=1, source_target_pairs={{0,1},{1,0},{2,3},{3,2},{4,5},{5,4},{6,7},{7,6},{8,9},{9,8},{10,11... | collective-permute-start | bytes 786440 | tf_op jit(solution)/shard_map/gradients/ppermute | solution.py:33
  67.0 26.8 %all-to-all-start.2 = ((bf16[32,64,128]{2,1,0:T(8,128)(2,1)}), bf16[32,64,128]{2,1,0:T(8,128)(2,1)S(1)}, u32[]{:S(2)}, u32[]{:S(2)}) async-start(bf16[32,64,128]{2,1,0:T(8,128)(2,1)} %get-tuple-element.67), calls=%async_computation.2 | async-start | bytes 1048576 | tf_op jit(solution)/shard_map/grams/all_to_all | solution.py:252
  76.2 28.3 %copy-start.1 = (s32[48]{0:T(128)S(1)}, s32[48]{0:T(128)}, u32[]{:S(2)}) copy-start(s32[48]{0:T(128)} %get-tuple-element.47.holder) | copy-start | bytes 580
  76.3 7.3 %collective-permute-start.19 = (bf16[1024,128]{1,0:T(8,128)(2,1)S(1)}, bf16[1024,128]{1,0:T(8,128)(2,1)S(1)}, u32[]{:S(2)}, u32[]{:S(2)}) collective-permute-start(bf16[1024,128]{1,0:T(8,128)(2,1)S(1)} %bitcast.9), channel_id=1, source_target_pairs={{0,6},{1,7},{2,0},{3,1},{4,2},{5,3},{6,4},{7,5},{8,14},{9,15},{10,... | collective-permute-start | bytes 786440 | tf_op jit(solution)/shard_map/roots/ppermute | solution.py:33
  76.8 9.4 %collective-permute-start.17 = (bf16[1024,128]{1,0:T(8,128)(2,1)S(1)}, bf16[1024,128]{1,0:T(8,128)(2,1)S(1)}, u32[]{:S(2)}, u32[]{:S(2)}) collective-permute-start(bf16[1024,128]{1,0:T(8,128)(2,1)S(1)} %bitcast.10), channel_id=1, source_target_pairs={{0,4},{1,5},{2,6},{3,7},{4,0},{5,1},{6,2},{7,3},{8,12},{9,13},{10,... | collective-permute-start | bytes 786440 | tf_op jit(solution)/shard_map/roots/ppermute | solution.py:33
  77.9 14.2 %collective-permute-start.15 = (bf16[1024,128]{1,0:T(8,128)(2,1)S(1)}, bf16[1024,128]{1,0:T(8,128)(2,1)S(1)}, u32[]{:S(2)}, u32[]{:S(2)}) collective-permute-start(bf16[1024,128]{1,0:T(8,128)(2,1)S(1)} %bitcast.11), channel_id=1, source_target_pairs={{0,2},{1,3},{2,4},{3,5},{4,6},{5,7},{6,0},{7,1},{8,10},{9,11},{10,... | collective-permute-start | bytes 786440 | tf_op jit(solution)/shard_map/roots/ppermute | solution.py:33
  78.4 14.2 %collective-permute-start.14 = (bf16[1024,128]{1,0:T(8,128)(2,1)S(1)}, bf16[1024,128]{1,0:T(8,128)(2,1)S(1)}, u32[]{:S(2)}, u32[]{:S(2)}) collective-permute-start(bf16[1024,128]{1,0:T(8,128)(2,1)S(1)} %bitcast.12), channel_id=1, source_target_pairs={{0,1},{1,0},{2,3},{3,2},{4,5},{5,4},{6,7},{7,6},{8,9},{9,8},{10,11... | collective-permute-start | bytes 786440 | tf_op jit(solution)/shard_map/roots/ppermute | solution.py:33
  83.5 9.1 %collective-permute-start.20 = (bf16[1024,128]{1,0:T(8,128)(2,1)S(1)}, bf16[1024,128]{1,0:T(8,128)(2,1)S(1)}, u32[]{:S(2)}, u32[]{:S(2)}) collective-permute-start(bf16[1024,128]{1,0:T(8,128)(2,1)S(1)} %collective-permute-done.19.refs_6_), channel_id=1, source_target_pairs={{0,1},{1,0},{2,3},{3,2},{4,5},{5,4},{6,7},{7,6},{8,9},{9,8},{10,11... | collective-permute-start | bytes 786440 | tf_op jit(solution)/shard_map/roots/ppermute | solution.py:33
  86.2 6.5 %collective-permute-start.18 = (bf16[1024,128]{1,0:T(8,128)(2,1)S(1)}, bf16[1024,128]{1,0:T(8,128)(2,1)S(1)}, u32[]{:S(2)}, u32[]{:S(2)}) collective-permute-start(bf16[1024,128]{1,0:T(8,128)(2,1)S(1)} %collective-permute-done.17.refs_4_), channel_id=1, source_target_pairs={{0,1},{1,0},{2,3},{3,2},{4,5},{5,4},{6,7},{7,6},{8,9},{9,8},{10,11... | collective-permute-start | bytes 786440 | tf_op jit(solution)/shard_map/roots/ppermute | solution.py:33
  92.1 1.7 %collective-permute-start.16 = (bf16[1024,128]{1,0:T(8,128)(2,1)S(1)}, bf16[1024,128]{1,0:T(8,128)(2,1)S(1)}, u32[]{:S(2)}, u32[]{:S(2)}) collective-permute-start(bf16[1024,128]{1,0:T(8,128)(2,1)S(1)} %collective-permute-done.15.refs_2_), channel_id=1, source_target_pairs={{0,1},{1,0},{2,3},{3,2},{4,5},{5,4},{6,7},{7,6},{8,9},{9,8},{10,11... | collective-permute-start | bytes 786440 | tf_op jit(solution)/shard_map/roots/ppermute | solution.py:33
  95.3 22.4 %all-to-all-start.3 = ((bf16[32,32,128]{2,1,0:T(8,128)(2,1)}), bf16[32,32,128]{2,1,0:T(8,128)(2,1)S(1)}, u32[]{:S(2)}, u32[]{:S(2)}) async-start(bf16[32,32,128]{2,1,0:T(8,128)(2,1)} %precondition.2), calls=%async_computation.3 | async-start | bytes 524288 | tf_op jit(solution)/shard_map/precondition/all_to_all | solution.py:252
  105.8 7.7 %collective-permute-start.21 = (bf16[2,6,64,128]{3,2,1,0:T(8,128)(2,1)S(1)}, bf16[2,6,64,128]{3,2,1,0:T(8,128)(2,1)S(1)}, u32[]{:S(2)}, u32[]{:S(2)}) collective-permute-start(bf16[2,6,64,128]{3,2,1,0:T(8,128)(2,1)S(1)} %get-tuple-element.77), channel_id=1, source_target_pairs={{0,2},{1,3},{2,4},{3,5},{4,6},{5,7},{6,0},{7,1},{8,10},{9,11},{10,... | collective-permute-start | bytes 589832 | tf_op jit(solution)/shard_map/precondition/ppermute | solution.py:33
  105.8 10.6 %collective-permute-start.22 = (bf16[2,6,64,128]{3,2,1,0:T(8,128)(2,1)S(1)}, bf16[2,6,64,128]{3,2,1,0:T(8,128)(2,1)S(1)}, u32[]{:S(2)}, u32[]{:S(2)}) collective-permute-start(bf16[2,6,64,128]{3,2,1,0:T(8,128)(2,1)S(1)} %get-tuple-element.78), channel_id=1, source_target_pairs={{0,4},{1,5},{2,6},{3,7},{4,0},{5,1},{6,2},{7,3},{8,12},{9,13},{10,... | collective-permute-start | bytes 589832 | tf_op jit(solution)/shard_map/precondition/ppermute | solution.py:33
  107.8 9.8 %collective-permute-start.23 = (bf16[2,6,64,128]{3,2,1,0:T(8,128)(2,1)S(1)}, bf16[2,6,64,128]{3,2,1,0:T(8,128)(2,1)S(1)}, u32[]{:S(2)}, u32[]{:S(2)}) collective-permute-start(bf16[2,6,64,128]{3,2,1,0:T(8,128)(2,1)S(1)} %get-tuple-element.79), channel_id=1, source_target_pairs={{0,6},{1,7},{2,0},{3,1},{4,2},{5,3},{6,4},{7,5},{8,14},{9,15},{10,... | collective-permute-start | bytes 589832 | tf_op jit(solution)/shard_map/precondition/ppermute | solution.py:33
  113.5 11.1 %copy-start.2 = (bf16[2,6,64,128]{3,2,1,0:T(8,128)(2,1)}, bf16[2,6,64,128]{3,2,1,0:T(8,128)(2,1)S(1)}, u32[]{:S(2)}) copy-start(bf16[2,6,64,128]{3,2,1,0:T(8,128)(2,1)S(1)} %collective-permute-done.21.refs_2_) | copy-start | bytes 589828
  116.4 8.3 %copy-start.3 = (bf16[2,6,64,128]{3,2,1,0:T(8,128)(2,1)}, bf16[2,6,64,128]{3,2,1,0:T(8,128)(2,1)S(1)}, u32[]{:S(2)}) copy-start(bf16[2,6,64,128]{3,2,1,0:T(8,128)(2,1)S(1)} %collective-permute-done.22.refs_4_) | copy-start | bytes 589828
  117.6 7.0 %copy-start.4 = (bf16[2,6,64,128]{3,2,1,0:T(8,128)(2,1)}, bf16[2,6,64,128]{3,2,1,0:T(8,128)(2,1)S(1)}, u32[]{:S(2)}) copy-start(bf16[2,6,64,128]{3,2,1,0:T(8,128)(2,1)S(1)} %collective-permute-done.23.refs_6_) | copy-start | bytes 589828
  117.6 5.6 %collective-permute-start.25 = (bf16[2,6,64,128]{3,2,1,0:T(8,128)(2,1)S(1)}, bf16[2,6,64,128]{3,2,1,0:T(8,128)(2,1)S(1)}, u32[]{:S(2)}, u32[]{:S(2)}) collective-permute-start(bf16[2,6,64,128]{3,2,1,0:T(8,128)(2,1)S(1)} %collective-permute-done.21.refs_2_), channel_id=1, source_target_pairs={{0,1},{1,0},{2,3},{3,2},{4,5},{5,4},{6,7},{7,6},{8,9},{9,8},{10,11... | collective-permute-start | bytes 589832 | tf_op jit(solution)/shard_map/precondition/ppermute | solution.py:33
  119.2 3.0 %collective-permute-start.24 = (bf16[6,64,128]{2,1,0:T(8,128)(2,1)S(1)}, bf16[6,64,128]{2,1,0:T(8,128)(2,1)S(1)}, u32[]{:S(2)}, u32[]{:S(2)}) collective-permute-start(bf16[6,64,128]{2,1,0:T(8,128)(2,1)S(1)} %get-tuple-element.83), channel_id=1, source_target_pairs={{0,1},{1,0},{2,3},{3,2},{4,5},{5,4},{6,7},{7,6},{8,9},{9,8},{10,11... | collective-permute-start | bytes 294920 | tf_op jit(solution)/shard_map/precondition/ppermute | solution.py:33
  119.3 10.2 %collective-permute-start.33 = (bf16[32,32,128]{2,1,0:T(8,128)(2,1)S(1)}, bf16[32,32,128]{2,1,0:T(8,128)(2,1)S(1)}, u32[]{:S(2)}, u32[]{:S(2)}) collective-permute-start(bf16[32,32,128]{2,1,0:T(8,128)(2,1)S(1)} %all-to-all-done.3.refs_0_), channel_id=1, source_target_pairs={{0,6},{1,7},{2,0},{3,1},{4,2},{5,3},{6,4},{7,5},{8,14},{9,15},{10,... | collective-permute-start | bytes 786440 | tf_op jit(solution)/shard_map/precondition/ppermute | solution.py:33
  121.6 12.2 %collective-permute-start.31 = (bf16[32,32,128]{2,1,0:T(8,128)(2,1)S(1)}, bf16[32,32,128]{2,1,0:T(8,128)(2,1)S(1)}, u32[]{:S(2)}, u32[]{:S(2)}) collective-permute-start(bf16[32,32,128]{2,1,0:T(8,128)(2,1)S(1)} %all-to-all-done.3.refs_0_), channel_id=1, source_target_pairs={{0,4},{1,5},{2,6},{3,7},{4,0},{5,1},{6,2},{7,3},{8,12},{9,13},{10,... | collective-permute-start | bytes 786440 | tf_op jit(solution)/shard_map/precondition/ppermute | solution.py:33
  121.6 14.7 %collective-permute-start.29 = (bf16[32,32,128]{2,1,0:T(8,128)(2,1)S(1)}, bf16[32,32,128]{2,1,0:T(8,128)(2,1)S(1)}, u32[]{:S(2)}, u32[]{:S(2)}) collective-permute-start(bf16[32,32,128]{2,1,0:T(8,128)(2,1)S(1)} %all-to-all-done.3.refs_0_), channel_id=1, source_target_pairs={{0,2},{1,3},{2,4},{3,5},{4,6},{5,7},{6,0},{7,1},{8,10},{9,11},{10,... | collective-permute-start | bytes 786440 | tf_op jit(solution)/shard_map/precondition/ppermute | solution.py:33
  122.2 2.4 %copy-start.15 = (bf16[6,64,128]{2,1,0:T(8,128)(2,1)}, bf16[6,64,128]{2,1,0:T(8,128)(2,1)S(1)}, u32[]{:S(2)}) copy-start(bf16[6,64,128]{2,1,0:T(8,128)(2,1)S(1)} %collective-permute-done.24.refs_1_) | copy-start | bytes 294916
  122.2 2.1 %collective-permute-start.26 = (bf16[2,6,64,128]{3,2,1,0:T(8,128)(2,1)S(1)}, bf16[2,6,64,128]{3,2,1,0:T(8,128)(2,1)S(1)}, u32[]{:S(2)}, u32[]{:S(2)}) collective-permute-start(bf16[2,6,64,128]{3,2,1,0:T(8,128)(2,1)S(1)} %collective-permute-done.22.refs_4_), channel_id=1, source_target_pairs={{0,1},{1,0},{2,3},{3,2},{4,5},{5,4},{6,7},{7,6},{8,9},{9,8},{10,11... | collective-permute-start | bytes 589832 | tf_op jit(solution)/shard_map/precondition/ppermute | solution.py:33
  123.2 1.4 %collective-permute-start.27 = (bf16[2,6,64,128]{3,2,1,0:T(8,128)(2,1)S(1)}, bf16[2,6,64,128]{3,2,1,0:T(8,128)(2,1)S(1)}, u32[]{:S(2)}, u32[]{:S(2)}) collective-permute-start(bf16[2,6,64,128]{3,2,1,0:T(8,128)(2,1)S(1)} %collective-permute-done.23.refs_6_), channel_id=1, source_target_pairs={{0,1},{1,0},{2,3},{3,2},{4,5},{5,4},{6,7},{7,6},{8,9},{9,8},{10,11... | collective-permute-start | bytes 589832 | tf_op jit(solution)/shard_map/precondition/ppermute | solution.py:33
  129.2 8.0 %collective-permute-start.28 = (bf16[32,32,128]{2,1,0:T(8,128)(2,1)S(1)}, bf16[32,32,128]{2,1,0:T(8,128)(2,1)S(1)}, u32[]{:S(2)}, u32[]{:S(2)}) collective-permute-start(bf16[32,32,128]{2,1,0:T(8,128)(2,1)S(1)} %all-to-all-done.3.refs_0_), channel_id=1, source_target_pairs={{0,1},{1,0},{2,3},{3,2},{4,5},{5,4},{6,7},{7,6},{8,9},{9,8},{10,11... | collective-permute-start | bytes 786440 | tf_op jit(solution)/shard_map/precondition/ppermute | solution.py:33
  129.5 7.7 %collective-permute-start.34 = (bf16[32,32,128]{2,1,0:T(8,128)(2,1)S(1)}, bf16[32,32,128]{2,1,0:T(8,128)(2,1)S(1)}, u32[]{:S(2)}, u32[]{:S(2)}) collective-permute-start(bf16[32,32,128]{2,1,0:T(8,128)(2,1)S(1)} %collective-permute-done.33.refs_6_), channel_id=1, source_target_pairs={{0,1},{1,0},{2,3},{3,2},{4,5},{5,4},{6,7},{7,6},{8,9},{9,8},{10,11... | collective-permute-start | bytes 786440 | tf_op jit(solution)/shard_map/precondition/ppermute | solution.py:33
  133.8 3.4 %collective-permute-start.32 = (bf16[32,32,128]{2,1,0:T(8,128)(2,1)S(1)}, bf16[32,32,128]{2,1,0:T(8,128)(2,1)S(1)}, u32[]{:S(2)}, u32[]{:S(2)}) collective-permute-start(bf16[32,32,128]{2,1,0:T(8,128)(2,1)S(1)} %collective-permute-done.31.refs_4_), channel_id=1, source_target_pairs={{0,1},{1,0},{2,3},{3,2},{4,5},{5,4},{6,7},{7,6},{8,9},{9,8},{10,11... | collective-permute-start | bytes 786440 | tf_op jit(solution)/shard_map/precondition/ppermute | solution.py:33
  136.3 2.0 %collective-permute-start.30 = (bf16[32,32,128]{2,1,0:T(8,128)(2,1)S(1)}, bf16[32,32,128]{2,1,0:T(8,128)(2,1)S(1)}, u32[]{:S(2)}, u32[]{:S(2)}) collective-permute-start(bf16[32,32,128]{2,1,0:T(8,128)(2,1)S(1)} %collective-permute-done.29.refs_2_), channel_id=1, source_target_pairs={{0,1},{1,0},{2,3},{3,2},{4,5},{5,4},{6,7},{7,6},{8,9},{9,8},{10,11... | collective-permute-start | bytes 786440 | tf_op jit(solution)/shard_map/precondition/ppermute | solution.py:33
  (7 other events, 6.4 us)

commit v6 on v5

--- a/solution.py
+++ b/solution.py
@@ -296,6 +296,7 @@
             [shape((CAP, 2 * ROWS, PART))] * 2 + [shape((2, CAP, 2 * ROWS, PART))] * 3,
             (holder, grams),
             [SMEM, VMEM],
+            vmem=61,
         )
     with jax.named_scope("precondition"):
         result = call(

time: 140 us -> 141 us (level)
  transfers between devices with their start and end apart: 39 -> 39, of which waited for: 17 -> 17; matrix products, arithmetic and copies ran while one was open for 0% -> 0% of each run, Pallas kernels for 3% -> 4%
where the time goes in v6:
time: 141 us
  starting transfers between devices  85 us (60%)
  waiting for transfers between devices  36.2 us (26%)
  Pallas kernels  17.4 us (12%)
    ppermute x35, starting transfers between devices, send(): lax.ppermute(value, 'worker', [(w, partner(w, k, other)) for w in range(N...  44.9 us
    all_to_all x4, starting transfers between devices, over_shard(): return lax.all_to_all(value, 'shard', 0, 0, tiled=True)  40.1 us
    ppermute x35, waiting for transfers between devices, send(): lax.ppermute(value, 'worker', [(w, partner(w, k, other)) for w in range(N...  36.2 us
    pallas_call x7, Pallas kernels, call(): pl.pallas_call(kernel, out_shape=outs, in_specs=in_specs or [VMEM] * len(...  17.4 us
  transfers between devices with their start and end apart: 39, of which 17 were waited for; matrix products, arithmetic and copies ran while one was open for 0% of the time, Pallas kernels for 4%

profile of v6, /device:TPU:1, one launch (start us, length us, event | category | flops | bytes accessed | tf_op | source)
XLA Modules:
  0.0 140.8 jit_solution(3726849459688988153)
XLA Ops:
  0.6 3.6 %roots.2 = (bf16[400,128]{1,0:T(8,128)(2,1)}, bf16[400,128]{1,0:T(8,128)(2,1)}, bf16[400,128]{1,0:T(8,128)(2,1)}, bf16[400,128]{1,0:T(8,128)(2,1)}, bf16[400,128...) custom-call(s32[32]{0:T(128)} %bitcast.23, ...), custom_call_target="tpu_custom_call" | custom-call | bytes 2097152 | tf_op jit(solution)/shard_map/roots/pallas_call | solution.py:66
  4.2 12.0 %all-to-all-start = ((bf16[32,32,128]{2,1,0:T(8,128)(2,1)}), bf16[32,32,128]{2,1,0:T(8,128)(2,1)S(1)}, u32[]{:S(2)}, u32[]{:S(2)}) async-start(bf16[32,32,128]{2,1,0:T(8,128)(2,1)} %get-tuple-element.48), calls=%async_computation | async-start | bytes 524288 | tf_op jit(solution)/shard_map/roots/all_to_all | solution.py:252
  16.2 1.0 collective-permute-start
  17.3 1.2 collective-permute-start.1
  18.5 1.5 %collective-permute-start.2 = (bf16[400,128]{1,0:T(8,128)(2,1)}, bf16[400,128]{1,0:T(8,128)(2,1)S(1)}, u32[]{:S(2)}, u32[]{:S(2)}) collective-permute-start(bf16[400,128]{1,0:T(8,128)(2,1)} %get-tuple-element.52), channel_id=1, source_target_pairs={{0,3},{1,2},{2,5},{3,4},{4,7},{5,6},{6,1},{7,0},{8,11},{9,10},{10,... | collective-permute-start | bytes 307208 | tf_op jit(solution)/shard_map/roots/ppermute | solution.py:33
  20.0 1.4 %collective-permute-start.3 = (bf16[400,128]{1,0:T(8,128)(2,1)}, bf16[400,128]{1,0:T(8,128)(2,1)S(1)}, u32[]{:S(2)}, u32[]{:S(2)}) collective-permute-start(bf16[400,128]{1,0:T(8,128)(2,1)} %get-tuple-element.53), channel_id=1, source_target_pairs={{0,4},{1,5},{2,6},{3,7},{4,0},{5,1},{6,2},{7,3},{8,12},{9,13},{10,... | collective-permute-start | bytes 307208 | tf_op jit(solution)/shard_map/roots/ppermute | solution.py:33
  21.4 1.9 %collective-permute-start.4 = (bf16[400,128]{1,0:T(8,128)(2,1)}, bf16[400,128]{1,0:T(8,128)(2,1)S(1)}, u32[]{:S(2)}, u32[]{:S(2)}) collective-permute-start(bf16[400,128]{1,0:T(8,128)(2,1)} %get-tuple-element.54), channel_id=1, source_target_pairs={{0,5},{1,4},{2,7},{3,6},{4,1},{5,0},{6,3},{7,2},{8,13},{9,12},{10,... | collective-permute-start | bytes 307208 | tf_op jit(solution)/shard_map/roots/ppermute | solution.py:33
  23.3 1.5 %collective-permute-start.5 = (bf16[400,128]{1,0:T(8,128)(2,1)}, bf16[400,128]{1,0:T(8,128)(2,1)S(1)}, u32[]{:S(2)}, u32[]{:S(2)}) collective-permute-start(bf16[400,128]{1,0:T(8,128)(2,1)} %get-tuple-element.55), channel_id=1, source_target_pairs={{0,6},{1,7},{2,0},{3,1},{4,2},{5,3},{6,4},{7,5},{8,14},{9,15},{10,... | collective-permute-start | bytes 307208 | tf_op jit(solution)/shard_map/roots/ppermute | solution.py:33
  24.7 0.9 collective-permute-start.6
  25.8 2.7 %collective-permute-done.3.refs_4_ = bf16[400,128]{1,0:T(8,128)(2,1)S(1)} collective-permute-done((bf16[400,128]{1,0:T(8,128)(2,1)}, bf16[400,128]{1,0:T(8,128)(2,1)S(1)}, u32[]{:S(2)}, u32[]{:S(2)}) %collective-permute-start.3) | collective-permute-done | bytes 102432 | tf_op jit(solution)/shard_map/roots/ppermute | solution.py:33
  28.5 2.4 %collective-permute-done.4.refs_5_ = bf16[400,128]{1,0:T(8,128)(2,1)S(1)} collective-permute-done((bf16[400,128]{1,0:T(8,128)(2,1)}, bf16[400,128]{1,0:T(8,128)(2,1)S(1)}, u32[]{:S(2)}, u32[]{:S(2)}) %collective-permute-start.4) | collective-permute-done | bytes 102432 | tf_op jit(solution)/shard_map/roots/ppermute | solution.py:33
  30.9 1.1 collective-permute-done.6.refs_7_
  32.6 2.5 %roots.3 = bf16[32,80,128]{2,1,0:T(8,128)(2,1)} custom-call(s32[48]{0:T(128)} %get-tuple-element.47.holder, bf16[400,128]{1,0:T(8,128)(2,1)} %get-tuple-element.57.refs_0_, bf16[400,128]{1,0:T(8,128)(2,1)} %copy-done.6, bf16[400,128]{1,0:T(8,128)(2,1)} %copy-done.7, bf16[400,128]{1,0:T(8,128)(2,1)} %copy-done.8, bf16[400,128]{1,0:T(8,128)(2,1)} %copy-done.9, ...), custom_call_target="tpu_custom_call" | custom-call | bytes 2097152 | tf_op jit(solution)/shard_map/roots/pallas_call | solution.py:66
  35.2 9.5 %all-to-all-start.1 = ((bf16[32,80,128]{2,1,0:T(8,128)(2,1)}), bf16[32,80,128]{2,1,0:T(8,128)(2,1)S(1)}, u32[]{:S(2)}, u32[]{:S(2)}) async-start(bf16[32,80,128]{2,1,0:T(8,128)(2,1)} %roots.3), calls=%async_computation.1 | async-start | bytes 1310720 | tf_op jit(solution)/shard_map/roots/all_to_all | solution.py:252
  44.7 2.7 %collective-permute-start.12 = (bf16[1024,128]{1,0:T(8,128)(2,1)S(1)}, bf16[1024,128]{1,0:T(8,128)(2,1)S(1)}, u32[]{:S(2)}, u32[]{:S(2)}) collective-permute-start(bf16[1024,128]{1,0:T(8,128)(2,1)S(1)} %bitcast.14), channel_id=1, source_target_pairs={{0,6},{1,7},{2,0},{3,1},{4,2},{5,3},{6,4},{7,5},{8,14},{9,15},{10,... | collective-permute-start | bytes 786440 | tf_op jit(solution)/shard_map/gradients/ppermute | solution.py:33
  47.3 1.2 collective-permute-start.10
  48.6 1.2 collective-permute-start.7
  49.8 3.0 %collective-permute-done.12.refs_6_ = bf16[1024,128]{1,0:T(8,128)(2,1)S(1)} collective-permute-done((bf16[1024,128]{1,0:T(8,128)(2,1)S(1)}, bf16[1024,128]{1,0:T(8,128)(2,1)S(1)}, u32[]{:S(2)}, u32[]{:S(2)}) %collective-permute-start.12) | collective-permute-done | bytes 262176 | tf_op jit(solution)/shard_map/gradients/ppermute | solution.py:33
  52.8 6.7 %collective-permute-start.13 = (bf16[1024,128]{1,0:T(8,128)(2,1)S(1)}, bf16[1024,128]{1,0:T(8,128)(2,1)S(1)}, u32[]{:S(2)}, u32[]{:S(2)}) collective-permute-start(bf16[1024,128]{1,0:T(8,128)(2,1)S(1)} %collective-permute-done.12.refs_6_), channel_id=1, source_target_pairs={{0,1},{1,0},{2,3},{3,2},{4,5},{5,4},{6,7},{7,6},{8,9},{9,8},{10,11... | collective-permute-start | bytes 786440 | tf_op jit(solution)/shard_map/gradients/ppermute | solution.py:33
  59.5 3.2 %collective-permute-done.8.refs_2_ = bf16[1024,128]{1,0:T(8,128)(2,1)S(1)} collective-permute-done((bf16[1024,128]{1,0:T(8,128)(2,1)S(1)}, bf16[1024,128]{1,0:T(8,128)(2,1)S(1)}, u32[]{:S(2)}, u32[]{:S(2)}) %collective-permute-start.8) | collective-permute-done | bytes 262176 | tf_op jit(solution)/shard_map/gradients/ppermute | solution.py:33
  63.2 1.1 collective-permute-done.9.refs_3_
  64.3 2.6 %grams.2 = (bf16[32,64,128]{2,1,0:T(8,128)(2,1)}, bf16[1024,128]{1,0:T(8,128)(2,1)S(1)}) custom-call(bf16[32,80,128]{2,1,0:T(8,128)(2,1)S(1)} %all-to-all-done.1.roots, bf16[1024,128]{1,0:T(8,128)(2,1)S(1)} %bitcast.18, bf16[1024,128]{1,0:T(8,128)(2,1)S(1)} %collective-permute-done.7.refs_1_, bf16[1024,128]{1,0:T(8,128)(2,1)S(1)} %collective-permute-done.8.refs_2_, ...), custom_call_target="tpu_custom_call" | custom-call | flops 805306368 | bytes 2097152 | tf_op jit(solution)/shard_map/grams/pallas_call | solution.py:66
  67.0 9.4 %all-to-all-start.2 = ((bf16[32,64,128]{2,1,0:T(8,128)(2,1)}), bf16[32,64,128]{2,1,0:T(8,128)(2,1)}, u32[]{:S(2)}, u32[]{:S(2)}) async-start(bf16[32,64,128]{2,1,0:T(8,128)(2,1)} %get-tuple-element.67), calls=%async_computation.2 | async-start | bytes 1048576 | tf_op jit(solution)/shard_map/grams/all_to_all | solution.py:252
  76.9 1.1 collective-permute-start.17
  78.5 1.5 %collective-permute-start.14 = (bf16[1024,128]{1,0:T(8,128)(2,1)S(1)}, bf16[1024,128]{1,0:T(8,128)(2,1)S(1)}, u32[]{:S(2)}, u32[]{:S(2)}) collective-permute-start(bf16[1024,128]{1,0:T(8,128)(2,1)S(1)} %bitcast.12), channel_id=1, source_target_pairs={{0,1},{1,0},{2,3},{3,2},{4,5},{5,4},{6,7},{7,6},{8,9},{9,8},{10,11... | collective-permute-start | bytes 786440 | tf_op jit(solution)/shard_map/roots/ppermute | solution.py:33
  80.0 3.6 %collective-permute-done.19.refs_6_ = bf16[1024,128]{1,0:T(8,128)(2,1)S(1)} collective-permute-done((bf16[1024,128]{1,0:T(8,128)(2,1)S(1)}, bf16[1024,128]{1,0:T(8,128)(2,1)S(1)}, u32[]{:S(2)}, u32[]{:S(2)}) %collective-permute-start.19) | collective-permute-done | bytes 262176 | tf_op jit(solution)/shard_map/roots/ppermute | solution.py:33
  83.6 2.7 %collective-permute-start.20 = (bf16[1024,128]{1,0:T(8,128)(2,1)S(1)}, bf16[1024,128]{1,0:T(8,128)(2,1)S(1)}, u32[]{:S(2)}, u32[]{:S(2)}) collective-permute-start(bf16[1024,128]{1,0:T(8,128)(2,1)S(1)} %collective-permute-done.19.refs_6_), channel_id=1, source_target_pairs={{0,1},{1,0},{2,3},{3,2},{4,5},{5,4},{6,7},{7,6},{8,9},{9,8},{10,11... | collective-permute-start | bytes 786440 | tf_op jit(solution)/shard_map/roots/ppermute | solution.py:33
  86.3 2.3 %collective-permute-start.18 = (bf16[1024,128]{1,0:T(8,128)(2,1)S(1)}, bf16[1024,128]{1,0:T(8,128)(2,1)S(1)}, u32[]{:S(2)}, u32[]{:S(2)}) collective-permute-start(bf16[1024,128]{1,0:T(8,128)(2,1)S(1)} %collective-permute-done.17.refs_4_), channel_id=1, source_target_pairs={{0,1},{1,0},{2,3},{3,2},{4,5},{5,4},{6,7},{7,6},{8,9},{9,8},{10,11... | collective-permute-start | bytes 786440 | tf_op jit(solution)/shard_map/roots/ppermute | solution.py:33
  88.6 3.7 %collective-permute-done.15.refs_2_ = bf16[1024,128]{1,0:T(8,128)(2,1)S(1)} collective-permute-done((bf16[1024,128]{1,0:T(8,128)(2,1)S(1)}, bf16[1024,128]{1,0:T(8,128)(2,1)S(1)}, u32[]{:S(2)}, u32[]{:S(2)}) %collective-permute-start.15) | collective-permute-done | bytes 262176 | tf_op jit(solution)/shard_map/roots/ppermute | solution.py:33
  92.7 1.1 collective-permute-done.16.refs_3_
  93.9 1.5 %precondition.2 = bf16[32,32,128]{2,1,0:T(8,128)(2,1)} custom-call(bf16[32,80,128]{2,1,0:T(8,128)(2,1)S(1)} %all-to-all-done.1.roots, bf16[1024,128]{1,0:T(8,128)(2,1)S(1)} %get-tuple-element.66.image, bf16[1024,128]{1,0:T(8,128)(2,1)S(1)} %bitcast.13, bf16[1024,128]{1,0:T(8,128)(2,1)S(1)} %collective-permute-done.14.refs_1_, ...), custom_call_target="tpu_custom_call" | custom-call | flops 268435456 | bytes 2097152 | tf_op jit(solution)/shard_map/precondition/pallas_call | solution.py:66
  95.4 9.1 %all-to-all-start.3 = ((bf16[32,32,128]{2,1,0:T(8,128)(2,1)}), bf16[32,32,128]{2,1,0:T(8,128)(2,1)S(1)}, u32[]{:S(2)}, u32[]{:S(2)}) async-start(bf16[32,32,128]{2,1,0:T(8,128)(2,1)} %precondition.2), calls=%async_computation.3 | async-start | bytes 524288 | tf_op jit(solution)/shard_map/precondition/all_to_all | solution.py:252
  104.5 2.0 %grams.3 = (bf16[6,64,128]{2,1,0:T(8,128)(2,1)}, bf16[6,64,128]{2,1,0:T(8,128)(2,1)}, bf16[2,6,64,128]{3,2,1,0:T(8,128)(2,1)}, bf16[2,6,64,128]{3,2,1,0:T(8,128)(2,1)}, bf16[2,6,64,128]{3,2,1,0:T(8,128)(2,1)}) custom-call(s32[48]{0:T(128)} %get-tuple-element.47.holder, bf16[32,64,128]{2,1,0:T(8,128)(2,1)} %all-to-all-done.2.grams), custom_call_target="tpu_custom_call" | custom-call | bytes 2097152 | tf_op jit(solution)/shard_map/grams/pallas_call | solution.py:66
  106.5 2.0 %collective-permute-start.22 = (bf16[2,6,64,128]{3,2,1,0:T(8,128)(2,1)}, bf16[2,6,64,128]{3,2,1,0:T(8,128)(2,1)S(1)}, u32[]{:S(2)}, u32[]{:S(2)}) collective-permute-start(bf16[2,6,64,128]{3,2,1,0:T(8,128)(2,1)} %get-tuple-element.78), channel_id=1, source_target_pairs={{0,4},{1,5},{2,6},{3,7},{4,0},{5,1},{6,2},{7,3},{8,12},{9,13},{10,... | collective-permute-start | bytes 589832 | tf_op jit(solution)/shard_map/precondition/ppermute | solution.py:33
  108.5 1.2 collective-permute-start.23
  109.7 4.7 %collective-permute-done.21.refs_2_ = bf16[2,6,64,128]{3,2,1,0:T(8,128)(2,1)S(1)} collective-permute-done((bf16[2,6,64,128]{3,2,1,0:T(8,128)(2,1)}, bf16[2,6,64,128]{3,2,1,0:T(8,128)(2,1)S(1)}, u32[]{:S(2)}, u32[]{:S(2)}) %collective-permute-start.21) | collective-permute-done | bytes 196640 | tf_op jit(solution)/shard_map/precondition/ppermute | solution.py:33
  114.4 2.9 %collective-permute-done.22.refs_4_ = bf16[2,6,64,128]{3,2,1,0:T(8,128)(2,1)S(1)} collective-permute-done((bf16[2,6,64,128]{3,2,1,0:T(8,128)(2,1)}, bf16[2,6,64,128]{3,2,1,0:T(8,128)(2,1)S(1)}, u32[]{:S(2)}, u32[]{:S(2)}) %collective-permute-start.22) | collective-permute-done | bytes 196640 | tf_op jit(solution)/shard_map/precondition/ppermute | solution.py:33
  117.3 1.3 collective-permute-done.23.refs_6_
  118.7 1.5 %collective-permute-start.25 = (bf16[2,6,64,128]{3,2,1,0:T(8,128)(2,1)S(1)}, bf16[2,6,64,128]{3,2,1,0:T(8,128)(2,1)S(1)}, u32[]{:S(2)}, u32[]{:S(2)}) collective-permute-start(bf16[2,6,64,128]{3,2,1,0:T(8,128)(2,1)S(1)} %collective-permute-done.21.refs_2_), channel_id=1, source_target_pairs={{0,1},{1,0},{2,3},{3,2},{4,5},{5,4},{6,7},{7,6},{8,9},{9,8},{10,11... | collective-permute-start | bytes 589832 | tf_op jit(solution)/shard_map/precondition/ppermute | solution.py:33
  120.2 2.3 %collective-permute-start.33 = (bf16[32,32,128]{2,1,0:T(8,128)(2,1)S(1)}, bf16[32,32,128]{2,1,0:T(8,128)(2,1)S(1)}, u32[]{:S(2)}, u32[]{:S(2)}) collective-permute-start(bf16[32,32,128]{2,1,0:T(8,128)(2,1)S(1)} %all-to-all-done.3.refs_0_), channel_id=1, source_target_pairs={{0,6},{1,7},{2,0},{3,1},{4,2},{5,3},{6,4},{7,5},{8,14},{9,15},{10,... | collective-permute-start | bytes 786440 | tf_op jit(solution)/shard_map/precondition/ppermute | solution.py:33
  123.2 1.0 collective-permute-start.26
  124.2 1.0 collective-permute-done.26.refs_5_
  126.3 3.8 %factors.1 = (f32[6,32,1024]{2,1,0:T(8,128)}, f32[6,32,1024]{2,1,0:T(8,128)}) custom-call(s32[48]{0:T(128)} %get-tuple-element.47.holder, f32[6,32,1024]{2,1,0:T(8,128)} %bitcast.19, f32[6,32,1024]{2,1,0:T(8,128)} %bitcast.20, bf16[6,64,128]{2,1,0:T(8,128)(2,1)} %get-tuple-element.82.refs_0_, bf16[6,64,128]{2,1,0:T(8,128)(2,1)} %copy-done.13, ...), custom_call_target="tpu_custom_call" | custom-call | bytes 20971520 | tf_op jit(solution)/shard_map/factors/pallas_call | solution.py:66
  130.5 4.3 %collective-permute-start.34 = (bf16[32,32,128]{2,1,0:T(8,128)(2,1)S(1)}, bf16[32,32,128]{2,1,0:T(8,128)(2,1)S(1)}, u32[]{:S(2)}, u32[]{:S(2)}) collective-permute-start(bf16[32,32,128]{2,1,0:T(8,128)(2,1)S(1)} %collective-permute-done.33.refs_6_), channel_id=1, source_target_pairs={{0,1},{1,0},{2,3},{3,2},{4,5},{5,4},{6,7},{7,6},{8,9},{9,8},{10,11... | collective-permute-start | bytes 786440 | tf_op jit(solution)/shard_map/precondition/ppermute | solution.py:33
  134.7 2.5 %collective-permute-done.29.refs_2_ = bf16[32,32,128]{2,1,0:T(8,128)(2,1)S(1)} collective-permute-done((bf16[32,32,128]{2,1,0:T(8,128)(2,1)S(1)}, bf16[32,32,128]{2,1,0:T(8,128)(2,1)S(1)}, u32[]{:S(2)}, u32[]{:S(2)}) %collective-permute-start.29) | collective-permute-done | bytes 262176 | tf_op jit(solution)/shard_map/precondition/ppermute | solution.py:33
  137.3 0.8 collective-permute-start.30
  138.1 1.1 collective-permute-done.30.refs_3_
  139.3 1.4 precondition.3
  (66 shorter events, 5.0 us)
Async XLA Ops:
  4.2 27.8 %all-to-all-start = ((bf16[32,32,128]{2,1,0:T(8,128)(2,1)}), bf16[32,32,128]{2,1,0:T(8,128)(2,1)S(1)}, u32[]{:S(2)}, u32[]{:S(2)}) async-start(bf16[32,32,128]{2,1,0:T(8,128)(2,1)} %get-tuple-element.48), calls=%async_computation | async-start | bytes 524288 | tf_op jit(solution)/shard_map/roots/all_to_all | solution.py:252
  16.2 7.0 %collective-permute-start = (bf16[400,128]{1,0:T(8,128)(2,1)}, bf16[400,128]{1,0:T(8,128)(2,1)S(1)}, u32[]{:S(2)}, u32[]{:S(2)}) collective-permute-start(bf16[400,128]{1,0:T(8,128)(2,1)} %get-tuple-element.50), channel_id=1, source_target_pairs={{0,1},{1,0},{2,3},{3,2},{4,5},{5,4},{6,7},{7,6},{8,9},{9,8},{10,11... | collective-permute-start | bytes 307208 | tf_op jit(solution)/shard_map/roots/ppermute | solution.py:33
  17.3 7.5 %collective-permute-start.1 = (bf16[400,128]{1,0:T(8,128)(2,1)}, bf16[400,128]{1,0:T(8,128)(2,1)S(1)}, u32[]{:S(2)}, u32[]{:S(2)}) collective-permute-start(bf16[400,128]{1,0:T(8,128)(2,1)} %get-tuple-element.51), channel_id=1, source_target_pairs={{0,2},{1,3},{2,4},{3,5},{4,6},{5,7},{6,0},{7,1},{8,10},{9,11},{10,... | collective-permute-start | bytes 307208 | tf_op jit(solution)/shard_map/roots/ppermute | solution.py:33
  18.5 7.3 %collective-permute-start.2 = (bf16[400,128]{1,0:T(8,128)(2,1)}, bf16[400,128]{1,0:T(8,128)(2,1)S(1)}, u32[]{:S(2)}, u32[]{:S(2)}) collective-permute-start(bf16[400,128]{1,0:T(8,128)(2,1)} %get-tuple-element.52), channel_id=1, source_target_pairs={{0,3},{1,2},{2,5},{3,4},{4,7},{5,6},{6,1},{7,0},{8,11},{9,10},{10,... | collective-permute-start | bytes 307208 | tf_op jit(solution)/shard_map/roots/ppermute | solution.py:33
  20.0 8.6 %collective-permute-start.3 = (bf16[400,128]{1,0:T(8,128)(2,1)}, bf16[400,128]{1,0:T(8,128)(2,1)S(1)}, u32[]{:S(2)}, u32[]{:S(2)}) collective-permute-start(bf16[400,128]{1,0:T(8,128)(2,1)} %get-tuple-element.53), channel_id=1, source_target_pairs={{0,4},{1,5},{2,6},{3,7},{4,0},{5,1},{6,2},{7,3},{8,12},{9,13},{10,... | collective-permute-start | bytes 307208 | tf_op jit(solution)/shard_map/roots/ppermute | solution.py:33
  21.4 9.5 %collective-permute-start.4 = (bf16[400,128]{1,0:T(8,128)(2,1)}, bf16[400,128]{1,0:T(8,128)(2,1)S(1)}, u32[]{:S(2)}, u32[]{:S(2)}) collective-permute-start(bf16[400,128]{1,0:T(8,128)(2,1)} %get-tuple-element.54), channel_id=1, source_target_pairs={{0,5},{1,4},{2,7},{3,6},{4,1},{5,0},{6,3},{7,2},{8,13},{9,12},{10,... | collective-permute-start | bytes 307208 | tf_op jit(solution)/shard_map/roots/ppermute | solution.py:33
  23.3 8.7 %copy-start.6 = (bf16[400,128]{1,0:T(8,128)(2,1)}, bf16[400,128]{1,0:T(8,128)(2,1)S(1)}, u32[]{:S(2)}) copy-start(bf16[400,128]{1,0:T(8,128)(2,1)S(1)} %collective-permute-done.refs_1_) | copy-start | bytes 307204
  23.3 7.6 %collective-permute-start.5 = (bf16[400,128]{1,0:T(8,128)(2,1)}, bf16[400,128]{1,0:T(8,128)(2,1)S(1)}, u32[]{:S(2)}, u32[]{:S(2)}) collective-permute-start(bf16[400,128]{1,0:T(8,128)(2,1)} %get-tuple-element.55), channel_id=1, source_target_pairs={{0,6},{1,7},{2,0},{3,1},{4,2},{5,3},{6,4},{7,5},{8,14},{9,15},{10,... | collective-permute-start | bytes 307208 | tf_op jit(solution)/shard_map/roots/ppermute | solution.py:33
  24.7 7.3 %copy-start.7 = (bf16[400,128]{1,0:T(8,128)(2,1)}, bf16[400,128]{1,0:T(8,128)(2,1)S(1)}, u32[]{:S(2)}) copy-start(bf16[400,128]{1,0:T(8,128)(2,1)S(1)} %collective-permute-done.1.refs_2_) | copy-start | bytes 307204
  24.7 7.3 %collective-permute-start.6 = (bf16[400,128]{1,0:T(8,128)(2,1)}, bf16[400,128]{1,0:T(8,128)(2,1)S(1)}, u32[]{:S(2)}, u32[]{:S(2)}) collective-permute-start(bf16[400,128]{1,0:T(8,128)(2,1)} %get-tuple-element.56), channel_id=1, source_target_pairs={{0,7},{1,6},{2,1},{3,0},{4,3},{5,2},{6,5},{7,4},{8,15},{9,14},{10,... | collective-permute-start | bytes 307208 | tf_op jit(solution)/shard_map/roots/ppermute | solution.py:33
  25.8 6.2 %copy-start.8 = (bf16[400,128]{1,0:T(8,128)(2,1)}, bf16[400,128]{1,0:T(8,128)(2,1)S(1)}, u32[]{:S(2)}) copy-start(bf16[400,128]{1,0:T(8,128)(2,1)S(1)} %collective-permute-done.2.refs_3_) | copy-start | bytes 307204
  28.5 3.5 %copy-start.9 = (bf16[400,128]{1,0:T(8,128)(2,1)}, bf16[400,128]{1,0:T(8,128)(2,1)S(1)}, u32[]{:S(2)}) copy-start(bf16[400,128]{1,0:T(8,128)(2,1)S(1)} %collective-permute-done.3.refs_4_) | copy-start | bytes 307204
  35.2 29.2 %all-to-all-start.1 = ((bf16[32,80,128]{2,1,0:T(8,128)(2,1)}), bf16[32,80,128]{2,1,0:T(8,128)(2,1)S(1)}, u32[]{:S(2)}, u32[]{:S(2)}) async-start(bf16[32,80,128]{2,1,0:T(8,128)(2,1)} %roots.3), calls=%async_computation.1 | async-start | bytes 1310720 | tf_op jit(solution)/shard_map/roots/all_to_all | solution.py:252
  44.7 8.1 %collective-permute-start.12 = (bf16[1024,128]{1,0:T(8,128)(2,1)S(1)}, bf16[1024,128]{1,0:T(8,128)(2,1)S(1)}, u32[]{:S(2)}, u32[]{:S(2)}) collective-permute-start(bf16[1024,128]{1,0:T(8,128)(2,1)S(1)} %bitcast.14), channel_id=1, source_target_pairs={{0,6},{1,7},{2,0},{3,1},{4,2},{5,3},{6,4},{7,5},{8,14},{9,15},{10,... | collective-permute-start | bytes 786440 | tf_op jit(solution)/shard_map/gradients/ppermute | solution.py:33
  47.3 12.2 %collective-permute-start.10 = (bf16[1024,128]{1,0:T(8,128)(2,1)S(1)}, bf16[1024,128]{1,0:T(8,128)(2,1)S(1)}, u32[]{:S(2)}, u32[]{:S(2)}) collective-permute-start(bf16[1024,128]{1,0:T(8,128)(2,1)S(1)} %bitcast.15), channel_id=1, source_target_pairs={{0,4},{1,5},{2,6},{3,7},{4,0},{5,1},{6,2},{7,3},{8,12},{9,13},{10,... | collective-permute-start | bytes 786440 | tf_op jit(solution)/shard_map/gradients/ppermute | solution.py:33
  48.6 14.1 %collective-permute-start.8 = (bf16[1024,128]{1,0:T(8,128)(2,1)S(1)}, bf16[1024,128]{1,0:T(8,128)(2,1)S(1)}, u32[]{:S(2)}, u32[]{:S(2)}) collective-permute-start(bf16[1024,128]{1,0:T(8,128)(2,1)S(1)} %bitcast.16), channel_id=1, source_target_pairs={{0,2},{1,3},{2,4},{3,5},{4,6},{5,7},{6,0},{7,1},{8,10},{9,11},{10,... | collective-permute-start | bytes 786440 | tf_op jit(solution)/shard_map/gradients/ppermute | solution.py:33
  48.6 14.6 %collective-permute-start.7 = (bf16[1024,128]{1,0:T(8,128)(2,1)S(1)}, bf16[1024,128]{1,0:T(8,128)(2,1)S(1)}, u32[]{:S(2)}, u32[]{:S(2)}) collective-permute-start(bf16[1024,128]{1,0:T(8,128)(2,1)S(1)} %bitcast.17), channel_id=1, source_target_pairs={{0,1},{1,0},{2,3},{3,2},{4,5},{5,4},{6,7},{7,6},{8,9},{9,8},{10,11... | collective-permute-start | bytes 786440 | tf_op jit(solution)/shard_map/gradients/ppermute | solution.py:33
  52.8 10.4 %collective-permute-start.13 = (bf16[1024,128]{1,0:T(8,128)(2,1)S(1)}, bf16[1024,128]{1,0:T(8,128)(2,1)S(1)}, u32[]{:S(2)}, u32[]{:S(2)}) collective-permute-start(bf16[1024,128]{1,0:T(8,128)(2,1)S(1)} %collective-permute-done.12.refs_6_), channel_id=1, source_target_pairs={{0,1},{1,0},{2,3},{3,2},{4,5},{5,4},{6,7},{7,6},{8,9},{9,8},{10,11... | collective-permute-start | bytes 786440 | tf_op jit(solution)/shard_map/gradients/ppermute | solution.py:33
  59.5 3.7 %collective-permute-start.11 = (bf16[1024,128]{1,0:T(8,128)(2,1)S(1)}, bf16[1024,128]{1,0:T(8,128)(2,1)S(1)}, u32[]{:S(2)}, u32[]{:S(2)}) collective-permute-start(bf16[1024,128]{1,0:T(8,128)(2,1)S(1)} %collective-permute-done.10.refs_4_), channel_id=1, source_target_pairs={{0,1},{1,0},{2,3},{3,2},{4,5},{5,4},{6,7},{7,6},{8,9},{9,8},{10,11... | collective-permute-start | bytes 786440 | tf_op jit(solution)/shard_map/gradients/ppermute | solution.py:33
  62.7 1.7 %collective-permute-start.9 = (bf16[1024,128]{1,0:T(8,128)(2,1)S(1)}, bf16[1024,128]{1,0:T(8,128)(2,1)S(1)}, u32[]{:S(2)}, u32[]{:S(2)}) collective-permute-start(bf16[1024,128]{1,0:T(8,128)(2,1)S(1)} %collective-permute-done.8.refs_2_), channel_id=1, source_target_pairs={{0,1},{1,0},{2,3},{3,2},{4,5},{5,4},{6,7},{7,6},{8,9},{9,8},{10,11... | collective-permute-start | bytes 786440 | tf_op jit(solution)/shard_map/gradients/ppermute | solution.py:33
  67.0 26.9 %all-to-all-start.2 = ((bf16[32,64,128]{2,1,0:T(8,128)(2,1)}), bf16[32,64,128]{2,1,0:T(8,128)(2,1)}, u32[]{:S(2)}, u32[]{:S(2)}) async-start(bf16[32,64,128]{2,1,0:T(8,128)(2,1)} %get-tuple-element.67), calls=%async_computation.2 | async-start | bytes 1048576 | tf_op jit(solution)/shard_map/grams/all_to_all | solution.py:252
  76.3 7.3 %collective-permute-start.19 = (bf16[1024,128]{1,0:T(8,128)(2,1)S(1)}, bf16[1024,128]{1,0:T(8,128)(2,1)S(1)}, u32[]{:S(2)}, u32[]{:S(2)}) collective-permute-start(bf16[1024,128]{1,0:T(8,128)(2,1)S(1)} %bitcast.9), channel_id=1, source_target_pairs={{0,6},{1,7},{2,0},{3,1},{4,2},{5,3},{6,4},{7,5},{8,14},{9,15},{10,... | collective-permute-start | bytes 786440 | tf_op jit(solution)/shard_map/roots/ppermute | solution.py:33
  76.9 9.4 %collective-permute-start.17 = (bf16[1024,128]{1,0:T(8,128)(2,1)S(1)}, bf16[1024,128]{1,0:T(8,128)(2,1)S(1)}, u32[]{:S(2)}, u32[]{:S(2)}) collective-permute-start(bf16[1024,128]{1,0:T(8,128)(2,1)S(1)} %bitcast.10), channel_id=1, source_target_pairs={{0,4},{1,5},{2,6},{3,7},{4,0},{5,1},{6,2},{7,3},{8,12},{9,13},{10,... | collective-permute-start | bytes 786440 | tf_op jit(solution)/shard_map/roots/ppermute | solution.py:33
  78.0 14.3 %collective-permute-start.15 = (bf16[1024,128]{1,0:T(8,128)(2,1)S(1)}, bf16[1024,128]{1,0:T(8,128)(2,1)S(1)}, u32[]{:S(2)}, u32[]{:S(2)}) collective-permute-start(bf16[1024,128]{1,0:T(8,128)(2,1)S(1)} %bitcast.11), channel_id=1, source_target_pairs={{0,2},{1,3},{2,4},{3,5},{4,6},{5,7},{6,0},{7,1},{8,10},{9,11},{10,... | collective-permute-start | bytes 786440 | tf_op jit(solution)/shard_map/roots/ppermute | solution.py:33
  78.5 14.2 %collective-permute-start.14 = (bf16[1024,128]{1,0:T(8,128)(2,1)S(1)}, bf16[1024,128]{1,0:T(8,128)(2,1)S(1)}, u32[]{:S(2)}, u32[]{:S(2)}) collective-permute-start(bf16[1024,128]{1,0:T(8,128)(2,1)S(1)} %bitcast.12), channel_id=1, source_target_pairs={{0,1},{1,0},{2,3},{3,2},{4,5},{5,4},{6,7},{7,6},{8,9},{9,8},{10,11... | collective-permute-start | bytes 786440 | tf_op jit(solution)/shard_map/roots/ppermute | solution.py:33
  83.6 9.1 %collective-permute-start.20 = (bf16[1024,128]{1,0:T(8,128)(2,1)S(1)}, bf16[1024,128]{1,0:T(8,128)(2,1)S(1)}, u32[]{:S(2)}, u32[]{:S(2)}) collective-permute-start(bf16[1024,128]{1,0:T(8,128)(2,1)S(1)} %collective-permute-done.19.refs_6_), channel_id=1, source_target_pairs={{0,1},{1,0},{2,3},{3,2},{4,5},{5,4},{6,7},{7,6},{8,9},{9,8},{10,11... | collective-permute-start | bytes 786440 | tf_op jit(solution)/shard_map/roots/ppermute | solution.py:33
  86.3 6.5 %collective-permute-start.18 = (bf16[1024,128]{1,0:T(8,128)(2,1)S(1)}, bf16[1024,128]{1,0:T(8,128)(2,1)S(1)}, u32[]{:S(2)}, u32[]{:S(2)}) collective-permute-start(bf16[1024,128]{1,0:T(8,128)(2,1)S(1)} %collective-permute-done.17.refs_4_), channel_id=1, source_target_pairs={{0,1},{1,0},{2,3},{3,2},{4,5},{5,4},{6,7},{7,6},{8,9},{9,8},{10,11... | collective-permute-start | bytes 786440 | tf_op jit(solution)/shard_map/roots/ppermute | solution.py:33
  92.3 1.6 %collective-permute-start.16 = (bf16[1024,128]{1,0:T(8,128)(2,1)S(1)}, bf16[1024,128]{1,0:T(8,128)(2,1)S(1)}, u32[]{:S(2)}, u32[]{:S(2)}) collective-permute-start(bf16[1024,128]{1,0:T(8,128)(2,1)S(1)} %collective-permute-done.15.refs_2_), channel_id=1, source_target_pairs={{0,1},{1,0},{2,3},{3,2},{4,5},{5,4},{6,7},{7,6},{8,9},{9,8},{10,11... | collective-permute-start | bytes 786440 | tf_op jit(solution)/shard_map/roots/ppermute | solution.py:33
  95.4 23.3 %all-to-all-start.3 = ((bf16[32,32,128]{2,1,0:T(8,128)(2,1)}), bf16[32,32,128]{2,1,0:T(8,128)(2,1)S(1)}, u32[]{:S(2)}, u32[]{:S(2)}) async-start(bf16[32,32,128]{2,1,0:T(8,128)(2,1)} %precondition.2), calls=%async_computation.3 | async-start | bytes 524288 | tf_op jit(solution)/shard_map/precondition/all_to_all | solution.py:252
  106.5 7.9 %collective-permute-start.21 = (bf16[2,6,64,128]{3,2,1,0:T(8,128)(2,1)}, bf16[2,6,64,128]{3,2,1,0:T(8,128)(2,1)S(1)}, u32[]{:S(2)}, u32[]{:S(2)}) collective-permute-start(bf16[2,6,64,128]{3,2,1,0:T(8,128)(2,1)} %get-tuple-element.77), channel_id=1, source_target_pairs={{0,2},{1,3},{2,4},{3,5},{4,6},{5,7},{6,0},{7,1},{8,10},{9,11},{10,... | collective-permute-start | bytes 589832 | tf_op jit(solution)/shard_map/precondition/ppermute | solution.py:33
  106.5 10.8 %collective-permute-start.22 = (bf16[2,6,64,128]{3,2,1,0:T(8,128)(2,1)}, bf16[2,6,64,128]{3,2,1,0:T(8,128)(2,1)S(1)}, u32[]{:S(2)}, u32[]{:S(2)}) collective-permute-start(bf16[2,6,64,128]{3,2,1,0:T(8,128)(2,1)} %get-tuple-element.78), channel_id=1, source_target_pairs={{0,4},{1,5},{2,6},{3,7},{4,0},{5,1},{6,2},{7,3},{8,12},{9,13},{10,... | collective-permute-start | bytes 589832 | tf_op jit(solution)/shard_map/precondition/ppermute | solution.py:33
  108.5 10.1 %collective-permute-start.23 = (bf16[2,6,64,128]{3,2,1,0:T(8,128)(2,1)}, bf16[2,6,64,128]{3,2,1,0:T(8,128)(2,1)S(1)}, u32[]{:S(2)}, u32[]{:S(2)}) collective-permute-start(bf16[2,6,64,128]{3,2,1,0:T(8,128)(2,1)} %get-tuple-element.79), channel_id=1, source_target_pairs={{0,6},{1,7},{2,0},{3,1},{4,2},{5,3},{6,4},{7,5},{8,14},{9,15},{10,... | collective-permute-start | bytes 589832 | tf_op jit(solution)/shard_map/precondition/ppermute | solution.py:33
  114.4 11.1 %copy-start = (bf16[2,6,64,128]{3,2,1,0:T(8,128)(2,1)}, bf16[2,6,64,128]{3,2,1,0:T(8,128)(2,1)S(1)}, u32[]{:S(2)}) copy-start(bf16[2,6,64,128]{3,2,1,0:T(8,128)(2,1)S(1)} %collective-permute-done.21.refs_2_) | copy-start | bytes 589828
  117.3 8.3 %copy-start.1 = (bf16[2,6,64,128]{3,2,1,0:T(8,128)(2,1)}, bf16[2,6,64,128]{3,2,1,0:T(8,128)(2,1)S(1)}, u32[]{:S(2)}) copy-start(bf16[2,6,64,128]{3,2,1,0:T(8,128)(2,1)S(1)} %collective-permute-done.22.refs_4_) | copy-start | bytes 589828
  118.7 6.9 %copy-start.2 = (bf16[2,6,64,128]{3,2,1,0:T(8,128)(2,1)}, bf16[2,6,64,128]{3,2,1,0:T(8,128)(2,1)S(1)}, u32[]{:S(2)}) copy-start(bf16[2,6,64,128]{3,2,1,0:T(8,128)(2,1)S(1)} %collective-permute-done.23.refs_6_) | copy-start | bytes 589828
  118.7 5.5 %collective-permute-start.25 = (bf16[2,6,64,128]{3,2,1,0:T(8,128)(2,1)S(1)}, bf16[2,6,64,128]{3,2,1,0:T(8,128)(2,1)S(1)}, u32[]{:S(2)}, u32[]{:S(2)}) collective-permute-start(bf16[2,6,64,128]{3,2,1,0:T(8,128)(2,1)S(1)} %collective-permute-done.21.refs_2_), channel_id=1, source_target_pairs={{0,1},{1,0},{2,3},{3,2},{4,5},{5,4},{6,7},{7,6},{8,9},{9,8},{10,11... | collective-permute-start | bytes 589832 | tf_op jit(solution)/shard_map/precondition/ppermute | solution.py:33
  120.1 3.0 %collective-permute-start.24 = (bf16[6,64,128]{2,1,0:T(8,128)(2,1)}, bf16[6,64,128]{2,1,0:T(8,128)(2,1)S(1)}, u32[]{:S(2)}, u32[]{:S(2)}) collective-permute-start(bf16[6,64,128]{2,1,0:T(8,128)(2,1)} %get-tuple-element.83), channel_id=1, source_target_pairs={{0,1},{1,0},{2,3},{3,2},{4,5},{5,4},{6,7},{7,6},{8,9},{9,8},{10,11... | collective-permute-start | bytes 294920 | tf_op jit(solution)/shard_map/precondition/ppermute | solution.py:33
  120.2 10.3 %collective-permute-start.33 = (bf16[32,32,128]{2,1,0:T(8,128)(2,1)S(1)}, bf16[32,32,128]{2,1,0:T(8,128)(2,1)S(1)}, u32[]{:S(2)}, u32[]{:S(2)}) collective-permute-start(bf16[32,32,128]{2,1,0:T(8,128)(2,1)S(1)} %all-to-all-done.3.refs_0_), channel_id=1, source_target_pairs={{0,6},{1,7},{2,0},{3,1},{4,2},{5,3},{6,4},{7,5},{8,14},{9,15},{10,... | collective-permute-start | bytes 786440 | tf_op jit(solution)/shard_map/precondition/ppermute | solution.py:33
  122.6 12.2 %collective-permute-start.31 = (bf16[32,32,128]{2,1,0:T(8,128)(2,1)S(1)}, bf16[32,32,128]{2,1,0:T(8,128)(2,1)S(1)}, u32[]{:S(2)}, u32[]{:S(2)}) collective-permute-start(bf16[32,32,128]{2,1,0:T(8,128)(2,1)S(1)} %all-to-all-done.3.refs_0_), channel_id=1, source_target_pairs={{0,4},{1,5},{2,6},{3,7},{4,0},{5,1},{6,2},{7,3},{8,12},{9,13},{10,... | collective-permute-start | bytes 786440 | tf_op jit(solution)/shard_map/precondition/ppermute | solution.py:33
  122.6 14.7 %collective-permute-start.29 = (bf16[32,32,128]{2,1,0:T(8,128)(2,1)S(1)}, bf16[32,32,128]{2,1,0:T(8,128)(2,1)S(1)}, u32[]{:S(2)}, u32[]{:S(2)}) collective-permute-start(bf16[32,32,128]{2,1,0:T(8,128)(2,1)S(1)} %all-to-all-done.3.refs_0_), channel_id=1, source_target_pairs={{0,2},{1,3},{2,4},{3,5},{4,6},{5,7},{6,0},{7,1},{8,10},{9,11},{10,... | collective-permute-start | bytes 786440 | tf_op jit(solution)/shard_map/precondition/ppermute | solution.py:33
  123.2 2.4 %copy-start.13 = (bf16[6,64,128]{2,1,0:T(8,128)(2,1)}, bf16[6,64,128]{2,1,0:T(8,128)(2,1)S(1)}, u32[]{:S(2)}) copy-start(bf16[6,64,128]{2,1,0:T(8,128)(2,1)S(1)} %collective-permute-done.24.refs_1_) | copy-start | bytes 294916
  123.2 2.1 %collective-permute-start.26 = (bf16[2,6,64,128]{3,2,1,0:T(8,128)(2,1)S(1)}, bf16[2,6,64,128]{3,2,1,0:T(8,128)(2,1)S(1)}, u32[]{:S(2)}, u32[]{:S(2)}) collective-permute-start(bf16[2,6,64,128]{3,2,1,0:T(8,128)(2,1)S(1)} %collective-permute-done.22.refs_4_), channel_id=1, source_target_pairs={{0,1},{1,0},{2,3},{3,2},{4,5},{5,4},{6,7},{7,6},{8,9},{9,8},{10,11... | collective-permute-start | bytes 589832 | tf_op jit(solution)/shard_map/precondition/ppermute | solution.py:33
  124.1 1.5 %copy-start.3 = (bf16[2,6,64,128]{3,2,1,0:T(8,128)(2,1)}, bf16[2,6,64,128]{3,2,1,0:T(8,128)(2,1)S(1)}, u32[]{:S(2)}) copy-start(bf16[2,6,64,128]{3,2,1,0:T(8,128)(2,1)S(1)} %collective-permute-done.25.refs_3_) | copy-start | bytes 589828
  124.1 1.4 %collective-permute-start.27 = (bf16[2,6,64,128]{3,2,1,0:T(8,128)(2,1)S(1)}, bf16[2,6,64,128]{3,2,1,0:T(8,128)(2,1)S(1)}, u32[]{:S(2)}, u32[]{:S(2)}) collective-permute-start(bf16[2,6,64,128]{3,2,1,0:T(8,128)(2,1)S(1)} %collective-permute-done.23.refs_6_), channel_id=1, source_target_pairs={{0,1},{1,0},{2,3},{3,2},{4,5},{5,4},{6,7},{7,6},{8,9},{9,8},{10,11... | collective-permute-start | bytes 589832 | tf_op jit(solution)/shard_map/precondition/ppermute | solution.py:33
  130.1 8.0 %collective-permute-start.28 = (bf16[32,32,128]{2,1,0:T(8,128)(2,1)S(1)}, bf16[32,32,128]{2,1,0:T(8,128)(2,1)S(1)}, u32[]{:S(2)}, u32[]{:S(2)}) collective-permute-start(bf16[32,32,128]{2,1,0:T(8,128)(2,1)S(1)} %all-to-all-done.3.refs_0_), channel_id=1, source_target_pairs={{0,1},{1,0},{2,3},{3,2},{4,5},{5,4},{6,7},{7,6},{8,9},{9,8},{10,11... | collective-permute-start | bytes 786440 | tf_op jit(solution)/shard_map/precondition/ppermute | solution.py:33
  130.5 7.7 %collective-permute-start.34 = (bf16[32,32,128]{2,1,0:T(8,128)(2,1)S(1)}, bf16[32,32,128]{2,1,0:T(8,128)(2,1)S(1)}, u32[]{:S(2)}, u32[]{:S(2)}) collective-permute-start(bf16[32,32,128]{2,1,0:T(8,128)(2,1)S(1)} %collective-permute-done.33.refs_6_), channel_id=1, source_target_pairs={{0,1},{1,0},{2,3},{3,2},{4,5},{5,4},{6,7},{7,6},{8,9},{9,8},{10,11... | collective-permute-start | bytes 786440 | tf_op jit(solution)/shard_map/precondition/ppermute | solution.py:33
  134.7 3.4 %collective-permute-start.32 = (bf16[32,32,128]{2,1,0:T(8,128)(2,1)S(1)}, bf16[32,32,128]{2,1,0:T(8,128)(2,1)S(1)}, u32[]{:S(2)}, u32[]{:S(2)}) collective-permute-start(bf16[32,32,128]{2,1,0:T(8,128)(2,1)S(1)} %collective-permute-done.31.refs_4_), channel_id=1, source_target_pairs={{0,1},{1,0},{2,3},{3,2},{4,5},{5,4},{6,7},{7,6},{8,9},{9,8},{10,11... | collective-permute-start | bytes 786440 | tf_op jit(solution)/shard_map/precondition/ppermute | solution.py:33
  137.3 2.0 %collective-permute-start.30 = (bf16[32,32,128]{2,1,0:T(8,128)(2,1)S(1)}, bf16[32,32,128]{2,1,0:T(8,128)(2,1)S(1)}, u32[]{:S(2)}, u32[]{:S(2)}) collective-permute-start(bf16[32,32,128]{2,1,0:T(8,128)(2,1)S(1)} %collective-permute-done.29.refs_2_), channel_id=1, source_target_pairs={{0,1},{1,0},{2,3},{3,2},{4,5},{5,4},{6,7},{7,6},{8,9},{9,8},{10,11... | collective-permute-start | bytes 786440 | tf_op jit(solution)/shard_map/precondition/ppermute | solution.py:33
  (5 other events, 4.3 us)
